TPU v7x, 32 devices: a whole 2x2x4 slice. The times are simulated.
32 devices in a mesh: patch: 32 (over z, y, x, core).
Axes of the slice: x: 2, y: 2, z: 4, core: 2. Of those that a mesh axis runs over, the one named last changes fastest.
Arguments:
- inputs: bfloat16 [96, 32, 32, 128], P('patch'), may hold values from -6 to 6
- cotangent: bfloat16 [96, 32, 32, 128], P('patch'), may hold values from -6 to 6
- weights: bfloat16 [3, 3, 128, 128], replicated, may hold values from -0.1875 to 0.1875
- bias_vector: float32 [128], replicated, may hold values from -3 to 3
- neighbours: int32 [96, 8], P('patch'), may hold values from 0 to 95, as said below
- rotations: int32 [96, 8], P('patch'), may hold values from 0 to 3
- corners: int32 [96, 8], P('patch'), may hold values from 0 to 1, as said below
Outputs:
- outputs: bfloat16 [96, 32, 32, 128], P('patch')
- input_grad: bfloat16 [96, 32, 32, 128], P('patch')
- weight_grad: float32 [3, 3, 128, 128], replicated
- bias_grad: float32 [128], replicated
Inputs may be any that keep to these rules, and one draw needn't show every extreme that they name: `neighbours`: the neighbour of a patch on device d lies on a device d + o (modulo the device count) with |o| <= 2; offsets 2 and -2 both occur. `corners`: the four side directions are always 1.
All inputs are finite; a program needn't handle non-finite values.
Results may differ from a plain program's by a relative error of at most 0.0035.
Values may be sent and summed in bfloat16 or wider, within the bound.
No kernel may reach another device: no remote copies, remote signals or barrier semaphores. Data moves between devices by JAX's collectives and lax.ppermute only.
A program may use at most 64 MiB of HBM per device.

v0:
```python
import math

import jax
import jax.numpy as jnp
from jax import lax
from jax.sharding import PartitionSpec as P

REACH = 2


DIRECTIONS = ((-1, -1), (-1, 0), (-1, 1), (0, -1), (0, 1), (1, -1), (1, 0), (1, 1))
SIDE_TABLE = (
    ((0, 0), (3, 1), (1, 3), (2, 2)),
    ((1, 0), (2, 1), (0, 3), (3, 2)),
    ((2, 0), (0, 2), (3, 3), (1, 1)),
    ((3, 0), (1, 2), (2, 3), (0, 1)),
)


def passed_along(value, axis, steps):
    count = lax.axis_size(axis)
    pairs = [(source, (source + steps) % count) for source in range(count)]
    return lax.ppermute(value, axis, pairs)


def aligned_span(step, length):
    if step < 0:
        return slice(length - 2, length)
    if step == 0:
        return slice(0, length)
    return slice(0, 2)


def outer_span(step, length):
    if step < 0:
        return slice(0, 2)
    if step == 0:
        return slice(2, length + 2)
    return slice(length + 2, length + 4)


def aligned_pad(step, length):
    if step < 0:
        return (length - 2, 0)
    if step == 0:
        return (0, 0)
    return (0, length - 2)


def wanted_side(row_step, col_step):
    if row_step < 0:
        return 1
    if row_step > 0:
        return 0
    if col_step < 0:
        return 3
    return 2


def side_views(patches):
    length = patches.shape[1]
    upper = patches[:, 0:2]
    lower = patches[:, length - 2 :]
    left_cols = jnp.swapaxes(patches[:, :, 0:2], 1, 2)
    right_cols = jnp.swapaxes(patches[:, :, length - 2 :], 1, 2)
    return jnp.stack([upper, lower, left_cols, right_cols], axis=1)


def flip_side(strip, code):
    if code & 1:
        strip = strip[:, ::-1]
    if code & 2:
        strip = strip[:, :, ::-1]
    return strip


def turned_side(sides, quarter, which):
    turns = quarter[:, None, None, None]
    result = None
    for k in range(4):
        slot, code = SIDE_TABLE[which][k]
        candidate = flip_side(sides[:, slot], code)
        result = candidate if result is None else jnp.where(turns == k, candidate, result)
    return result


def extend_patch(center, gathered, rotations, corners):
    pieces = {}
    length = center.shape[1]
    for j, (row_step, col_step) in enumerate(DIRECTIONS):
        strip = turned_side(gathered[:, j], rotations[:, j], wanted_side(row_step, col_step))
        if row_step != 0:
            region = strip[:, :, aligned_span(col_step, length)]
        else:
            region = jnp.swapaxes(strip, 1, 2)
        present = corners[:, j][:, None, None, None] > 0
        pieces[row_step, col_step] = jnp.where(present, region, jnp.zeros_like(region))
    upper = jnp.concatenate([pieces[-1, -1], pieces[-1, 0], pieces[-1, 1]], axis=2)
    middle = jnp.concatenate([pieces[0, -1], center, pieces[0, 1]], axis=2)
    lower = jnp.concatenate([pieces[1, -1], pieces[1, 0], pieces[1, 1]], axis=2)
    return jnp.concatenate([upper, middle, lower], axis=1)


def dilated_conv(extended, kernel):
    return lax.conv_general_dilated(
        extended,
        kernel,
        (1, 1),
        "VALID",
        rhs_dilation=(2, 2),
        dimension_numbers=("NHWC", "HWIO", "NHWC"),
        preferred_element_type=jnp.float32,
    )


def collect_edges(strips):
    blocks = {0: strips}
    for offset in range(-REACH, REACH + 1):
        if offset != 0:
            blocks[offset] = passed_along(strips, "patch", -offset)
    return jnp.concatenate([blocks[offset] for offset in range(-REACH, REACH + 1)], axis=0)


def deliver_terms(pooled, patches_here):

    def member(offset):
        start = (offset + REACH) * patches_here
        return pooled[start : start + patches_here]

    total = member(0)
    for offset in range(-REACH, REACH + 1):
        if offset != 0:
            total = total + passed_along(
                member(offset).astype(jnp.bfloat16), "patch", offset
            ).astype(jnp.float32)
    return total


def side_terms(region, quarter, which):
    turns = quarter[:, None, None, None]
    slots = [None, None, None, None]
    for k in range(4):
        slot, code = SIDE_TABLE[which][k]
        slots[slot] = jnp.where(turns == k, flip_side(region, code), jnp.zeros_like(region))
    return jnp.stack(slots, axis=1)


def body(inputs, cotangent, weights, bias_vector, neighbours, rotations, corners):
    patches_here, length, _, chans = inputs.shape
    devices_all = lax.axis_size("patch")
    own_index = lax.axis_index("patch")
    owners = neighbours // patches_here
    offset = (owners - own_index) % devices_all
    offset = jnp.where(offset > devices_all // 2, offset - devices_all, offset)
    places = (offset + REACH) * patches_here + neighbours % patches_here
    pooled_edges = collect_edges(side_views(inputs))
    gathered = pooled_edges[places]
    extended = extend_patch(inputs, gathered, rotations, corners)
    outputs = (dilated_conv(extended, weights) + bias_vector).astype(jnp.bfloat16)
    padded_grad = jnp.pad(cotangent, ((0, 0), (4, 4), (4, 4), (0, 0)))
    flipped = jnp.swapaxes(weights[::-1, ::-1], 2, 3)
    ext_grad = dilated_conv(padded_grad, flipped)
    parts = []
    for j, (row_step, col_step) in enumerate(DIRECTIONS):
        region = ext_grad[:, outer_span(row_step, length), outer_span(col_step, length)]
        present = corners[:, j][:, None, None, None] > 0
        region = jnp.where(present, region, jnp.zeros_like(region))
        if row_step != 0:
            region = jnp.pad(region, ((0, 0), (0, 0), aligned_pad(col_step, length), (0, 0)))
        else:
            region = jnp.swapaxes(region, 1, 2)
        parts.append(side_terms(region, rotations[:, j], wanted_side(row_step, col_step)))
    returned = jnp.stack(parts, axis=1)
    pooled_terms = jnp.zeros(((2 * REACH + 1) * patches_here,) + returned.shape[2:], jnp.float32)
    pooled_terms = pooled_terms.at[places.reshape(-1)].add(
        returned.reshape((-1,) + returned.shape[2:])
    )
    arrived = deliver_terms(pooled_terms, patches_here)
    rest = length - 2
    added = jnp.pad(arrived[:, 0], ((0, 0), (0, rest), (0, 0), (0, 0)))
    added = added + jnp.pad(arrived[:, 1], ((0, 0), (rest, 0), (0, 0), (0, 0)))
    added = added + jnp.pad(jnp.swapaxes(arrived[:, 2], 1, 2), ((0, 0), (0, 0), (0, rest), (0, 0)))
    added = added + jnp.pad(jnp.swapaxes(arrived[:, 3], 1, 2), ((0, 0), (0, 0), (rest, 0), (0, 0)))
    input_grad = (ext_grad[:, 2 : length + 2, 2 : length + 2] + added).astype(jnp.bfloat16)
    taps = []
    for a in range(3):
        for b in range(3):
            window = extended[:, 2 * a : 2 * a + length, 2 * b : 2 * b + length]
            taps.append(
                jnp.einsum("pijc,pijd->cd", window, cotangent, preferred_element_type=jnp.float32)
            )
    weight_local = jnp.stack(taps, axis=0).reshape(3, 3, chans, chans)
    bias_local = jnp.sum(cotangent.astype(jnp.float32), axis=(0, 1, 2))
    weight_total, bias_total = lax.psum((weight_local, bias_local), "patch")
    factor = 1.0 / (length * math.sqrt(patches_here * devices_all))
    return (outputs, input_grad, weight_total * factor, bias_total * factor)


def solution(mesh):
    in_specs = (
        P("patch", None, None, None),
        P("patch", None, None, None),
        P(),
        P(),
        P("patch", None),
        P("patch", None),
        P("patch", None),
    )
    out_specs = (P("patch", None, None, None), P("patch", None, None, None), P(), P())
    return jax.shard_map(body, mesh=mesh, in_specs=in_specs, out_specs=out_specs, check_vma=False)
```

profile of v0, /device:TPU:0, one launch (start us, length us, event | category | flops | bytes accessed | tf_op | source)
XLA Modules:
  0.0 260.9 jit_solution(13896437651739778682)
XLA Ops:
  7.2 1.1 fusion.96
  9.9 2.9 %collective-permute-start = (bf16[3,4,2,32,128]{4,3,2,1,0:T(8,128)(2,1)}, bf16[3,4,2,32,128]{4,3,2,1,0:T(8,128)(2,1)}, u32[]{:S(2)}, u32[]{:S(2)}) collective-permute-start(bf16[3,4,2,32,128]{4,3,2,1,0:T(8,128)(2,1)} %pad_maximum_fusion.4), channel_id=1, source_target_pairs={{0,2},{1,3},{2,4},{3,5},{4,6},{5,7},{6,8},{7,9},{8,10},{9,11},{10,... | collective-permute-start | bytes 589832 | tf_op jit(solution)/shard_map/ppermute | solution.py:23
  12.9 5.3 %collective-permute-start.2 = (bf16[3,4,2,32,128]{4,3,2,1,0:T(8,128)(2,1)}, bf16[3,4,2,32,128]{4,3,2,1,0:T(8,128)(2,1)}, u32[]{:S(2)}, u32[]{:S(2)}) collective-permute-start(bf16[3,4,2,32,128]{4,3,2,1,0:T(8,128)(2,1)} %pad_maximum_fusion.4), channel_id=1, source_target_pairs={{0,31},{1,0},{2,1},{3,2},{4,3},{5,4},{6,5},{7,6},{8,7},{9,8},{10,9... | collective-permute-start | bytes 589832 | tf_op jit(solution)/shard_map/ppermute | solution.py:23
  18.7 2.2 compare_reduce_fusion
  20.9 1.3 fusion.77
  22.2 1.4 copy.230
  24.5 3.3 %fusion.11 = f32[36,24,5,128]{3,1,2,0:T(8,128)S(1)} fusion(bf16[3,3,128,128]{3,2,1,0:T(8,128)(2,1)S(1)} %copy-done, bf16[32,3,8,9,128]{4,0,3,2,1:T(8,128)(2,1)S(1)} %fusion.6, pred[24,5]{0,1:T(8,128)(4,1)S(1)} %copy-done.52), kind=kOutput, calls=%fused_computation.19 | convolution fusion | flops 1133015040 | bytes 4276344 | tf_op jit(solution)/shard_map/conv_general_dilated | solution.py:105
  38.0 1.4 select_bitcast_fusion.3
  42.5 1.0 select_bitcast_fusion.31
  46.1 1.0 select_bitcast_fusion.18
  50.6 2.0 copy.116
  53.0 6.1 %scatter_fusion = f32[15,4,2,32,128]{4,3,2,1,0:T(8,128)S(1)} fusion(f32[15,4,2,32,128]{4,3,2,1,0:T(8,128)S(1)} %broadcast_in_dim.359, s32[24]{0:T(128)S(1)} %fusion.86, f32[24,4,2,32,128]{4,3,2,1,0:T(8,128)} %bitcast.362), kind=kCustom, calls=%fused_computation.1 | custom fusion | flops 786432 | bytes 9437280 | tf_op jit(solution)/shard_map/scatter-add | solution.py:175
  59.1 1.5 copy.216
  60.6 1.4 fusion.95
  62.0 2.9 %collective-permute-start.4 = (bf16[3,4,2,32,128]{4,2,0,3,1:T(2,128)(2,1)}, bf16[3,4,2,32,128]{4,2,0,3,1:T(2,128)(2,1)}, u32[]{:S(2)}, u32[]{:S(2)}) collective-permute-start(bf16[3,4,2,32,128]{4,2,0,3,1:T(2,128)(2,1)} %get-tuple-element.82), channel_id=1, source_target_pairs={{0,30},{1,31},{2,0},{3,1},{4,2},{5,3},{6,4},{7,5},{8,6},{9,7},{10,... | collective-permute-start | bytes 589832 | tf_op jit(solution)/shard_map/ppermute | solution.py:23
  65.4 37.7 %psum.15 = f32[128]{0:T(128)S(1)} all-reduce(f32[128]{0:T(128)S(1)} %convert_reduce_fusion), channel_id=1, replica_groups=mesh['patch'=32] {'patch'}, use_global_device_ids=true, to_apply=%region_3.4 | all-reduce | flops 128 | bytes 1024 | tf_op jit(solution)/shard_map/psum | solution.py:194
  103.5 2.8 %copy.117 = f32[15,4,2,32,128]{4,2,0,3,1:T(2,128)} copy(f32[15,4,2,32,128]{4,3,2,1,0:T(8,128)S(1)} %scatter_fusion) | data formatting | bytes 3932160 | tf_op jit(solution)/shard_map/scatter-add | solution.py:175
  106.4 2.1 collective-permute-start.5
  116.7 2.7 %maximum_maximum_fusion.1 = (bf16[3,34,36,128]{3,2,0,1:T(8,128)(2,1)S(1)}, bf16[3,34,36,128]{3,2,0,1:T(8,128)(2,1)S(1)}) fusion(bf16[3,2,2,128]{3,2,0,1:T(2,128)(2,1)S(1)} %get-tuple-element.151, bf16[3,2,32,128]{3,2,0,1:T(8,128)(2,1)S(1)} %get-tuple-element.147, bf16[3,2,2,128]{3,2,0,1:T(2,128)(2,1)S(1)} %get-tuple-element.152, ...), kind=kLoop, calls=%fused_computation.40 | loop fusion | flops 11280384 | bytes 2875392 | tf_op jit(solution)/shard_map/concatenate | solution.py:101
  124.7 1.7 fusion.35
  127.5 2.7 %add_convert_fusion = bf16[32,24,5,128]{3,1,2,0:T(8,128)(2,1)S(1)} fusion(bf16[3,3,128,128]{3,2,1,0:T(8,128)(2,1)S(1)} %copy-done, bf16[36,3,8,9,128]{4,0,3,2,1:T(8,128)(2,1)S(1)} %fusion.2, f32[128]{0:T(128)S(1)} %copy-done.50, pred[24,5]{0,1:T(8,128)(4,1)S(1)} %copy-done.51), kind=kOutput, calls=%fused_computation.11 | convolution fusion | flops 1133936640 | bytes 3269240 | tf_op jit(solution)/shard_map/conv_general_dilated | solution.py:105
  131.8 1.2 copy.135
  133.0 119.1 %all-reduce.10.cloned.1.call-done = f32[3,3,128,128]{3,2,1,0:T(8,128)} async-done(((f32[3,3,128,128]{3,2,1,0:T(8,128)}), f32[3,3,128,128]{3,2,1,0:T(8,128)}) %all-reduce.10.cloned.1.call-update) | async-done | bytes 589840 | tf_op jit(solution)/shard_map/psum | solution.py:194
  252.1 1.9 broadcast_multiply_fusion
  (256 shorter events, 38.6 us)
Async XLA Ops:
  7.2 17.0 %copy-start = (bf16[3,3,128,128]{3,2,1,0:T(8,128)(2,1)S(1)}, bf16[3,3,128,128]{3,2,1,0:T(8,128)(2,1)}, u32[]{:S(2)}) copy-start(bf16[3,3,128,128]{3,2,1,0:T(8,128)(2,1)} %param.9) | copy-start | bytes 884740
  7.2 244.9 %all-reduce.10.cloned.1.call-start = ((), (), s32[]{:S(2)}) async-start(), calls=%async_computation | async-start | bytes 1179648 | tf_op jit(solution)/shard_map/psum | solution.py:194
  9.9 96.5 %collective-permute-start = (bf16[3,4,2,32,128]{4,3,2,1,0:T(8,128)(2,1)}, bf16[3,4,2,32,128]{4,3,2,1,0:T(8,128)(2,1)}, u32[]{:S(2)}, u32[]{:S(2)}) collective-permute-start(bf16[3,4,2,32,128]{4,3,2,1,0:T(8,128)(2,1)} %pad_maximum_fusion.4), channel_id=1, source_target_pairs={{0,2},{1,3},{2,4},{3,5},{4,6},{5,7},{6,8},{7,9},{8,10},{9,11},{10,... | collective-permute-start | bytes 589832 | tf_op jit(solution)/shard_map/ppermute | solution.py:23
  12.9 96.6 %collective-permute-start.1 = (bf16[3,4,2,32,128]{4,3,2,1,0:T(8,128)(2,1)}, bf16[3,4,2,32,128]{4,3,2,1,0:T(8,128)(2,1)}, u32[]{:S(2)}, u32[]{:S(2)}) collective-permute-start(bf16[3,4,2,32,128]{4,3,2,1,0:T(8,128)(2,1)} %pad_maximum_fusion.4), channel_id=1, source_target_pairs={{0,1},{1,2},{2,3},{3,4},{4,5},{5,6},{6,7},{7,8},{8,9},{9,10},{10,1... | collective-permute-start | bytes 589832 | tf_op jit(solution)/shard_map/ppermute | solution.py:23
  12.9 97.6 %collective-permute-start.2 = (bf16[3,4,2,32,128]{4,3,2,1,0:T(8,128)(2,1)}, bf16[3,4,2,32,128]{4,3,2,1,0:T(8,128)(2,1)}, u32[]{:S(2)}, u32[]{:S(2)}) collective-permute-start(bf16[3,4,2,32,128]{4,3,2,1,0:T(8,128)(2,1)} %pad_maximum_fusion.4), channel_id=1, source_target_pairs={{0,31},{1,0},{2,1},{3,2},{4,3},{5,4},{6,5},{7,6},{8,7},{9,8},{10,9... | collective-permute-start | bytes 589832 | tf_op jit(solution)/shard_map/ppermute | solution.py:23
  18.2 94.1 %collective-permute-start.3 = (bf16[3,4,2,32,128]{4,3,2,1,0:T(8,128)(2,1)}, bf16[3,4,2,32,128]{4,3,2,1,0:T(8,128)(2,1)}, u32[]{:S(2)}, u32[]{:S(2)}) collective-permute-start(bf16[3,4,2,32,128]{4,3,2,1,0:T(8,128)(2,1)} %pad_maximum_fusion.4), channel_id=1, source_target_pairs={{0,30},{1,31},{2,0},{3,1},{4,2},{5,3},{6,4},{7,5},{8,6},{9,7},{10,... | collective-permute-start | bytes 589832 | tf_op jit(solution)/shard_map/ppermute | solution.py:23
  22.2 9.0 %copy-start.43 = (pred[3]{0:T(512)(128)(4,1)}, pred[3]{0:T(512)(128)(4,1)S(1)}, u32[]{:S(2)}) copy-start(pred[3]{0:T(512)(128)(4,1)S(1)} %get-tuple-element.55) | copy-start | bytes 13
  22.2 9.0 %copy-start.47 = (pred[3]{0:T(512)(128)(4,1)}, pred[3]{0:T(512)(128)(4,1)S(1)}, u32[]{:S(2)}) copy-start(pred[3]{0:T(512)(128)(4,1)S(1)} %get-tuple-element.53) | copy-start | bytes 13
  22.2 12.4 %copy-start.41 = (pred[3]{0:T(512)(128)(4,1)}, pred[3]{0:T(512)(128)(4,1)S(1)}, u32[]{:S(2)}) copy-start(pred[3]{0:T(512)(128)(4,1)S(1)} %get-tuple-element.50) | copy-start | bytes 13
  22.2 12.4 %copy-start.45 = (pred[3]{0:T(512)(128)(4,1)}, pred[3]{0:T(512)(128)(4,1)S(1)}, u32[]{:S(2)}) copy-start(pred[3]{0:T(512)(128)(4,1)S(1)} %get-tuple-element.51) | copy-start | bytes 13
  28.8 10.6 %copy-start.1 = (f32[36,3,36,128]{3,2,1,0:T(8,128)}, f32[36,3,36,128]{3,2,1,0:T(8,128)S(1)}, u32[]{:S(2)}) copy-start(f32[36,3,36,128]{3,2,1,0:T(8,128)S(1)} %copy.229) | copy-start | bytes 5971972
  39.5 8.4 %copy-start.28 = (pred[3]{0:T(512)(128)(4,1)S(1)}, pred[3]{0:T(512)(128)(4,1)}, u32[]{:S(2)}) copy-start(pred[3]{0:T(512)(128)(4,1)} %get-tuple-element.30) | copy-start | bytes 13
  39.5 9.6 %copy-start.18 = (f32[3,2,32,128]{3,2,0,1:T(8,128)S(1)}, f32[3,2,32,128]{3,2,0,1:T(8,128)}, u32[]{:S(2)}) copy-start(f32[3,2,32,128]{3,2,0,1:T(8,128)} %rev.188) | copy-start | bytes 294916
  39.6 9.6 %copy-start.33 = (pred[3]{0:T(512)(128)(4,1)S(1)}, pred[3]{0:T(512)(128)(4,1)}, u32[]{:S(2)}) copy-start(pred[3]{0:T(512)(128)(4,1)} %get-tuple-element.20) | copy-start | bytes 13
  39.6 9.6 %copy-start.35 = (pred[3]{0:T(512)(128)(4,1)S(1)}, pred[3]{0:T(512)(128)(4,1)}, u32[]{:S(2)}) copy-start(pred[3]{0:T(512)(128)(4,1)} %get-tuple-element.21) | copy-start | bytes 13
  39.6 9.7 %copy-start.29 = (pred[3]{0:T(512)(128)(4,1)S(1)}, pred[3]{0:T(512)(128)(4,1)}, u32[]{:S(2)}) copy-start(pred[3]{0:T(512)(128)(4,1)} %get-tuple-element.132) | copy-start | bytes 13
  39.6 9.7 %copy-start.31 = (pred[3]{0:T(512)(128)(4,1)S(1)}, pred[3]{0:T(512)(128)(4,1)}, u32[]{:S(2)}) copy-start(pred[3]{0:T(512)(128)(4,1)} %get-tuple-element.142) | copy-start | bytes 13
  39.7 9.7 %copy-start.13 = (f32[3,1,2,32,128]{4,3,0,2,1:T(8,128)S(1)}, f32[3,1,2,32,128]{4,3,0,2,1:T(8,128)}, u32[]{:S(2)}) copy-start(f32[3,1,2,32,128]{4,3,0,2,1:T(8,128)} %get-tuple-element.158) | copy-start | bytes 294916
  41.4 8.1 %copy-start.32 = (pred[3]{0:T(512)(128)(4,1)S(1)}, pred[3]{0:T(512)(128)(4,1)}, u32[]{:S(2)}) copy-start(pred[3]{0:T(512)(128)(4,1)} %get-tuple-element.143) | copy-start | bytes 13
  41.4 8.1 %copy-start.39 = (pred[3]{0:T(512)(128)(4,1)S(1)}, pred[3]{0:T(512)(128)(4,1)}, u32[]{:S(2)}) copy-start(pred[3]{0:T(512)(128)(4,1)} %get-tuple-element.135) | copy-start | bytes 13
  62.0 62.6 %collective-permute-start.4 = (bf16[3,4,2,32,128]{4,2,0,3,1:T(2,128)(2,1)}, bf16[3,4,2,32,128]{4,2,0,3,1:T(2,128)(2,1)}, u32[]{:S(2)}, u32[]{:S(2)}) collective-permute-start(bf16[3,4,2,32,128]{4,2,0,3,1:T(2,128)(2,1)} %get-tuple-element.82), channel_id=1, source_target_pairs={{0,30},{1,31},{2,0},{3,1},{4,2},{5,3},{6,4},{7,5},{8,6},{9,7},{10,... | collective-permute-start | bytes 589832 | tf_op jit(solution)/shard_map/ppermute | solution.py:23
  106.4 18.2 %collective-permute-start.5 = (bf16[3,4,2,32,128]{4,2,0,3,1:T(2,128)(2,1)}, bf16[3,4,2,32,128]{4,2,0,3,1:T(2,128)(2,1)}, u32[]{:S(2)}, u32[]{:S(2)}) collective-permute-start(bf16[3,4,2,32,128]{4,2,0,3,1:T(2,128)(2,1)} %get-tuple-element.85), channel_id=1, source_target_pairs={{0,31},{1,0},{2,1},{3,2},{4,3},{5,4},{6,5},{7,6},{8,7},{9,8},{10,9... | collective-permute-start | bytes 589832 | tf_op jit(solution)/shard_map/ppermute | solution.py:23
  109.5 15.2 %collective-permute-start.6 = (bf16[3,4,2,32,128]{4,2,0,3,1:T(2,128)(2,1)}, bf16[3,4,2,32,128]{4,2,0,3,1:T(2,128)(2,1)}, u32[]{:S(2)}, u32[]{:S(2)}) collective-permute-start(bf16[3,4,2,32,128]{4,2,0,3,1:T(2,128)(2,1)} %get-tuple-element.84), channel_id=1, source_target_pairs={{0,1},{1,2},{2,3},{3,4},{4,5},{5,6},{6,7},{7,8},{8,9},{9,10},{10,1... | collective-permute-start | bytes 589832 | tf_op jit(solution)/shard_map/ppermute | solution.py:23
  110.5 14.1 %collective-permute-start.7 = (bf16[3,4,2,32,128]{4,2,0,3,1:T(2,128)(2,1)}, bf16[3,4,2,32,128]{4,2,0,3,1:T(2,128)(2,1)}, u32[]{:S(2)}, u32[]{:S(2)}) collective-permute-start(bf16[3,4,2,32,128]{4,2,0,3,1:T(2,128)(2,1)} %get-tuple-element.83), channel_id=1, source_target_pairs={{0,2},{1,3},{2,4},{3,5},{4,6},{5,7},{6,8},{7,9},{8,10},{9,11},{10,... | collective-permute-start | bytes 589832 | tf_op jit(solution)/shard_map/ppermute | solution.py:23
  (38 other events, 92.5 us)
Sparse Core Ops, SparseCore 0:
  124.1 127.8 all-reduce.9
where the time goes:
time: 262 us; the launch traced here: 261 us
  waiting for transfers between devices  119 us (45%)
  blocking collectives  37.7 us (14%)
  other arithmetic  33.6 us (13%)
  local copies, waits for them, and re-layouts  30.7 us (12%)
  between operations  15.3 us (6%)
  starting transfers between devices  14.6 us (6%)
  matrix products  9.84 us (4%)
    psum x1, waiting for transfers between devices, body(): weight_total, bias_total = lax.psum((weight_local, bias_local), 'patch')  119 us
    psum x1, blocking collectives, body(): weight_total, bias_total = lax.psum((weight_local, bias_local), 'patch')  37.7 us
    ppermute x8, starting transfers between devices, passed_along(): return lax.ppermute(value, axis, pairs)  14.5 us
    another operation x25, other arithmetic, side_terms(): return jnp.stack(slots, axis=1)  13.6 us
    unnamed x127, local copies, waits for them, and re-layouts  9.88 us
    rev x32, local copies, waits for them, and re-layouts, flip_side(): strip = strip[:, :, ::-1]  7.06 us
    scatter-add x1, other arithmetic, body(): pooled_terms.at[places.reshape(-1)]  6.1 us
    conv_general_dilated x2, matrix products, dilated_conv(): lax.conv_general_dilated(extended, kernel, (1, 1), 'VALID', rhs_dilation=...  6.06 us
  transfers between devices with their start and end apart: 9, of which 1 were waited for; matrix products, arithmetic and copies ran while one was open for 26% of the time, Pallas kernels for 0%

commit v1 on v0

v1 whole, which is shorter than its diff:
```python
import functools
import math

import jax
import jax.numpy as jnp
import numpy as np
from jax import lax
from jax.experimental import pallas as pl
from jax.experimental.pallas import tpu as pltpu
from jax.sharding import PartitionSpec as P

REACH = 2
BF = jnp.bfloat16
F32 = jnp.float32

DIRECTIONS = ((-1, -1), (-1, 0), (-1, 1), (0, -1), (0, 1), (1, -1), (1, 0), (1, 1))
SIDE_TABLE = (
    ((0, 0), (3, 1), (1, 3), (2, 2)),
    ((1, 0), (2, 1), (0, 3), (3, 2)),
    ((2, 0), (0, 2), (3, 3), (1, 1)),
    ((3, 0), (1, 2), (2, 3), (0, 1)),
)
SIDE_DIRECTION = (1, 6, 3, 4)
SIDE_ENDS = ((0, 2), (5, 7))
SIDE_TAPS = (((0, 0), (0, 1), (0, 2)), ((2, 0), (2, 1), (2, 2)), ((0, 0), (1, 0), (2, 0)), ((0, 2), (1, 2), (2, 2)))


def wanted_side(row_step, col_step):
    if row_step < 0:
        return 1
    if row_step > 0:
        return 0
    return 3 if col_step < 0 else 2


def flip_tables(length):
    size = 2 * length
    flips = np.zeros((4, size, size), np.float32)
    for code in range(4):
        for r in range(2):
            for k in range(length):
                rr = 1 - r if code & 1 else r
                kk = length - 1 - k if code & 2 else k
                flips[code, r * length + k, rr * length + kk] = 1
    back = np.zeros((2, size, size), np.float32)
    ahead = np.zeros((2, size, size), np.float32)
    for r in range(2):
        for k in range(length):
            back[int(k < 2), r * length + k, r * length + (k - 2) % length] = 1
            ahead[int(k >= length - 2), r * length + k, r * length + (k + 2) % length] = 1
    sides = np.stack([np.concatenate([back[0] @ f, f, ahead[0] @ f]) for f in flips])
    ends = np.stack([np.concatenate([back[1] @ f, ahead[1] @ f]) for f in flips])
    return flips, sides, ends


def place_of(me, neighbour, rotation, which, patches_here, devices):
    owner = lax.div(neighbour, patches_here)
    within = neighbour - owner * patches_here
    offset = owner - me
    offset = jnp.where(offset < 0, offset + devices, offset)
    core = lax.rem(me, 2)
    to_mate = jnp.where(core == 0, 1, devices - 1)
    block = jnp.where(offset == to_mate, 3, 4)
    block = jnp.where(offset == 2, 2, block)
    block = jnp.where(offset == devices - 2, 1, block)
    block = jnp.where(offset == 0, 0, block)
    slot, code = SIDE_TABLE[which][0]
    for k in range(1, 4):
        slot = jnp.where(rotation == k, SIDE_TABLE[which][k][0], slot)
        code = jnp.where(rotation == k, SIDE_TABLE[which][k][1], code)
    return (block * patches_here + within) * 4 + slot, code


def dot(a, b):
    return jnp.dot(a, b, preferred_element_type=F32)


def column_strip(wide_ref, first, length):
    return jnp.concatenate([wide_ref[pl.ds(first + c, length, stride=length), :] for c in range(2)], axis=0)


def add_columns(wide_ref, first, length, strip):
    for c in range(2):
        at = pl.ds(first + c, length, stride=length)
        wide_ref[at, :] = wide_ref[at, :] + strip[c * length : (c + 1) * length]


def spread(ext_ref, wide, length):
    count = length * length
    column = lax.broadcasted_iota(jnp.int32, (count, 1), 0) & (length - 1)
    pad = 2 * length
    back = jnp.where(column >= 2, pltpu.roll(wide, 2, 0), 0.0)
    ahead = jnp.where(column < length - 2, pltpu.roll(wide, count - 2, 0), 0.0)
    ext_ref[pad : pad + count, 0:128] = back.astype(BF)
    ext_ref[pad : pad + count, 128:256] = wide.astype(BF)
    ext_ref[pad : pad + count, 256:384] = ahead.astype(BF)


def clear_rows(ext_ref, length):
    pad = 2 * length
    empty = jnp.zeros((pad, 384), BF)
    ext_ref[0:pad, :] = empty
    ext_ref[pad + length * length :, :] = empty


def pack_kernel(x_ref, out_ref, wide_ref, *, length):
    count = length * length
    for p in range(x_ref.shape[0]):
        out_ref[4 * p] = x_ref[p, 0 : 2 * length, :]
        out_ref[4 * p + 1] = x_ref[p, count - 2 * length :, :]
        wide_ref[...] = x_ref[p].astype(F32)
        out_ref[4 * p + 2] = column_strip(wide_ref, 0, length).astype(BF)
        out_ref[4 * p + 3] = column_strip(wide_ref, length - 2, length).astype(BF)


def local_kernel(
    me_ref, nb_ref, rot_ref, cor_ref, x_ref, cot_ref, w_ref, flip_ref,
    dw_ref, bias_ref, dx_ref, strips_ref, own_ref, far_ref, near_ref,
    ext_ref, wide_ref, pool_ref, *, length, devices,
):
    patches = x_ref.shape[0]
    count = length * length
    me = me_ref[0]
    clear_rows(ext_ref, length)
    pool_ref[...] = jnp.zeros_like(pool_ref)
    total_bias = jnp.zeros((1, 128), F32)
    chunk = min(count, 256)
    flipped = [
        jnp.concatenate([w_ref[(2 - a) * 3 + 2], w_ref[(2 - a) * 3 + 1], w_ref[(2 - a) * 3]], axis=1) for a in range(3)
    ]
    along = lax.broadcasted_iota(jnp.int32, (length, 1), 0)
    for p in range(patches):
        wide = cot_ref[p].astype(F32)
        wide_ref[...] = wide
        total_bias = total_bias + jnp.sum(wide, axis=0, keepdims=True)
        spread(ext_ref, wide, length)
        strips = [
            cot_ref[p, 0 : 2 * length, :],
            cot_ref[p, count - 2 * length :, :],
            column_strip(wide_ref, 0, length).astype(BF),
            column_strip(wide_ref, length - 2, length).astype(BF),
        ]
        for s in range(4):
            strips_ref[s, 2 * length * p : 2 * length * (p + 1), :] = strips[s]
            taps = [w_ref[a * 3 + b] for a, b in SIDE_TAPS[s]]
            terms = lax.dot_general(
                strips[s], jnp.concatenate(taps, axis=0), (((1,), (1,)), ((), ())), preferred_element_type=F32
            )
            side, first, last = [], [], []
            for r in range(2):
                rows = slice(r * length, (r + 1) * length)
                ahead = pltpu.roll(terms[rows, 0:128], length - 2, 0)
                back = pltpu.roll(terms[rows, 256:384], 2, 0)
                side.append(
                    terms[rows, 128:256]
                    + jnp.where(along < length - 2, ahead, 0.0)
                    + jnp.where(along >= 2, back, 0.0)
                )
                first.append(jnp.where(along >= length - 2, ahead, 0.0))
                last.append(jnp.where(along < 2, back, 0.0))
            sent = [(SIDE_DIRECTION[s], side)]
            if s < 2:
                sent += [(SIDE_ENDS[s][0], first), (SIDE_ENDS[s][1], last)]
            for j, term in sent:
                where_to, code = place_of(
                    me, nb_ref[p, j], rot_ref[p, j], wanted_side(*DIRECTIONS[j]), patches, devices
                )
                value = dot(flip_ref[code], jnp.concatenate(term, axis=0).astype(BF))
                value = value * (cor_ref[p, j] > 0).astype(F32)
                pool_ref[where_to] = pool_ref[where_to] + value
        turned = x_ref[p].T
        for a in range(3):
            grads = dot(turned, ext_ref[2 * length * a : 2 * length * a + count, :])
            for b in range(3):
                tap = (2 - a) * 3 + 2 - b
                rows = slice(tap * 128, (tap + 1) * 128)
                part = grads[:, b * 128 : (b + 1) * 128]
                dw_ref[rows, :] = part if p == 0 else dw_ref[rows, :] + part
        for start in range(0, count, chunk):
            total = None
            for a in range(3):
                at = start + 2 * length * a
                part = lax.dot_general(
                    ext_ref[at : at + chunk, :], flipped[a], (((1,), (1,)), ((), ())), preferred_element_type=F32
                )
                total = part if total is None else total + part
            dx_ref[p, start : start + chunk, :] = total.astype(BF)
    bias_ref[...] = jnp.broadcast_to(total_bias, bias_ref.shape)
    block = 4 * patches
    own_ref[...] = pool_ref[0:block]
    far_ref[...] = pool_ref[block : 3 * block]
    near_ref[...] = pool_ref[3 * block :].astype(BF)


def halo_kernel(
    me_ref, nb_ref, rot_ref, cor_ref, own_ref, low_ref, high_ref, mate_ref, across_ref, strips_ref, dw_ref, bias_ref,
    side_ref, end_ref, out_ref, halo_ref, pool_ref, *, length, devices, factor,
):
    block = own_ref.shape[0]
    patches = block // 4
    for i, source in enumerate((own_ref, low_ref, high_ref, mate_ref, across_ref)):
        pool_ref[i * block : (i + 1) * block] = source[...]
    me = me_ref[0]
    size = 2 * length
    for p in range(patches):

        def fetch(j):
            at, code = place_of(me, nb_ref[p, j], rot_ref[p, j], wanted_side(*DIRECTIONS[j]), patches, devices)
            return pool_ref[at], code

        for s in range(4):
            source, code = fetch(SIDE_DIRECTION[s])
            shifted = dot(side_ref[code], source)
            parts = [shifted[0:size], shifted[size : 2 * size], shifted[2 * size :]]
            if s < 2:
                for which, j in ((0, SIDE_ENDS[s][0]), (1, SIDE_ENDS[s][1])):
                    source, code = fetch(j)
                    corner = dot(end_ref[code, which * size : (which + 1) * size, :], source)
                    parts[2 * which] = parts[2 * which] + corner * (cor_ref[p, j] > 0).astype(F32)
            for i in range(3):
                halo_ref[s, p * size : (p + 1) * size, i * 128 : (i + 1) * 128] = parts[i].astype(BF)
    out_ref[0 : 9 * 128, :] = dw_ref[...]
    for s in range(4):
        grads = lax.dot_general(
            halo_ref[s], strips_ref[s], (((0,), (0,)), ((), ())), preferred_element_type=F32
        )
        for i, (a, b) in enumerate(SIDE_TAPS[s]):
            rows = slice((a * 3 + b) * 128, (a * 3 + b + 1) * 128)
            out_ref[rows, :] = out_ref[rows, :] + grads[i * 128 : (i + 1) * 128]
    out_ref[0 : 9 * 128, :] = out_ref[0 : 9 * 128, :] * factor
    out_ref[9 * 128 : 9 * 128 + 8, :] = bias_ref[...] * factor
    out_ref[9 * 128 + 8 :, :] = jnp.zeros((out_ref.shape[0] - 9 * 128 - 8, 128), F32)


def forward_kernel(x_ref, w_ref, bias_ref, halo_ref, out_ref, ext_ref, wide_ref, *, length):
    patches = x_ref.shape[0]
    count = length * length
    size = 2 * length
    chunk = min(count, 256)
    clear_rows(ext_ref, length)
    borders = []
    for s in range(4):
        taps = jnp.concatenate([w_ref[a * 3 + b] for a, b in SIDE_TAPS[s]], axis=0)
        borders.append(dot(halo_ref[s], taps))
    rows_of = [jnp.concatenate([w_ref[a * 3 + b] for b in range(3)], axis=0) for a in range(3)]
    for p in range(patches):
        spread(ext_ref, x_ref[p].astype(F32), length)
        for start in range(0, count, chunk):
            total = jnp.broadcast_to(bias_ref[...], (chunk, 128))
            for a in range(3):
                at = start + size * a
                total = total + dot(ext_ref[at : at + chunk, :], rows_of[a])
            wide_ref[start : start + chunk, :] = total
        mine = slice(p * size, (p + 1) * size)
        wide_ref[0:size, :] = wide_ref[0:size, :] + borders[0][mine]
        wide_ref[count - size :, :] = wide_ref[count - size :, :] + borders[1][mine]
        add_columns(wide_ref, 0, length, borders[2][mine])
        add_columns(wide_ref, length - 2, length, borders[3][mine])
        out_ref[p] = wide_ref[...].astype(BF)


def join_kernel(dx_ref, own_ref, mate_ref, low_ref, high_ref, out_ref, wide_ref, *, length):
    count = length * length
    size = 2 * length
    for p in range(dx_ref.shape[0]):
        wide_ref[...] = dx_ref[p].astype(F32)
        strips = []
        for s in range(4):
            i = 4 * p + s
            strips.append(
                own_ref[i] + mate_ref[i].astype(F32) + low_ref[i].astype(F32) + high_ref[i].astype(F32)
            )
        wide_ref[0:size, :] = wide_ref[0:size, :] + strips[0]
        wide_ref[count - size :, :] = wide_ref[count - size :, :] + strips[1]
        add_columns(wide_ref, 0, length, strips[2])
        add_columns(wide_ref, length - 2, length, strips[3])
        out_ref[p] = wide_ref[...].astype(BF)


def vmem():
    return pl.BlockSpec(memory_space=pltpu.VMEM)


def smem():
    return pl.BlockSpec(memory_space=pltpu.SMEM)


def call(kernel, name, n_smem, n_vmem, outs, scratch, flops, nbytes):
    return pl.pallas_call(
        kernel,
        name=name,
        out_shape=outs,
        in_specs=[smem()] * n_smem + [vmem()] * n_vmem,
        out_specs=jax.tree.map(lambda _: vmem(), outs),
        scratch_shapes=scratch,
        compiler_params=pltpu.CompilerParams(vmem_limit_bytes=40 * 1024 * 1024),
        cost_estimate=pl.CostEstimate(flops=flops, bytes_accessed=nbytes, transcendentals=0),
    )


def shifted(value, steps):
    count = lax.axis_size("patch")
    return lax.ppermute(value, "patch", [(d, (d + steps) % count) for d in range(count)])


def swapped(value, mask):
    return lax.ppermute(value, "patch", [(d, d ^ mask) for d in range(lax.axis_size("patch"))])


def part_of(value, index, size):
    return lax.dynamic_slice_in_dim(value, index * size, size)


def summed(value, me, devices):
    rows = value.shape[0]
    core = me % 2
    half = rows // 2
    mine = part_of(value, core, half) + swapped(part_of(value, 1 - core, half), 1)
    quarter = half // 4
    at = (me // 2) % 4
    arrived = [swapped(part_of(mine, at ^ k, quarter).astype(BF), 2 * k) for k in range(1, 4)]
    mine = part_of(mine, at, quarter)
    for a in arrived:
        mine = mine + a.astype(F32)
    step = 8
    while step < devices:
        sent = mine.astype(BF)
        mine = sent.astype(F32) + swapped(sent, step).astype(F32)
        if 2 * step < devices:
            other = swapped(sent, 2 * step).astype(F32) + swapped(sent, 3 * step).astype(F32)
            mine = mine + other
        step *= 4
    pieces = jnp.stack([mine] + [swapped(mine, 2 * k) for k in range(1, 4)])
    whole = jnp.concatenate([lax.dynamic_index_in_dim(pieces, at ^ k, 0, False) for k in range(4)])
    other = swapped(whole, 1)
    low = jnp.where(core == 0, whole, other)
    high = jnp.where(core == 0, other, whole)
    return jnp.concatenate([low, high])


def body(inputs, cotangent, weights, bias_vector, neighbours, rotations, corners):
    patches, length, _, chans = inputs.shape
    devices = lax.axis_size("patch")
    count = length * length
    size = 2 * length
    block = 4 * patches
    me = lax.axis_index("patch")
    me_arr = me.reshape(1).astype(jnp.int32)
    core = me % 2
    x = inputs.reshape(patches, count, chans)
    cot = cotangent.reshape(patches, count, chans)
    w = weights.reshape(9, chans, chans)
    flips, sides, ends = (jnp.asarray(t, BF) for t in flip_tables(length))
    strip_block = jax.ShapeDtypeStruct((block, size, chans), BF)
    strip_block_wide = jax.ShapeDtypeStruct((block, size, chans), F32)
    conv_flops = 2 * 9 * patches * count * chans * chans

    edges = call(
        functools.partial(pack_kernel, length=length), "pack_edges", 0, 1, strip_block,
        [pltpu.VMEM((count, chans), F32)], 0, 2 * x.size,
    )(x)
    from_low = shifted(edges, 2)
    from_high = shifted(edges, -2)
    from_mate = swapped(edges, 1)
    from_across = swapped(jnp.where(core == 0, from_high, from_low), 1)

    dw, bias_part, dx, strips, own, far, near = call(
        functools.partial(local_kernel, length=length, devices=devices), "own_pixels", 4, 4,
        (
            jax.ShapeDtypeStruct((9 * chans, chans), F32),
            jax.ShapeDtypeStruct((8, chans), F32),
            jax.ShapeDtypeStruct((patches, count, chans), BF),
            jax.ShapeDtypeStruct((4, patches * size, chans), BF),
            strip_block_wide,
            jax.ShapeDtypeStruct((2 * block, size, chans), F32),
            jax.ShapeDtypeStruct((2 * block, size, chans), BF),
        ),
        [
            pltpu.VMEM((count + 2 * size, 3 * chans), BF),
            pltpu.VMEM((count, chans), F32),
            pltpu.VMEM((5 * block, size, chans), F32),
        ],
        2 * conv_flops, 6 * x.size,
    )(me_arr, neighbours, rotations, corners, x, cot, w, flips)

    factor = 1.0 / (length * math.sqrt(patches * devices))
    grads, halo = call(
        functools.partial(halo_kernel, length=length, devices=devices, factor=factor), "halo_kernel_grad", 4, 10,
        (
            jax.ShapeDtypeStruct((10 * chans, chans), F32),
            jax.ShapeDtypeStruct((4, patches * size, 3 * chans), BF),
        ),
        [pltpu.VMEM((5 * block, size, chans), BF)],
        conv_flops // 8, 2 * x.size,
    )(me_arr, neighbours, rotations, corners, edges, from_low, from_high, from_mate, from_across, strips, dw,
      bias_part, sides, ends)

    total = summed(grads, me, devices)

    outputs = call(
        functools.partial(forward_kernel, length=length), "forward", 0, 4,
        jax.ShapeDtypeStruct((patches, count, chans), BF),
        [pltpu.VMEM((count + 2 * size, 3 * chans), BF), pltpu.VMEM((count, chans), F32)],
        conv_flops, 4 * x.size,
    )(x, w, bias_vector.reshape(1, chans), halo)

    near_in = swapped(near, 1)
    mate_terms, cross_terms = near_in[:block], near_in[block:].astype(F32)
    to_low = (far[:block] + jnp.where(core == 1, cross_terms, 0.0)).astype(BF)
    to_high = (far[block:] + jnp.where(core == 0, cross_terms, 0.0)).astype(BF)
    terms_high = shifted(to_low, -2)
    terms_low = shifted(to_high, 2)
    input_grad = call(
        functools.partial(join_kernel, length=length), "join_input_grad", 0, 5,
        jax.ShapeDtypeStruct((patches, count, chans), BF),
        [pltpu.VMEM((count, chans), F32)], 0, 5 * x.size,
    )(dx, own, mate_terms, terms_low, terms_high)

    weight_grad = total[: 9 * chans].reshape(weights.shape)
    bias_grad = total[9 * chans]
    return (outputs.reshape(inputs.shape), input_grad.reshape(inputs.shape), weight_grad, bias_grad)


def solution(mesh):
    in_specs = (
        P("patch", None, None, None),
        P("patch", None, None, None),
        P(),
        P(),
        P("patch", None),
        P("patch", None),
        P("patch", None),
    )
    out_specs = (P("patch", None, None, None), P("patch", None, None, None), P(), P())
    return jax.shard_map(body, mesh=mesh, in_specs=in_specs, out_specs=out_specs, check_vma=False)
```

time: 262 us -> 75.3 us (0.29)
  waiting for transfers between devices: 119 us -> 22.7 us
  blocking collectives: 37.7 us -> 0 us
  other arithmetic: 33.6 us -> 5.25 us
  local copies, waits for them, and re-layouts: 30.7 us -> 8.37 us
  between operations: 15.3 us -> 0.84 us
  Pallas kernels: 0 us -> 13 us
  starting transfers between devices: 14.6 us -> 24.7 us
  matrix products: 9.84 us -> 0 us
    psum x1 -> x0, waiting for transfers between devices: 119 us -> none  [body(): weight_total, bias_total = lax.psum((weight_local, bias_local), 'patch')]
    psum x1 -> x0, blocking collectives: 37.7 us -> none  [body(): weight_total, bias_total = lax.psum((weight_local, bias_local), 'patch')]
    ppermute x8 -> x18, waiting for transfers between devices: 0.02 us -> 22.7 us  [the longest x14 13.7 us: swapped(): lax.ppermute(value, 'patch', [(d, d ^ mask) for d in range(lax.axis_size(...]
    another operation x27 -> x1, other arithmetic: 14.3 us -> 1.03 us  [summed(): pieces = jnp.stack([mine] + [swapped(mine, 2 * k) for k in range(1, 4)])]
    pallas_call x0 -> x5, Pallas kernels: none -> 13 us  [the longest x1 6.29 us: body(): call(functools.partial(local_kernel, length=length, devices=devices), 'ow...]
    ppermute x8 -> x18, starting transfers between devices: 14.5 us -> 24.7 us  [the longest x4 12.7 us: shifted(): lax.ppermute(value, 'patch', [(d, (d + steps) % count) for d in range(cou...]
    rev x36 -> x0, local copies, waits for them, and re-layouts: 7.08 us -> none  [the longest x32 7.06 us: flip_side(): strip = strip[:, :, ::-1]]
    scatter-add x1 -> x0, other arithmetic: 6.1 us -> none  [body(): pooled_terms.at[places.reshape(-1)]]
  transfers between devices with their start and end apart: 9 -> 18, of which waited for: 1 -> 13; matrix products, arithmetic and copies ran while one was open for 26% -> 3% of each run, Pallas kernels for 0% -> 15%
where the time goes in v1:
time: 75.3 us; the launch traced here: 74.8 us
  starting transfers between devices  24.7 us (33%)
  waiting for transfers between devices  22.7 us (30%)
  Pallas kernels  13 us (17%)
  local copies, waits for them, and re-layouts  8.37 us (11%)
  other arithmetic  5.25 us (7%)
  between operations  0.84 us (1%)
    ppermute x14, waiting for transfers between devices, swapped(): lax.ppermute(value, 'patch', [(d, d ^ mask) for d in range(lax.axis_size(...  13.7 us
    ppermute x4, starting transfers between devices, shifted(): lax.ppermute(value, 'patch', [(d, (d + steps) % count) for d in range(cou...  12.7 us
    ppermute x14, starting transfers between devices, swapped(): lax.ppermute(value, 'patch', [(d, d ^ mask) for d in range(lax.axis_size(...  12 us
    ppermute x4, waiting for transfers between devices, shifted(): lax.ppermute(value, 'patch', [(d, (d + steps) % count) for d in range(cou...  8.98 us
    unnamed x34, local copies, waits for them, and re-layouts  7.12 us
    pallas_call x1, Pallas kernels, body(): call(functools.partial(local_kernel, length=length, devices=devices), 'ow...  6.29 us
    pallas_call x1, Pallas kernels, body(): call(functools.partial(forward_kernel, length=length), 'forward', 0, 4, j...  3.32 us
    pallas_call x1, Pallas kernels, body(): call(functools.partial(halo_kernel, length=length, devices=devices, facto...  1.83 us
  transfers between devices with their start and end apart: 18, of which 13 were waited for; matrix products, arithmetic and copies ran while one was open for 3% of the time, Pallas kernels for 15%

profile of v1, /device:TPU:0, one launch (start us, length us, event | category | flops | bytes accessed | tf_op | source)
XLA Modules:
  0.0 74.8 jit_solution(6829380339285104982)
XLA Ops:
  1.9 3.0 %collective-permute-start = (bf16[12,64,128]{2,1,0:T(8,128)(2,1)S(1)}, bf16[12,64,128]{2,1,0:T(8,128)(2,1)S(1)}, u32[]{:S(2)}, u32[]{:S(2)}) collective-permute-start(bf16[12,64,128]{2,1,0:T(8,128)(2,1)S(1)} %pack_edges.1.own_ref), channel_id=1, source_target_pairs={{0,2},{1,3},{2,4},{3,5},{4,6},{5,7},{6,8},{7,9},{8,10},{9,11},{10,... | collective-permute-start | bytes 589832 | tf_op jit(solution)/shard_map/ppermute | solution.py:303
  4.9 4.1 %collective-permute-start.1 = (bf16[12,64,128]{2,1,0:T(8,128)(2,1)S(1)}, bf16[12,64,128]{2,1,0:T(8,128)(2,1)S(1)}, u32[]{:S(2)}, u32[]{:S(2)}) collective-permute-start(bf16[12,64,128]{2,1,0:T(8,128)(2,1)S(1)} %pack_edges.1.own_ref), channel_id=1, source_target_pairs={{0,30},{1,31},{2,0},{3,1},{4,2},{5,3},{6,4},{7,5},{8,6},{9,7},{10,... | collective-permute-start | bytes 589832 | tf_op jit(solution)/shard_map/ppermute | solution.py:303
  9.0 4.9 %collective-permute-done.low_ref = bf16[12,64,128]{2,1,0:T(8,128)(2,1)S(1)} collective-permute-done((bf16[12,64,128]{2,1,0:T(8,128)(2,1)S(1)}, bf16[12,64,128]{2,1,0:T(8,128)(2,1)S(1)}, u32[]{:S(2)}, u32[]{:S(2)}) %collective-permute-start) | collective-permute-done | bytes 196640 | tf_op jit(solution)/shard_map/ppermute | solution.py:303
  13.9 1.3 %collective-permute-done.1.high_ref = bf16[12,64,128]{2,1,0:T(8,128)(2,1)S(1)} collective-permute-done((bf16[12,64,128]{2,1,0:T(8,128)(2,1)S(1)}, bf16[12,64,128]{2,1,0:T(8,128)(2,1)S(1)}, u32[]{:S(2)}, u32[]{:S(2)}) %collective-permute-start.1) | collective-permute-done | bytes 196640 | tf_op jit(solution)/shard_map/ppermute | solution.py:303
  16.6 1.1 %copy-done.8 = bf16[3,32,32,128]{3,2,1,0:T(8,128)(2,1)S(1)} copy-done((bf16[3,32,32,128]{3,2,1,0:T(8,128)(2,1)S(1)}, bf16[3,32,32,128]{3,2,1,0:T(8,128)(2,1)}, u32[]{:S(2)}) %copy-start.8) | copy-done | bytes 786456
  19.6 6.3 %own_pixels.1 = (f32[1152,128]{1,0:T(8,128)S(1)}, f32[8,128]{1,0:T(8,128)S(1)}, bf16[3,1024,128]{2,1,0:T(8,128)(2,1)S(1)}, bf16[4,192,128]{2,1,0:T(8,128)(2,1)S(...) custom-call(s32[1]{0:T(128)} %bitcast.3.me_ref, ...), custom_call_target="tpu_custom_call" | custom-call | flops 1811939328 | bytes 2359296 | tf_op jit(solution)/shard_map/own_pixels/pallas_call | solution.py:367
  26.6 1.8 %halo_kernel_grad.1 = (f32[1280,128]{1,0:T(8,128)S(1)}, bf16[4,192,384]{2,1,0:T(8,128)(2,1)S(1)}) custom-call(s32[1]{0:T(128)} %bitcast.3.me_ref, s32[3,8]{1,0:T(4,128)S(1)} %copy-done.5, s32[3,8]{1,0:T(4,128)S(1)} %copy-done.6, s32[3,8]{1,0:T(4,128)S(1)} %copy-done.7, bf16[12,64,128]{2,1,0:T(8,128)(2,1)S(1)} %pack_edges.1.own_ref, ...), custom_call_target="tpu_custom_call" | custom-call | flops 113246208 | bytes 786432 | tf_op jit(solution)/shard_map/halo_kernel_grad/pallas_call | solution.py:387
  30.0 1.3 %collective-permute-done.7 = f32[640,128]{1,0:T(8,128)S(1)} collective-permute-done((f32[640,128]{1,0:T(8,128)S(1)}, f32[640,128]{1,0:T(8,128)S(1)}, u32[]{:S(2)}, u32[]{:S(2)}) %collective-permute-start.7) | collective-permute-done | bytes 327712 | tf_op jit(solution)/shard_map/ppermute | solution.py:307
  33.7 2.5 %collective-permute-start.8 = (bf16[160,128]{1,0:T(8,128)(2,1)}, bf16[160,128]{1,0:T(8,128)(2,1)}, u32[]{:S(2)}, u32[]{:S(2)}) collective-permute-start(bf16[160,128]{1,0:T(8,128)(2,1)} %get-tuple-element.30), channel_id=1, source_target_pairs={{0,2},{1,3},{2,0},{3,1},{4,6},{5,7},{6,4},{7,5},{8,10},{9,11},{10,... | collective-permute-start | bytes 122888 | tf_op jit(solution)/shard_map/ppermute | solution.py:307
  36.5 1.6 %collective-permute-done.10 = bf16[160,128]{1,0:T(8,128)(2,1)S(1)} collective-permute-done((bf16[160,128]{1,0:T(8,128)(2,1)}, bf16[160,128]{1,0:T(8,128)(2,1)S(1)}, u32[]{:S(2)}, u32[]{:S(2)}) %collective-permute-start.10) | collective-permute-done | bytes 40992 | tf_op jit(solution)/shard_map/ppermute | solution.py:307
  38.1 1.1 %collective-permute-done.8 = bf16[160,128]{1,0:T(8,128)(2,1)} collective-permute-done((bf16[160,128]{1,0:T(8,128)(2,1)}, bf16[160,128]{1,0:T(8,128)(2,1)}, u32[]{:S(2)}, u32[]{:S(2)}) %collective-permute-start.8) | collective-permute-done | bytes 40992 | tf_op jit(solution)/shard_map/ppermute | solution.py:307
  41.1 1.3 %collective-permute-start.11 = (bf16[160,128]{1,0:T(8,128)(2,1)S(1)}, bf16[160,128]{1,0:T(8,128)(2,1)S(1)}, u32[]{:S(2)}, u32[]{:S(2)}) collective-permute-start(bf16[160,128]{1,0:T(8,128)(2,1)S(1)} %add_convert_fusion), channel_id=1, source_target_pairs={{0,8},{1,9},{2,10},{3,11},{4,12},{5,13},{6,14},{7,15},{8,0},{9,1},... | collective-permute-start | bytes 122888 | tf_op jit(solution)/shard_map/ppermute | solution.py:307
  42.4 2.6 %collective-permute-start.12 = (bf16[160,128]{1,0:T(8,128)(2,1)S(1)}, bf16[160,128]{1,0:T(8,128)(2,1)S(1)}, u32[]{:S(2)}, u32[]{:S(2)}) collective-permute-start(bf16[160,128]{1,0:T(8,128)(2,1)S(1)} %add_convert_fusion), channel_id=1, source_target_pairs={{0,16},{1,17},{2,18},{3,19},{4,20},{5,21},{6,22},{7,23},{8,24},{9,... | collective-permute-start | bytes 122888 | tf_op jit(solution)/shard_map/ppermute | solution.py:307
  45.6 2.2 %collective-permute-done.12 = bf16[160,128]{1,0:T(8,128)(2,1)S(1)} collective-permute-done((bf16[160,128]{1,0:T(8,128)(2,1)S(1)}, bf16[160,128]{1,0:T(8,128)(2,1)S(1)}, u32[]{:S(2)}, u32[]{:S(2)}) %collective-permute-start.12) | collective-permute-done | bytes 40992 | tf_op jit(solution)/shard_map/ppermute | solution.py:307
  47.8 3.0 %collective-permute-done.13 = bf16[160,128]{1,0:T(8,128)(2,1)S(1)} collective-permute-done((bf16[160,128]{1,0:T(8,128)(2,1)S(1)}, bf16[160,128]{1,0:T(8,128)(2,1)S(1)}, u32[]{:S(2)}, u32[]{:S(2)}) %collective-permute-start.13) | collective-permute-done | bytes 40992 | tf_op jit(solution)/shard_map/ppermute | solution.py:307
  51.5 1.5 %collective-permute-start.16 = (f32[160,128]{1,0:T(8,128)}, f32[160,128]{1,0:T(8,128)}, u32[]{:S(2)}, u32[]{:S(2)}) collective-permute-start(f32[160,128]{1,0:T(8,128)} %add_add_fusion), channel_id=1, source_target_pairs={{0,6},{1,7},{2,4},{3,5},{4,2},{5,3},{6,0},{7,1},{8,14},{9,15},{10,... | collective-permute-start | bytes 245768 | tf_op jit(solution)/shard_map/ppermute | solution.py:307
  53.5 1.4 %collective-permute-start.15 = (f32[160,128]{1,0:T(8,128)}, f32[160,128]{1,0:T(8,128)}, u32[]{:S(2)}, u32[]{:S(2)}) collective-permute-start(f32[160,128]{1,0:T(8,128)} %add_add_fusion), channel_id=1, source_target_pairs={{0,4},{1,5},{2,6},{3,7},{4,0},{5,1},{6,2},{7,3},{8,12},{9,13},{10,... | collective-permute-start | bytes 245768 | tf_op jit(solution)/shard_map/ppermute | solution.py:307
  55.0 2.2 %collective-permute-done.16 = f32[160,128]{1,0:T(8,128)} collective-permute-done((f32[160,128]{1,0:T(8,128)}, f32[160,128]{1,0:T(8,128)}, u32[]{:S(2)}, u32[]{:S(2)}) %collective-permute-start.16) | collective-permute-done | bytes 81952 | tf_op jit(solution)/shard_map/ppermute | solution.py:307
  59.6 1.5 %collective-permute-start.5 = (bf16[12,64,128]{2,1,0:T(8,128)(2,1)S(1)}, bf16[12,64,128]{2,1,0:T(8,128)(2,1)S(1)}, u32[]{:S(2)}, u32[]{:S(2)}) collective-permute-start(bf16[12,64,128]{2,1,0:T(8,128)(2,1)S(1)} %get-tuple-element.23), channel_id=1, source_target_pairs={{0,2},{1,3},{2,4},{3,5},{4,6},{5,7},{6,8},{7,9},{8,10},{9,11},{10,... | collective-permute-start | bytes 589832 | tf_op jit(solution)/shard_map/ppermute | solution.py:303
  61.2 4.1 %collective-permute-start.6 = (bf16[12,64,128]{2,1,0:T(8,128)(2,1)S(1)}, bf16[12,64,128]{2,1,0:T(8,128)(2,1)S(1)}, u32[]{:S(2)}, u32[]{:S(2)}) collective-permute-start(bf16[12,64,128]{2,1,0:T(8,128)(2,1)S(1)} %get-tuple-element.22), channel_id=1, source_target_pairs={{0,30},{1,31},{2,0},{3,1},{4,2},{5,3},{6,4},{7,5},{8,6},{9,7},{10,... | collective-permute-start | bytes 589832 | tf_op jit(solution)/shard_map/ppermute | solution.py:303
  66.0 3.3 %forward.1 = bf16[3,1024,128]{2,1,0:T(8,128)(2,1)} custom-call(bf16[3,1024,128]{2,1,0:T(8,128)(2,1)S(1)} %bitcast.24, bf16[9,128,128]{2,1,0:T(8,128)(2,1)S(1)} %bitcast.27, f32[1,128]{1,0:T(1,128)S(1)} %bitcast.28, bf16[4,192,384]{2,1,0:T(8,128)(2,1)S(1)} %copy-done.10), custom_call_target="tpu_custom_call" | custom-call | flops 905969664 | bytes 1572864 | tf_op jit(solution)/shard_map/forward/pallas_call | solution.py:400
  69.3 1.4 %collective-permute-done.5.low_ref = bf16[12,64,128]{2,1,0:T(8,128)(2,1)S(1)} collective-permute-done((bf16[12,64,128]{2,1,0:T(8,128)(2,1)S(1)}, bf16[12,64,128]{2,1,0:T(8,128)(2,1)S(1)}, u32[]{:S(2)}, u32[]{:S(2)}) %collective-permute-start.5) | collective-permute-done | bytes 196640 | tf_op jit(solution)/shard_map/ppermute | solution.py:303
  70.7 1.4 %collective-permute-done.6.high_ref = bf16[12,64,128]{2,1,0:T(8,128)(2,1)S(1)} collective-permute-done((bf16[12,64,128]{2,1,0:T(8,128)(2,1)S(1)}, bf16[12,64,128]{2,1,0:T(8,128)(2,1)S(1)}, u32[]{:S(2)}, u32[]{:S(2)}) %collective-permute-start.6) | collective-permute-done | bytes 196640 | tf_op jit(solution)/shard_map/ppermute | solution.py:303
  72.0 1.4 %join_input_grad.1 = bf16[3,1024,128]{2,1,0:T(8,128)(2,1)} custom-call(bf16[3,1024,128]{2,1,0:T(8,128)(2,1)S(1)} %get-tuple-element.17.dx_ref, f32[12,64,128]{2,1,0:T(8,128)S(1)} %get-tuple-element.18.own_ref, bf16[12,64,128]{2,1,0:T(8,128)(2,1)S(1)} %slice.24.mate_ref, bf16[12,64,128]{2,1,0:T(8,128)(2,1)S(1)} %collective-permute-done.5.low_ref, ...), custom_call_target="tpu_custom_call" | custom-call | bytes 1966080 | tf_op jit(solution)/shard_map/join_input_grad/pallas_call | solution.py:413
  (65 shorter events, 17.7 us)
Async XLA Ops:
  1.8 14.2 %copy-start.1 = (bf16[3,32,32,128]{3,2,1,0:T(8,128)(2,1)S(1)}, bf16[3,32,32,128]{3,2,1,0:T(8,128)(2,1)}, u32[]{:S(2)}) copy-start(bf16[3,32,32,128]{3,2,1,0:T(8,128)(2,1)} %param.10) | copy-start | bytes 2359300
  1.9 12.0 %collective-permute-start = (bf16[12,64,128]{2,1,0:T(8,128)(2,1)S(1)}, bf16[12,64,128]{2,1,0:T(8,128)(2,1)S(1)}, u32[]{:S(2)}, u32[]{:S(2)}) collective-permute-start(bf16[12,64,128]{2,1,0:T(8,128)(2,1)S(1)} %pack_edges.1.own_ref), channel_id=1, source_target_pairs={{0,2},{1,3},{2,4},{3,5},{4,6},{5,7},{6,8},{7,9},{8,10},{9,11},{10,... | collective-permute-start | bytes 589832 | tf_op jit(solution)/shard_map/ppermute | solution.py:303
  4.9 10.3 %collective-permute-start.1 = (bf16[12,64,128]{2,1,0:T(8,128)(2,1)S(1)}, bf16[12,64,128]{2,1,0:T(8,128)(2,1)S(1)}, u32[]{:S(2)}, u32[]{:S(2)}) collective-permute-start(bf16[12,64,128]{2,1,0:T(8,128)(2,1)S(1)} %pack_edges.1.own_ref), channel_id=1, source_target_pairs={{0,30},{1,31},{2,0},{3,1},{4,2},{5,3},{6,4},{7,5},{8,6},{9,7},{10,... | collective-permute-start | bytes 589832 | tf_op jit(solution)/shard_map/ppermute | solution.py:303
  9.0 17.6 %collective-permute-start.2 = (bf16[12,64,128]{2,1,0:T(8,128)(2,1)S(1)}, bf16[12,64,128]{2,1,0:T(8,128)(2,1)S(1)}, u32[]{:S(2)}, u32[]{:S(2)}) collective-permute-start(bf16[12,64,128]{2,1,0:T(8,128)(2,1)S(1)} %pack_edges.1.own_ref), channel_id=1, source_target_pairs={{0,1},{1,0},{2,3},{3,2},{4,5},{5,4},{6,7},{7,6},{8,9},{9,8},{10,11... | collective-permute-start | bytes 589832 | tf_op jit(solution)/shard_map/ppermute | solution.py:307
  16.0 10.7 %collective-permute-start.3 = (bf16[12,64,128]{2,1,0:T(8,128)(2,1)}, bf16[12,64,128]{2,1,0:T(8,128)(2,1)}, u32[]{:S(2)}, u32[]{:S(2)}) collective-permute-start(bf16[12,64,128]{2,1,0:T(8,128)(2,1)} %broadcast_select_fusion), channel_id=1, source_target_pairs={{0,1},{1,0},{2,3},{3,2},{4,5},{5,4},{6,7},{7,6},{8,9},{9,8},{10,11... | collective-permute-start | bytes 589832 | tf_op jit(solution)/shard_map/ppermute | solution.py:307
  19.6 7.1 %copy-start.3 = (bf16[4,192,64]{2,1,0:T(8,128)(2,1)S(1)}, bf16[4,192,64]{2,1,0:T(8,128)(2,1)}, u32[]{:S(2)}) copy-start(bf16[4,192,64]{2,1,0:T(8,128)(2,1)} %constant.68.clone.side_ref) | copy-start | bytes 294916
  19.6 7.1 %copy-start.4 = (bf16[4,128,64]{2,1,0:T(8,128)(2,1)S(1)}, bf16[4,128,64]{2,1,0:T(8,128)(2,1)}, u32[]{:S(2)}) copy-start(bf16[4,128,64]{2,1,0:T(8,128)(2,1)} %constant.69.clone.end_ref) | copy-start | bytes 196612
  29.5 1.8 %collective-permute-start.7 = (f32[640,128]{1,0:T(8,128)S(1)}, f32[640,128]{1,0:T(8,128)S(1)}, u32[]{:S(2)}, u32[]{:S(2)}) collective-permute-start(f32[640,128]{1,0:T(8,128)S(1)} %constant_dynamic-slice_fusion), channel_id=1, source_target_pairs={{0,1},{1,0},{2,3},{3,2},{4,5},{5,4},{6,7},{7,6},{8,9},{9,8},{10,11... | collective-permute-start | bytes 983048 | tf_op jit(solution)/shard_map/ppermute | solution.py:307
  32.3 22.7 %copy-start.12 = (bf16[24,64,128]{2,1,0:T(8,128)(2,1)S(1)}, bf16[24,64,128]{2,1,0:T(8,128)(2,1)}, u32[]{:S(2)}) copy-start(bf16[24,64,128]{2,1,0:T(8,128)(2,1)} %copy-done.11) | copy-start | bytes 1179652
  33.0 5.1 %collective-permute-start.10 = (bf16[160,128]{1,0:T(8,128)(2,1)}, bf16[160,128]{1,0:T(8,128)(2,1)S(1)}, u32[]{:S(2)}, u32[]{:S(2)}) collective-permute-start(bf16[160,128]{1,0:T(8,128)(2,1)} %get-tuple-element.31), channel_id=1, source_target_pairs={{0,6},{1,7},{2,4},{3,5},{4,2},{5,3},{6,0},{7,1},{8,14},{9,15},{10,... | collective-permute-start | bytes 122888 | tf_op jit(solution)/shard_map/ppermute | solution.py:307
  33.7 5.5 %collective-permute-start.8 = (bf16[160,128]{1,0:T(8,128)(2,1)}, bf16[160,128]{1,0:T(8,128)(2,1)}, u32[]{:S(2)}, u32[]{:S(2)}) collective-permute-start(bf16[160,128]{1,0:T(8,128)(2,1)} %get-tuple-element.30), channel_id=1, source_target_pairs={{0,2},{1,3},{2,0},{3,1},{4,6},{5,7},{6,4},{7,5},{8,10},{9,11},{10,... | collective-permute-start | bytes 122888 | tf_op jit(solution)/shard_map/ppermute | solution.py:307
  36.2 4.1 %collective-permute-start.9 = (bf16[160,128]{1,0:T(8,128)(2,1)S(1)}, bf16[160,128]{1,0:T(8,128)(2,1)}, u32[]{:S(2)}, u32[]{:S(2)}) collective-permute-start(bf16[160,128]{1,0:T(8,128)(2,1)S(1)} %get-tuple-element.32), channel_id=1, source_target_pairs={{0,4},{1,5},{2,6},{3,7},{4,0},{5,1},{6,2},{7,3},{8,12},{9,13},{10,... | collective-permute-start | bytes 122888 | tf_op jit(solution)/shard_map/ppermute | solution.py:307
  41.1 4.5 %collective-permute-start.11 = (bf16[160,128]{1,0:T(8,128)(2,1)S(1)}, bf16[160,128]{1,0:T(8,128)(2,1)S(1)}, u32[]{:S(2)}, u32[]{:S(2)}) collective-permute-start(bf16[160,128]{1,0:T(8,128)(2,1)S(1)} %add_convert_fusion), channel_id=1, source_target_pairs={{0,8},{1,9},{2,10},{3,11},{4,12},{5,13},{6,14},{7,15},{8,0},{9,1},... | collective-permute-start | bytes 122888 | tf_op jit(solution)/shard_map/ppermute | solution.py:307
  42.4 5.3 %collective-permute-start.12 = (bf16[160,128]{1,0:T(8,128)(2,1)S(1)}, bf16[160,128]{1,0:T(8,128)(2,1)S(1)}, u32[]{:S(2)}, u32[]{:S(2)}) collective-permute-start(bf16[160,128]{1,0:T(8,128)(2,1)S(1)} %add_convert_fusion), channel_id=1, source_target_pairs={{0,16},{1,17},{2,18},{3,19},{4,20},{5,21},{6,22},{7,23},{8,24},{9,... | collective-permute-start | bytes 122888 | tf_op jit(solution)/shard_map/ppermute | solution.py:307
  45.0 5.8 %collective-permute-start.13 = (bf16[160,128]{1,0:T(8,128)(2,1)S(1)}, bf16[160,128]{1,0:T(8,128)(2,1)S(1)}, u32[]{:S(2)}, u32[]{:S(2)}) collective-permute-start(bf16[160,128]{1,0:T(8,128)(2,1)S(1)} %add_convert_fusion), channel_id=1, source_target_pairs={{0,24},{1,25},{2,26},{3,27},{4,28},{5,29},{6,30},{7,31},{8,16},{9,... | collective-permute-start | bytes 122888 | tf_op jit(solution)/shard_map/ppermute | solution.py:307
  51.5 5.7 %collective-permute-start.16 = (f32[160,128]{1,0:T(8,128)}, f32[160,128]{1,0:T(8,128)}, u32[]{:S(2)}, u32[]{:S(2)}) collective-permute-start(f32[160,128]{1,0:T(8,128)} %add_add_fusion), channel_id=1, source_target_pairs={{0,6},{1,7},{2,4},{3,5},{4,2},{5,3},{6,0},{7,1},{8,14},{9,15},{10,... | collective-permute-start | bytes 245768 | tf_op jit(solution)/shard_map/ppermute | solution.py:307
  53.0 4.8 %collective-permute-start.14 = (f32[160,128]{1,0:T(8,128)}, f32[160,128]{1,0:T(8,128)}, u32[]{:S(2)}, u32[]{:S(2)}) collective-permute-start(f32[160,128]{1,0:T(8,128)} %add_add_fusion), channel_id=1, source_target_pairs={{0,2},{1,3},{2,0},{3,1},{4,6},{5,7},{6,4},{7,5},{8,10},{9,11},{10,... | collective-permute-start | bytes 245768 | tf_op jit(solution)/shard_map/ppermute | solution.py:307
  53.5 4.8 %collective-permute-start.15 = (f32[160,128]{1,0:T(8,128)}, f32[160,128]{1,0:T(8,128)}, u32[]{:S(2)}, u32[]{:S(2)}) collective-permute-start(f32[160,128]{1,0:T(8,128)} %add_add_fusion), channel_id=1, source_target_pairs={{0,4},{1,5},{2,6},{3,7},{4,0},{5,1},{6,2},{7,3},{8,12},{9,13},{10,... | collective-permute-start | bytes 245768 | tf_op jit(solution)/shard_map/ppermute | solution.py:307
  55.0 4.5 %collective-permute-start.4 = (bf16[24,64,128]{2,1,0:T(8,128)(2,1)S(1)}, bf16[24,64,128]{2,1,0:T(8,128)(2,1)S(1)}, u32[]{:S(2)}, u32[]{:S(2)}) collective-permute-start(bf16[24,64,128]{2,1,0:T(8,128)(2,1)S(1)} %copy-done.12), channel_id=1, source_target_pairs={{0,1},{1,0},{2,3},{3,2},{4,5},{5,4},{6,7},{7,6},{8,9},{9,8},{10,11... | collective-permute-start | bytes 1179656 | tf_op jit(solution)/shard_map/ppermute | solution.py:307
  59.4 14.0 %collective-permute-start.17 = (f32[640,128]{1,0:T(8,128)S(1)}, f32[640,128]{1,0:T(8,128)S(1)}, u32[]{:S(2)}, u32[]{:S(2)}) collective-permute-start(f32[640,128]{1,0:T(8,128)S(1)} %pad_maximum_fusion.2), channel_id=1, source_target_pairs={{0,1},{1,0},{2,3},{3,2},{4,5},{5,4},{6,7},{7,6},{8,9},{9,8},{10,11... | collective-permute-start | bytes 983048 | tf_op jit(solution)/shard_map/ppermute | solution.py:307
  59.5 5.8 %copy-start.10 = (bf16[4,192,384]{2,1,0:T(8,128)(2,1)S(1)}, bf16[4,192,384]{2,1,0:T(8,128)(2,1)}, u32[]{:S(2)}) copy-start(bf16[4,192,384]{2,1,0:T(8,128)(2,1)} %copy-done.9) | copy-start | bytes 1769476
  59.6 5.7 %copy-start.14 = (bf16[3,3,128,128]{3,2,1,0:T(8,128)(2,1)S(1)}, bf16[3,3,128,128]{3,2,1,0:T(8,128)(2,1)}, u32[]{:S(2)}) copy-start(bf16[3,3,128,128]{3,2,1,0:T(8,128)(2,1)} %param.12) | copy-start | bytes 884740
  59.6 11.0 %collective-permute-start.5 = (bf16[12,64,128]{2,1,0:T(8,128)(2,1)S(1)}, bf16[12,64,128]{2,1,0:T(8,128)(2,1)S(1)}, u32[]{:S(2)}, u32[]{:S(2)}) collective-permute-start(bf16[12,64,128]{2,1,0:T(8,128)(2,1)S(1)} %get-tuple-element.23), channel_id=1, source_target_pairs={{0,2},{1,3},{2,4},{3,5},{4,6},{5,7},{6,8},{7,9},{8,10},{9,11},{10,... | collective-permute-start | bytes 589832 | tf_op jit(solution)/shard_map/ppermute | solution.py:303
  61.2 10.9 %collective-permute-start.6 = (bf16[12,64,128]{2,1,0:T(8,128)(2,1)S(1)}, bf16[12,64,128]{2,1,0:T(8,128)(2,1)S(1)}, u32[]{:S(2)}, u32[]{:S(2)}) collective-permute-start(bf16[12,64,128]{2,1,0:T(8,128)(2,1)S(1)} %get-tuple-element.22), channel_id=1, source_target_pairs={{0,30},{1,31},{2,0},{3,1},{4,2},{5,3},{6,4},{7,5},{8,6},{9,7},{10,... | collective-permute-start | bytes 589832 | tf_op jit(solution)/shard_map/ppermute | solution.py:303
  (11 other events, 9.4 us)

commit v2 on v1

v2 whole, which is shorter than its diff:
```python
import functools
import math

import jax
import jax.numpy as jnp
import numpy as np
from jax import lax
from jax.experimental import pallas as pl
from jax.experimental.pallas import tpu as pltpu
from jax.sharding import PartitionSpec as P

ROOM = 12
BF = jnp.bfloat16
F32 = jnp.float32

DIRECTIONS = ((-1, -1), (-1, 0), (-1, 1), (0, -1), (0, 1), (1, -1), (1, 0), (1, 1))
SIDE_TABLE = (
    ((0, 0), (3, 1), (1, 3), (2, 2)),
    ((1, 0), (2, 1), (0, 3), (3, 2)),
    ((2, 0), (0, 2), (3, 3), (1, 1)),
    ((3, 0), (1, 2), (2, 3), (0, 1)),
)
SIDE_DIRECTION = (1, 6, 3, 4)
SIDE_ENDS = ((0, 2), (5, 7))
SIDE_TAPS = (((0, 0), (0, 1), (0, 2)), ((2, 0), (2, 1), (2, 2)), ((0, 0), (1, 0), (2, 0)), ((0, 2), (1, 2), (2, 2)))


def wanted_side(row_step, col_step):
    if row_step < 0:
        return 1
    if row_step > 0:
        return 0
    return 3 if col_step < 0 else 2


def flip_tables(length):
    size = 2 * length
    flips = np.zeros((4, size, size), np.float32)
    for code in range(4):
        for r in range(2):
            for k in range(length):
                rr = 1 - r if code & 1 else r
                kk = length - 1 - k if code & 2 else k
                flips[code, r * length + k, rr * length + kk] = 1
    back = np.zeros((2, size, size), np.float32)
    ahead = np.zeros((2, size, size), np.float32)
    for r in range(2):
        for k in range(length):
            back[int(k < 2), r * length + k, r * length + (k - 2) % length] = 1
            ahead[int(k >= length - 2), r * length + k, r * length + (k + 2) % length] = 1
    sides = np.stack([np.concatenate([back[0] @ f, f, ahead[0] @ f]) for f in flips])
    ends = np.stack([np.concatenate([back[1] @ f, ahead[1] @ f]) for f in flips])
    return flips, sides, ends


def place_of(me, neighbour, rotation, which, patches_here, devices):
    owner = lax.div(neighbour, patches_here)
    within = neighbour - owner * patches_here
    offset = owner - me
    offset = jnp.where(offset < 0, offset + devices, offset)
    core = lax.rem(me, 2)
    to_mate = jnp.where(core == 0, 1, devices - 1)
    block = jnp.where(offset == to_mate, 3, 4)
    block = jnp.where(offset == 2, 2, block)
    block = jnp.where(offset == devices - 2, 1, block)
    block = jnp.where(offset == 0, 0, block)
    slot, code = SIDE_TABLE[which][0]
    for k in range(1, 4):
        slot = jnp.where(rotation == k, SIDE_TABLE[which][k][0], slot)
        code = jnp.where(rotation == k, SIDE_TABLE[which][k][1], code)
    return (block * patches_here + within) * 4 + slot, code


def dot(a, b):
    return jnp.dot(a, b, preferred_element_type=F32)


def column_strip(wide_ref, first, length):
    return jnp.concatenate([wide_ref[pl.ds(first + c, length, stride=length), :] for c in range(2)], axis=0)


def add_columns(wide_ref, first, length, strip):
    for c in range(2):
        at = pl.ds(first + c, length, stride=length)
        wide_ref[at, :] = wide_ref[at, :] + strip[c * length : (c + 1) * length]


def spread(ext_ref, wide, length):
    count = length * length
    column = lax.broadcasted_iota(jnp.int32, (count, 1), 0) & (length - 1)
    pad = 2 * length
    back = jnp.where(column >= 2, pltpu.roll(wide, 2, 0), 0.0)
    ahead = jnp.where(column < length - 2, pltpu.roll(wide, count - 2, 0), 0.0)
    ext_ref[pad : pad + count, 0:128] = back.astype(BF)
    ext_ref[pad : pad + count, 128:256] = wide.astype(BF)
    ext_ref[pad : pad + count, 256:384] = ahead.astype(BF)


def clear_rows(ext_ref, length):
    pad = 2 * length
    empty = jnp.zeros((pad, 384), BF)
    ext_ref[0:pad, :] = empty
    ext_ref[pad + length * length :, :] = empty


def begin(source, target, sem):
    copy = pltpu.make_async_copy(source, target, sem)
    copy.start()
    return copy


def finish(copies):
    for copy in copies:
        copy.wait()


def pack_kernel(x_ref, out_ref, x_vm, out_vm, wide_ref, sems, *, length):
    count = length * length
    patches = x_vm.shape[0]
    arriving = [begin(x_ref.at[p], x_vm.at[p], sems.at[p]) for p in range(patches)]
    leaving = []
    for p in range(patches):
        arriving[p].wait()
        out_vm[4 * p] = x_vm[p, 0 : 2 * length, :]
        out_vm[4 * p + 1] = x_vm[p, count - 2 * length :, :]
        wide_ref[...] = x_vm[p].astype(F32)
        out_vm[4 * p + 2] = column_strip(wide_ref, 0, length).astype(BF)
        out_vm[4 * p + 3] = column_strip(wide_ref, length - 2, length).astype(BF)
        rows = pl.ds(4 * p, 4)
        leaving.append(begin(out_vm.at[rows], out_ref.at[rows], sems.at[patches + p]))
    finish(leaving)


def own_kernel(
    me_ref, nb_ref, rot_ref, cor_ref, x_ref, cot_ref, w_ref, bias_in_ref, flip_ref,
    strips_ref, own_ref, far_ref, near_ref, dw_ref, dx_ref, mid_ref,
    nb_sm, rot_sm, cor_sm, x_vm, cot_vm, w_vm, bias_in_vm, flip_vm,
    strips_vm, near_vm, dw_vm, dx_vm, mid_vm, ext_ref, wide_ref, pool_ref, sems, *, length, devices,
):
    patches = x_vm.shape[0]
    count = length * length
    size = 2 * length
    block = 4 * patches
    chunk = min(count, 256)
    sources = [nb_ref, rot_ref, cor_ref, w_ref, bias_in_ref, flip_ref]
    targets = [nb_sm, rot_sm, cor_sm, w_vm, bias_in_vm, flip_vm]
    arriving = [begin(a, b, sems.at[i]) for i, (a, b) in enumerate(zip(sources, targets))]
    used = len(arriving)
    cots = [begin(cot_ref.at[p], cot_vm.at[p], sems.at[used + p]) for p in range(patches)]
    used += patches
    xs = [begin(x_ref.at[p], x_vm.at[p], sems.at[used + p]) for p in range(patches)]
    used += patches
    leaving = []
    me = me_ref[0]
    pool_ref[...] = jnp.zeros_like(pool_ref)
    clear_rows(ext_ref, length)
    along = lax.broadcasted_iota(jnp.int32, (length, 1), 0)
    finish(arriving)
    taps = [jnp.concatenate([w_vm[a * 3 + b] for a, b in SIDE_TAPS[s]], axis=0) for s in range(4)]
    for p in range(patches):
        cots[p].wait()
        wide_ref[...] = cot_vm[p].astype(F32)
        strips = [
            cot_vm[p, 0:size, :],
            cot_vm[p, count - size :, :],
            column_strip(wide_ref, 0, length).astype(BF),
            column_strip(wide_ref, length - 2, length).astype(BF),
        ]
        for s in range(4):
            strips_vm[s, size * p : size * (p + 1), :] = strips[s]
            terms = lax.dot_general(strips[s], taps[s], (((1,), (1,)), ((), ())), preferred_element_type=F32)
            side, first, last = [], [], []
            for r in range(2):
                rows = slice(r * length, (r + 1) * length)
                ahead = pltpu.roll(terms[rows, 0:128], length - 2, 0)
                back = pltpu.roll(terms[rows, 256:384], 2, 0)
                side.append(
                    terms[rows, 128:256]
                    + jnp.where(along < length - 2, ahead, 0.0)
                    + jnp.where(along >= 2, back, 0.0)
                )
                first.append(jnp.where(along >= length - 2, ahead, 0.0))
                last.append(jnp.where(along < 2, back, 0.0))
            sent = [(SIDE_DIRECTION[s], side)]
            if s < 2:
                sent += [(SIDE_ENDS[s][0], first), (SIDE_ENDS[s][1], last)]
            for j, term in sent:
                where_to, code = place_of(
                    me, nb_sm[p, j], rot_sm[p, j], wanted_side(*DIRECTIONS[j]), patches, devices
                )
                value = dot(flip_vm[code], jnp.concatenate(term, axis=0).astype(BF))
                value = value * (cor_sm[p, j] > 0).astype(F32)
                pool_ref[where_to] = pool_ref[where_to] + value
    near_vm[...] = pool_ref[3 * block :].astype(BF)
    for source, target in (
        (strips_vm, strips_ref), (near_vm, near_ref),
        (pool_ref.at[pl.ds(0, block)], own_ref), (pool_ref.at[pl.ds(block, 2 * block)], far_ref),
    ):
        leaving.append(begin(source, target, sems.at[used]))
        used += 1

    total_bias = jnp.zeros((1, 128), F32)
    flipped = [
        jnp.concatenate([w_vm[(2 - a) * 3 + 2], w_vm[(2 - a) * 3 + 1], w_vm[(2 - a) * 3]], axis=1) for a in range(3)
    ]
    rows_of = [jnp.concatenate([w_vm[a * 3 + b] for b in range(3)], axis=0) for a in range(3)]
    for p in range(patches):
        wide = cot_vm[p].astype(F32)
        total_bias = total_bias + jnp.sum(wide, axis=0, keepdims=True)
        spread(ext_ref, wide, length)
        xs[p].wait()
        turned = x_vm[p].T
        for a in range(3):
            grads = dot(turned, ext_ref[size * a : size * a + count, :])
            for b in range(3):
                tap = (2 - a) * 3 + 2 - b
                rows = slice(tap * 128, (tap + 1) * 128)
                part = grads[:, b * 128 : (b + 1) * 128]
                dw_vm[rows, :] = part if p == 0 else dw_vm[rows, :] + part
        for start in range(0, count, chunk):
            total = None
            for a in range(3):
                at = start + size * a
                part = lax.dot_general(
                    ext_ref[at : at + chunk, :], flipped[a], (((1,), (1,)), ((), ())), preferred_element_type=F32
                )
                total = part if total is None else total + part
            dx_vm[p, start : start + chunk, :] = total.astype(BF)
        leaving.append(begin(dx_vm.at[p], dx_ref.at[p], sems.at[used]))
        used += 1
    dw_vm[9 * 128 :, :] = jnp.zeros((dw_vm.shape[0] - 9 * 128, 128), F32)
    dw_vm[9 * 128 : 9 * 128 + 8, :] = jnp.broadcast_to(total_bias, (8, 128))
    leaving.append(begin(dw_vm, dw_ref, sems.at[used]))
    used += 1
    for p in range(patches):
        spread(ext_ref, x_vm[p].astype(F32), length)
        for start in range(0, count, chunk):
            total = jnp.broadcast_to(bias_in_vm[...], (chunk, 128))
            for a in range(3):
                at = start + size * a
                total = total + dot(ext_ref[at : at + chunk, :], rows_of[a])
            mid_vm[p, start : start + chunk, :] = total
        leaving.append(begin(mid_vm.at[p], mid_ref.at[p], sems.at[used]))
        used += 1
    finish(leaving)


def halo_kernel(
    me_ref, nb_ref, rot_ref, cor_ref, own_ref, low_ref, high_ref, mate_ref, across_ref, strips_ref, dw_ref,
    side_ref, end_ref, keep_ref, send_ref, halo_ref,
    nb_sm, rot_sm, cor_sm, pool_ref, strips_vm, total_ref, side_vm, end_vm, halo_vm, sems, *, length, devices, factor,
):
    block = pool_ref.shape[0] // 5
    patches = block // 4
    sources = [nb_ref, rot_ref, cor_ref, side_ref, end_ref]
    targets = [nb_sm, rot_sm, cor_sm, side_vm, end_vm]
    arriving = [begin(a, b, sems.at[i]) for i, (a, b) in enumerate(zip(sources, targets))]
    used = len(arriving)
    later = [begin(strips_ref, strips_vm, sems.at[used]), begin(dw_ref, total_ref, sems.at[used + 1])]
    used += 2
    for i, source in enumerate((own_ref, low_ref, high_ref, mate_ref, across_ref)):
        pool_ref[i * block : (i + 1) * block] = source[...]
    me = me_ref[0]
    size = 2 * length
    finish(arriving)
    for p in range(patches):

        def fetch(j):
            at, code = place_of(me, nb_sm[p, j], rot_sm[p, j], wanted_side(*DIRECTIONS[j]), patches, devices)
            return pool_ref[at], code

        for s in range(4):
            source, code = fetch(SIDE_DIRECTION[s])
            shifted = dot(side_vm[code], source)
            parts = [shifted[0:size], shifted[size : 2 * size], shifted[2 * size :]]
            if s < 2:
                for which, j in ((0, SIDE_ENDS[s][0]), (1, SIDE_ENDS[s][1])):
                    source, code = fetch(j)
                    corner = dot(end_vm[code, which * size : (which + 1) * size, :], source)
                    parts[2 * which] = parts[2 * which] + corner * (cor_sm[p, j] > 0).astype(F32)
            for i in range(3):
                halo_vm[s, p * size : (p + 1) * size, i * 128 : (i + 1) * 128] = parts[i].astype(BF)
    leaving = [begin(halo_vm, halo_ref, sems.at[used])]
    finish(later)
    for s in range(4):
        grads = lax.dot_general(
            halo_vm[s], strips_vm[s], (((0,), (0,)), ((), ())), preferred_element_type=F32
        )
        for i, (a, b) in enumerate(SIDE_TAPS[s]):
            rows = slice((a * 3 + b) * 128, (a * 3 + b + 1) * 128)
            total_ref[rows, :] = total_ref[rows, :] + grads[i * 128 : (i + 1) * 128]
    half = total_ref.shape[0] // 2
    core = lax.rem(me, 2)
    send_ref[...] = total_ref[pl.ds(pl.multiple_of((1 - core) * half, 128), half), :] * factor
    keep_ref[...] = total_ref[pl.ds(pl.multiple_of(core * half, 128), half), :] * factor
    finish(leaving)


def forward_kernel(mid_ref, w_ref, halo_ref, out_ref, mid_vm, w_vm, halo_vm, out_vm, sems, *, length):
    count = length * length
    size = 2 * length
    patches = mid_vm.shape[0]
    arriving = [begin(w_ref, w_vm, sems.at[0]), begin(halo_ref, halo_vm, sems.at[1])]
    mids = [begin(mid_ref.at[p], mid_vm.at[p], sems.at[2 + p]) for p in range(patches)]
    finish(arriving)
    borders = []
    for s in range(4):
        taps = jnp.concatenate([w_vm[a * 3 + b] for a, b in SIDE_TAPS[s]], axis=0)
        borders.append(dot(halo_vm[s], taps))
    leaving = []
    for p in range(patches):
        mids[p].wait()
        mine = slice(p * size, (p + 1) * size)
        wide_ref = mid_vm.at[p]
        wide_ref[0:size, :] = wide_ref[0:size, :] + borders[0][mine]
        wide_ref[count - size :, :] = wide_ref[count - size :, :] + borders[1][mine]
        add_columns(wide_ref, 0, length, borders[2][mine])
        add_columns(wide_ref, length - 2, length, borders[3][mine])
        out_vm[p] = wide_ref[...].astype(BF)
        leaving.append(begin(out_vm.at[p], out_ref.at[p], sems.at[2 + patches + p]))
    finish(leaving)


def join_kernel(
    dx_ref, own_ref, near_ref, low_ref, high_ref, out_ref,
    dx_vm, own_vm, out_vm, wide_ref, sems, *, length,
):
    count = length * length
    size = 2 * length
    patches = dx_vm.shape[0]
    arriving = [begin(own_ref, own_vm, sems.at[0])]
    used = len(arriving)
    dxs = [begin(dx_ref.at[p], dx_vm.at[p], sems.at[used + p]) for p in range(patches)]
    used += patches
    finish(arriving)
    leaving = []
    for p in range(patches):
        dxs[p].wait()
        wide_ref[...] = dx_vm[p].astype(F32)
        strips = []
        for s in range(4):
            i = 4 * p + s
            strips.append(own_vm[i] + near_ref[i].astype(F32) + low_ref[i].astype(F32) + high_ref[i].astype(F32))
        wide_ref[0:size, :] = wide_ref[0:size, :] + strips[0]
        wide_ref[count - size :, :] = wide_ref[count - size :, :] + strips[1]
        add_columns(wide_ref, 0, length, strips[2])
        add_columns(wide_ref, length - 2, length, strips[3])
        out_vm[p] = wide_ref[...].astype(BF)
        leaving.append(begin(out_vm.at[p], out_ref.at[p], sems.at[used]))
        used += 1
    finish(leaving)


def result_kernel(me_ref, mine_ref, other_ref, grad_ref, bias_ref, sems, *, taps):
    core = lax.rem(me_ref[0], 2)
    half = mine_ref.shape[0]
    rest = taps - half

    def write(low_ref, high_ref):
        leaving = [
            begin(low_ref, grad_ref.at[pl.ds(0, half)], sems.at[0]),
            begin(high_ref.at[pl.ds(0, rest)], grad_ref.at[pl.ds(half, rest)], sems.at[1]),
        ]
        bias_ref[...] = high_ref[rest : rest + 1, :]
        finish(leaving)

    @pl.when(core == 0)
    def _():
        write(mine_ref, other_ref)

    @pl.when(core == 1)
    def _():
        write(other_ref, mine_ref)


def call(kernel, name, operands, outs, scratch, copies, small=(), room=4):
    spaces = {"s": pltpu.SMEM, "h": pltpu.HBM, "a": pl.ANY, "v": pltpu.VMEM}
    out_specs = [pl.BlockSpec(memory_space=pltpu.VMEM if i in small else pl.ANY) for i in range(len(outs))]
    return pl.pallas_call(
        kernel,
        name=name,
        out_shape=list(outs),
        in_specs=[pl.BlockSpec(memory_space=spaces[o]) for o in operands],
        out_specs=out_specs,
        scratch_shapes=list(scratch) + [pltpu.SemaphoreType.DMA((copies,))],
        compiler_params=pltpu.CompilerParams(vmem_limit_bytes=(64 - room) * 1024 * 1024),
        cost_estimate=pl.CostEstimate(flops=0, bytes_accessed=0, transcendentals=0),
    )


def shifted(value, steps):
    count = lax.axis_size("patch")
    return lax.ppermute(value, "patch", [(d, (d + steps) % count) for d in range(count)])


def swapped(value, mask):
    return lax.ppermute(value, "patch", [(d, d ^ mask) for d in range(lax.axis_size("patch"))])


def part_of(value, index, size):
    return lax.dynamic_slice_in_dim(value, index * size, size)


def summed(keep, send, me, devices, between, last):
    mine = keep + swapped(send, 1)
    quarter = mine.shape[0] // 4
    at = (me // 2) % 4
    arrived = [swapped(part_of(mine, at ^ k, quarter).astype(BF), 2 * k) for k in range(1, 4)]
    mine = part_of(mine, at, quarter)
    for a in arrived:
        mine = mine + a.astype(F32)
    step = 8
    while step < devices:
        sent = mine.astype(BF)
        arrived = [swapped(sent, k * step) for k in range(1, 4 if 2 * step < devices else 2)]
        if 4 * step >= devices:
            arrived = between(arrived)
        mine = sent.astype(F32) + arrived[0].astype(F32)
        if len(arrived) > 1:
            mine = mine + (arrived[1].astype(F32) + arrived[2].astype(F32))
        step *= 4
    pieces = jnp.stack([mine] + [swapped(mine, 2 * k) for k in range(1, 4)])
    whole = jnp.concatenate([lax.dynamic_index_in_dim(pieces, at ^ k, 0, False) for k in range(4)])
    whole = last(whole)
    return whole, swapped(whole, 1)


def body(inputs, cotangent, weights, bias_vector, neighbours, rotations, corners):
    patches, length, _, chans = inputs.shape
    devices = lax.axis_size("patch")
    count = length * length
    size = 2 * length
    block = 4 * patches
    rows = 10 * chans
    me = lax.axis_index("patch")
    me_arr = me.reshape(1).astype(jnp.int32)
    core = me % 2
    x = inputs.reshape(patches, count, chans)
    cot = cotangent.reshape(patches, count, chans)
    w = weights.reshape(9, chans, chans)
    flips, sides, ends = (jnp.asarray(t, BF) for t in flip_tables(length))
    shape = jax.ShapeDtypeStruct
    scratch = pltpu.VMEM
    tables = (me_arr, neighbours, rotations, corners)
    table_scratch = [pltpu.SMEM(neighbours.shape, jnp.int32)] * 3

    (edges,) = call(
        functools.partial(pack_kernel, length=length), "pack_edges", "h", [shape((block, size, chans), BF)],
        [scratch(x.shape, BF), scratch((block, size, chans), BF), scratch((count, chans), F32)], 2 * patches,
    )(x)
    from_low = shifted(edges, 2)
    from_high = shifted(edges, -2)
    from_mate = swapped(edges, 1)

    strips, own, far, near, dw, dx, mid = call(
        functools.partial(own_kernel, length=length, devices=devices), "own_pixels", "shhhhhhhh",
        [
            shape((4, patches * size, chans), BF),
            shape((block, size, chans), F32),
            shape((2 * block, size, chans), F32),
            shape((2 * block, size, chans), BF),
            shape((rows, chans), F32),
            shape(x.shape, BF),
            shape(x.shape, F32),
        ],
        table_scratch
        + [
            scratch(x.shape, BF),
            scratch(x.shape, BF),
            scratch(w.shape, BF),
            scratch((1, chans), F32),
            scratch(flips.shape, BF),
            scratch((4, patches * size, chans), BF),
            scratch((2 * block, size, chans), BF),
            scratch((rows, chans), F32),
            scratch(x.shape, BF),
            scratch(x.shape, F32),
            scratch((count + 2 * size, 3 * chans), BF),
            scratch((count, chans), F32),
            scratch((5 * block, size, chans), F32),
        ],
        6 + 4 * patches + 5,
    )(*tables, x, cot, w, bias_vector.reshape(1, chans), flips)
    near_in = swapped(near, 1)

    from_low, from_high, dw = lax.optimization_barrier((from_low, from_high, dw))
    from_across = swapped(jnp.where(core == 0, from_high, from_low), 1)

    cross_terms = near_in[block:].astype(F32)
    to_low = (far[:block] + jnp.where(core == 1, cross_terms, 0.0)).astype(BF)
    to_high = (far[block:] + jnp.where(core == 0, cross_terms, 0.0)).astype(BF)

    factor = 1.0 / (length * math.sqrt(patches * devices))
    keep, send, halo = call(
        functools.partial(halo_kernel, length=length, devices=devices, factor=factor), "halo_kernel_grad",
        "shhhvvvvvaahh",
        [
            shape((rows // 2, chans), F32),
            shape((rows // 2, chans), F32),
            shape((4, patches * size, 3 * chans), BF),
        ],
        table_scratch
        + [
            scratch((5 * block, size, chans), BF),
            scratch(strips.shape, BF),
            scratch((rows, chans), F32),
            scratch(sides.shape, BF),
            scratch(ends.shape, BF),
            scratch((4, patches * size, 3 * chans), BF),
        ],
        8, small=(0, 1), room=ROOM,
    )(*tables, edges, from_low, from_high, from_mate, from_across, strips, dw, sides, ends)

    (outputs,) = call(
        functools.partial(forward_kernel, length=length), "add_halo_outputs", "aha", [shape(x.shape, BF)],
        [scratch(x.shape, F32), scratch(w.shape, BF), scratch(halo.shape, BF), scratch(x.shape, BF)], 2 + 2 * patches, room=ROOM,
    )(mid, w, halo)

    terms_high = shifted(to_low, -2)
    terms_low = shifted(to_high, 2)
    results = {}

    def between(value):
        value, results["high"], results["low"], results["out"] = lax.optimization_barrier(
            (value, terms_high, terms_low, outputs)
        )
        return value

    def last(value):
        (input_grad,) = call(
            functools.partial(join_kernel, length=length), "join_input_grad", "aavvv", [shape(x.shape, BF)],
            [
                scratch(x.shape, BF),
                scratch((block, size, chans), F32),
                scratch(x.shape, BF),
                scratch((count, chans), F32),
            ],
            1 + 2 * patches, room=ROOM,
        )(dx, own, near_in, results["low"], results["high"])
        value, results["in"] = lax.optimization_barrier((value, input_grad))
        return value

    mine, other = summed(keep, send, me, devices, between, last)
    weight_grad, bias_grad = call(
        functools.partial(result_kernel, taps=9 * chans), "order_kernel_grad", "svv",
        [shape((9 * chans, chans), F32), shape((1, chans), F32)], [], 2, small=(1,), room=ROOM,
    )(me_arr, mine, other)
    return (
        results["out"].reshape(inputs.shape),
        results["in"].reshape(inputs.shape),
        weight_grad.reshape(weights.shape),
        bias_grad.reshape(bias_vector.shape),
    )


def solution(mesh):
    in_specs = (
        P("patch", None, None, None),
        P("patch", None, None, None),
        P(),
        P(),
        P("patch", None),
        P("patch", None),
        P("patch", None),
    )
    out_specs = (P("patch", None, None, None), P("patch", None, None, None), P(), P())
    return jax.shard_map(body, mesh=mesh, in_specs=in_specs, out_specs=out_specs, check_vma=False)
```

time: 75.3 us -> 57 us (0.76)
  waiting for transfers between devices: 22.7 us -> 11.8 us
  Pallas kernels: 13 us -> 20.8 us
  local copies, waits for them, and re-layouts: 8.37 us -> 1.05 us
  other arithmetic: 5.25 us -> 0.26 us
  starting transfers between devices: 24.7 us -> 22 us
    ppermute x4, waiting for transfers between devices: 8.98 us -> 0.65 us  [shifted(): lax.ppermute(value, 'patch', [(d, (d + steps) % count) for d in range(cou...]
    pallas_call x4 -> x5, Pallas kernels: 11.1 us -> 17.7 us  [the longest x1 10.5 us: body(): call(functools.partial(own_kernel, length=length, devices=devices), 'own_...]
    unnamed x34 -> x24, local copies, waits for them, and re-layouts: 7.12 us -> 0.98 us
    ppermute x4, starting transfers between devices: 12.7 us -> 9.13 us  [shifted(): lax.ppermute(value, 'patch', [(d, (d + steps) % count) for d in range(cou...]
    ppermute x14, waiting for transfers between devices: 13.7 us -> 11.1 us  [swapped(): lax.ppermute(value, 'patch', [(d, d ^ mask) for d in range(lax.axis_size(...]
    add x2, other arithmetic: 1.66 us -> 0.06 us  [the longest x1 0.03 us: summed(): mine = keep + swapped(send, 1)]
    pallas_call x1, Pallas kernels: 1.83 us -> 3.04 us  [body(): call(functools.partial(halo_kernel, length=length, devices=devices, facto...]
    another operation x1, other arithmetic: 1.03 us -> 0.02 us  [summed(): pieces = jnp.stack([mine] + [swapped(mine, 2 * k) for k in range(1, 4)])]
  transfers between devices with their start and end apart: 18 -> 18, of which waited for: 13 -> 7; matrix products, arithmetic and copies ran while one was open for 3% -> 0% of each run, Pallas kernels for 15% -> 25%
where the time goes in v2:
time: 57 us; the launch traced here: 56.8 us
  starting transfers between devices  22 us (39%)
  Pallas kernels  20.8 us (36%)
  waiting for transfers between devices  11.8 us (21%)
  local copies, waits for them, and re-layouts  1.05 us (2%)
  between operations  0.92 us (2%)
    ppermute x14, starting transfers between devices, swapped(): lax.ppermute(value, 'patch', [(d, d ^ mask) for d in range(lax.axis_size(...  12.9 us
    ppermute x14, waiting for transfers between devices, swapped(): lax.ppermute(value, 'patch', [(d, d ^ mask) for d in range(lax.axis_size(...  11.1 us
    pallas_call x1, Pallas kernels, body(): call(functools.partial(own_kernel, length=length, devices=devices), 'own_...  10.5 us
    ppermute x4, starting transfers between devices, shifted(): lax.ppermute(value, 'patch', [(d, (d + steps) % count) for d in range(cou...  9.13 us
    pallas_call x1, Pallas kernels, body(): call(functools.partial(halo_kernel, length=length, devices=devices, facto...  3.04 us
    pallas_call x1, Pallas kernels, body(): call(functools.partial(forward_kernel, length=length), 'add_halo_outputs'...  2.52 us
    pallas_call x1, Pallas kernels, body(): call(functools.partial(pack_kernel, length=length), 'pack_edges', 'h', [s...  1.93 us
    pallas_call x1, Pallas kernels, last(): call(functools.partial(join_kernel, length=length), 'join_input_grad', 'a...  1.5 us
  transfers between devices with their start and end apart: 18, of which 7 were waited for; matrix products, arithmetic and copies ran while one was open for 0% of the time, Pallas kernels for 25%

profile of v2, /device:TPU:0, one launch (start us, length us, event | category | flops | bytes accessed | tf_op | source)
XLA Modules:
  0.0 56.8 jit_solution(18317196953735156965)
XLA Ops:
  0.7 1.9 %pack_edges.1.own_ref = bf16[12,64,128]{2,1,0:T(8,128)(2,1)} custom-call(bf16[3,1024,128]{2,1,0:T(8,128)(2,1)} %bitcast.23), custom_call_target="tpu_custom_call" | custom-call | tf_op jit(solution)/shard_map/pack_edges/pallas_call | solution.py:447
  2.6 3.0 %collective-permute-start = (bf16[12,64,128]{2,1,0:T(8,128)(2,1)}, bf16[12,64,128]{2,1,0:T(8,128)(2,1)S(1)}, u32[]{:S(2)}, u32[]{:S(2)}) collective-permute-start(bf16[12,64,128]{2,1,0:T(8,128)(2,1)} %pack_edges.1.own_ref), channel_id=1, source_target_pairs={{0,2},{1,3},{2,4},{3,5},{4,6},{5,7},{6,8},{7,9},{8,10},{9,11},{10,... | collective-permute-start | bytes 589832 | tf_op jit(solution)/shard_map/ppermute | solution.py:393
  5.6 4.1 %collective-permute-start.1 = (bf16[12,64,128]{2,1,0:T(8,128)(2,1)}, bf16[12,64,128]{2,1,0:T(8,128)(2,1)S(1)}, u32[]{:S(2)}, u32[]{:S(2)}) collective-permute-start(bf16[12,64,128]{2,1,0:T(8,128)(2,1)} %pack_edges.1.own_ref), channel_id=1, source_target_pairs={{0,30},{1,31},{2,0},{3,1},{4,2},{5,3},{6,4},{7,5},{8,6},{9,7},{10,... | collective-permute-start | bytes 589832 | tf_op jit(solution)/shard_map/ppermute | solution.py:393
  9.7 10.5 %own_pixels.1 = (bf16[4,192,128]{2,1,0:T(8,128)(2,1)}, f32[12,64,128]{2,1,0:T(8,128)}, f32[24,64,128]{2,1,0:T(8,128)}, bf16[24,64,128]{2,1,0:T(8,128)(2,1)}, f32...) custom-call(s32[1]{0:T(128)} %bitcast.me_ref, s32[3,8]{1,0:T(4,128)} %nb_ref.3, ...), custom_call_target="tpu_custom_call" | custom-call | tf_op jit(solution)/shard_map/own_pixels/pallas_call | solution.py:455
  20.2 0.6 collective-permute-start.3
  20.8 1.1 %collective-permute-done.3.across_ref = bf16[12,64,128]{2,1,0:T(8,128)(2,1)S(1)} collective-permute-done((bf16[12,64,128]{2,1,0:T(8,128)(2,1)S(1)}, bf16[12,64,128]{2,1,0:T(8,128)(2,1)S(1)}, u32[]{:S(2)}, u32[]{:S(2)}) %collective-permute-start.3) | collective-permute-done | bytes 196640 | tf_op jit(solution)/shard_map/ppermute | solution.py:397
  21.9 0.9 %copy-done.6 = bf16[4,192,128]{2,1,0:T(8,128)(2,1)S(1)} copy-done((bf16[4,192,128]{2,1,0:T(8,128)(2,1)S(1)}, bf16[4,192,128]{2,1,0:T(8,128)(2,1)}, u32[]{:S(2)}) %copy-start.6) | copy-done | bytes 196632
  22.8 3.0 %halo_kernel_grad.1 = (f32[640,128]{1,0:T(8,128)S(1)}, f32[640,128]{1,0:T(8,128)}, bf16[4,192,384]{2,1,0:T(8,128)(2,1)}) custom-call(s32[1]{0:T(128)} %bitcast.me_ref, s32[3,8]{1,0:T(4,128)S(1)} %copy-done.8, s32[3,8]{1,0:T(4,128)S(1)} %copy-done.9, s32[3,8]{1,0:T(4,128)S(1)} %copy-done.10, bf16[12,64,128]{2,1,0:T(8,128)(2,1)S(1)} %copy-done.2, ...), custom_call_target="tpu_custom_call" | custom-call | tf_op jit(solution)/shard_map/halo_kernel_grad/pallas_call | solution.py:494
  25.9 0.4 collective-permute-start.4
  26.3 0.1 collective-permute-start.11
  26.5 1.3 %collective-permute-done.4 = f32[640,128]{1,0:T(8,128)S(1)} collective-permute-done((f32[640,128]{1,0:T(8,128)}, f32[640,128]{1,0:T(8,128)S(1)}, u32[]{:S(2)}, u32[]{:S(2)}) %collective-permute-start.4) | collective-permute-done | bytes 327712 | tf_op jit(solution)/shard_map/ppermute | solution.py:397
  28.0 3.4 %collective-permute-start.7 = (bf16[160,128]{1,0:T(8,128)(2,1)S(1)}, bf16[160,128]{1,0:T(8,128)(2,1)S(1)}, u32[]{:S(2)}, u32[]{:S(2)}) collective-permute-start(bf16[160,128]{1,0:T(8,128)(2,1)S(1)} %get-tuple-element.57), channel_id=1, source_target_pairs={{0,6},{1,7},{2,4},{3,5},{4,2},{5,3},{6,0},{7,1},{8,14},{9,15},{10,... | collective-permute-start | bytes 122888 | tf_op jit(solution)/shard_map/ppermute | solution.py:397
  31.4 0.1 fusion.3
  31.6 2.0 %collective-permute-start.12 = (bf16[12,64,128]{2,1,0:T(8,128)(2,1)S(1)}, bf16[12,64,128]{2,1,0:T(8,128)(2,1)S(1)}, u32[]{:S(2)}, u32[]{:S(2)}) collective-permute-start(bf16[12,64,128]{2,1,0:T(8,128)(2,1)S(1)} %get-tuple-element.51), channel_id=1, source_target_pairs={{0,30},{1,31},{2,0},{3,1},{4,2},{5,3},{6,4},{7,5},{8,6},{9,7},{10,... | collective-permute-start | bytes 589832 | tf_op jit(solution)/shard_map/ppermute | solution.py:393
  33.6 3.3 %collective-permute-done.7 = bf16[160,128]{1,0:T(8,128)(2,1)S(1)} collective-permute-done((bf16[160,128]{1,0:T(8,128)(2,1)S(1)}, bf16[160,128]{1,0:T(8,128)(2,1)S(1)}, u32[]{:S(2)}, u32[]{:S(2)}) %collective-permute-start.7) | collective-permute-done | bytes 40992 | tf_op jit(solution)/shard_map/ppermute | solution.py:397
  37.1 4.3 %collective-permute-start.9 = (bf16[160,128]{1,0:T(8,128)(2,1)S(1)}, bf16[160,128]{1,0:T(8,128)(2,1)S(1)}, u32[]{:S(2)}, u32[]{:S(2)}) collective-permute-start(bf16[160,128]{1,0:T(8,128)(2,1)S(1)} %add_convert_fusion), channel_id=1, source_target_pairs={{0,16},{1,17},{2,18},{3,19},{4,20},{5,21},{6,22},{7,23},{8,24},{9,... | collective-permute-start | bytes 122888 | tf_op jit(solution)/shard_map/ppermute | solution.py:397
  41.4 2.5 %add_halo_outputs.1 = bf16[3,1024,128]{2,1,0:T(8,128)(2,1)} custom-call(f32[3,1024,128]{2,1,0:T(8,128)} %get-tuple-element.36.mid_ref, bf16[9,128,128]{2,1,0:T(8,128)(2,1)S(1)} %bitcast.22, bf16[4,192,384]{2,1,0:T(8,128)(2,1)S(1)} %copy-done.3), custom_call_target="tpu_custom_call" | custom-call | tf_op jit(solution)/shard_map/add_halo_outputs/pallas_call | solution.py:514
  44.0 0.6 %collective-permute-done.13.low_ref = bf16[12,64,128]{2,1,0:T(8,128)(2,1)S(1)} collective-permute-done((bf16[12,64,128]{2,1,0:T(8,128)(2,1)S(1)}, bf16[12,64,128]{2,1,0:T(8,128)(2,1)S(1)}, u32[]{:S(2)}, u32[]{:S(2)}) %collective-permute-start.13) | collective-permute-done | bytes 196640 | tf_op jit(solution)/shard_map/ppermute | solution.py:393
  44.7 3.6 %collective-permute-start.15 = (f32[160,128]{1,0:T(8,128)S(1)}, f32[160,128]{1,0:T(8,128)S(1)}, u32[]{:S(2)}, u32[]{:S(2)}) collective-permute-start(f32[160,128]{1,0:T(8,128)S(1)} %add_add_fusion), channel_id=1, source_target_pairs={{0,4},{1,5},{2,6},{3,7},{4,0},{5,1},{6,2},{7,3},{8,12},{9,13},{10,... | collective-permute-start | bytes 245768 | tf_op jit(solution)/shard_map/ppermute | solution.py:397
  48.3 1.5 %join_input_grad.1 = bf16[3,1024,128]{2,1,0:T(8,128)(2,1)} custom-call(bf16[3,1024,128]{2,1,0:T(8,128)(2,1)S(1)} %copy-done.1, f32[12,64,128]{2,1,0:T(8,128)S(1)} %copy-done.4, bf16[24,64,128]{2,1,0:T(8,128)(2,1)S(1)} %collective-permute-done.11.near_ref, bf16[12,64,128]{2,1,0:T(8,128)(2,1)S(1)} %collective-permute-done.13.low_ref, ...), custom_call_target="tpu_custom_call" | custom-call | tf_op jit(solution)/shard_map/join_input_grad/pallas_call | solution.py:530
  49.8 1.2 %collective-permute-done.15 = f32[160,128]{1,0:T(8,128)S(1)} collective-permute-done((f32[160,128]{1,0:T(8,128)S(1)}, f32[160,128]{1,0:T(8,128)S(1)}, u32[]{:S(2)}, u32[]{:S(2)}) %collective-permute-start.15) | collective-permute-done | bytes 81952 | tf_op jit(solution)/shard_map/ppermute | solution.py:397
  51.0 2.6 %collective-permute-done.16 = f32[160,128]{1,0:T(8,128)S(1)} collective-permute-done((f32[160,128]{1,0:T(8,128)S(1)}, f32[160,128]{1,0:T(8,128)S(1)}, u32[]{:S(2)}, u32[]{:S(2)}) %collective-permute-start.16) | collective-permute-done | bytes 81952 | tf_op jit(solution)/shard_map/ppermute | solution.py:397
  53.8 1.6 %collective-permute-done.17.other_ref = f32[640,128]{1,0:T(8,128)S(1)} collective-permute-done((f32[640,128]{1,0:T(8,128)S(1)}, f32[640,128]{1,0:T(8,128)S(1)}, u32[]{:S(2)}, u32[]{:S(2)}) %collective-permute-start.17) | collective-permute-done | bytes 327712 | tf_op jit(solution)/shard_map/ppermute | solution.py:397
  55.4 1.3 %order_kernel_grad.1 = (f32[1152,128]{1,0:T(8,128)}, f32[1,128]{1,0:T(1,128)}) custom-call(s32[1]{0:T(128)} %bitcast.me_ref, f32[640,128]{1,0:T(8,128)S(1)} %pad_maximum_fusion.1.mine_ref, f32[640,128]{1,0:T(8,128)S(1)} %collective-permute-done.17.other_ref), custom_call_target="tpu_custom_call" | custom-call | tf_op jit(solution)/shard_map/order_kernel_grad/pallas_call | solution.py:544
  (51 shorter events, 0.8 us)
Async XLA Ops:
  0.6 21.2 %copy-start.5 = (bf16[4,192,64]{2,1,0:T(8,128)(2,1)S(1)}, bf16[4,192,64]{2,1,0:T(8,128)(2,1)}, u32[]{:S(2)}) copy-start(bf16[4,192,64]{2,1,0:T(8,128)(2,1)} %constant.64.clone.side_ref) | copy-start | bytes 294916
  0.6 21.2 %copy-start.7 = (bf16[4,128,64]{2,1,0:T(8,128)(2,1)S(1)}, bf16[4,128,64]{2,1,0:T(8,128)(2,1)}, u32[]{:S(2)}) copy-start(bf16[4,128,64]{2,1,0:T(8,128)(2,1)} %constant.65.clone.end_ref) | copy-start | bytes 196612
  0.7 21.2 %copy-start.8 = (s32[3,8]{1,0:T(4,128)S(1)}, s32[3,8]{1,0:T(4,128)}, u32[]{:S(2)}) copy-start(s32[3,8]{1,0:T(4,128)} %nb_ref.3) | copy-start | bytes 292
  0.7 21.2 %copy-start.9 = (s32[3,8]{1,0:T(4,128)S(1)}, s32[3,8]{1,0:T(4,128)}, u32[]{:S(2)}) copy-start(s32[3,8]{1,0:T(4,128)} %rot_ref.3) | copy-start | bytes 292
  0.7 21.2 %copy-start.10 = (s32[3,8]{1,0:T(4,128)S(1)}, s32[3,8]{1,0:T(4,128)}, u32[]{:S(2)}) copy-start(s32[3,8]{1,0:T(4,128)} %cor_ref.3) | copy-start | bytes 292
  2.6 19.2 %copy-start.2 = (bf16[12,64,128]{2,1,0:T(8,128)(2,1)S(1)}, bf16[12,64,128]{2,1,0:T(8,128)(2,1)}, u32[]{:S(2)}) copy-start(bf16[12,64,128]{2,1,0:T(8,128)(2,1)} %pack_edges.1.own_ref) | copy-start | bytes 589828
  2.6 17.5 %collective-permute-start = (bf16[12,64,128]{2,1,0:T(8,128)(2,1)}, bf16[12,64,128]{2,1,0:T(8,128)(2,1)S(1)}, u32[]{:S(2)}, u32[]{:S(2)}) collective-permute-start(bf16[12,64,128]{2,1,0:T(8,128)(2,1)} %pack_edges.1.own_ref), channel_id=1, source_target_pairs={{0,2},{1,3},{2,4},{3,5},{4,6},{5,7},{6,8},{7,9},{8,10},{9,11},{10,... | collective-permute-start | bytes 589832 | tf_op jit(solution)/shard_map/ppermute | solution.py:393
  5.6 14.5 %collective-permute-start.1 = (bf16[12,64,128]{2,1,0:T(8,128)(2,1)}, bf16[12,64,128]{2,1,0:T(8,128)(2,1)S(1)}, u32[]{:S(2)}, u32[]{:S(2)}) collective-permute-start(bf16[12,64,128]{2,1,0:T(8,128)(2,1)} %pack_edges.1.own_ref), channel_id=1, source_target_pairs={{0,30},{1,31},{2,0},{3,1},{4,2},{5,3},{6,4},{7,5},{8,6},{9,7},{10,... | collective-permute-start | bytes 589832 | tf_op jit(solution)/shard_map/ppermute | solution.py:393
  9.7 11.1 %collective-permute-start.2 = (bf16[12,64,128]{2,1,0:T(8,128)(2,1)}, bf16[12,64,128]{2,1,0:T(8,128)(2,1)S(1)}, u32[]{:S(2)}, u32[]{:S(2)}) collective-permute-start(bf16[12,64,128]{2,1,0:T(8,128)(2,1)} %pack_edges.1.own_ref), channel_id=1, source_target_pairs={{0,1},{1,0},{2,3},{3,2},{4,5},{5,4},{6,7},{7,6},{8,9},{9,8},{10,11... | collective-permute-start | bytes 589832 | tf_op jit(solution)/shard_map/ppermute | solution.py:397
  20.2 1.6 %collective-permute-start.3 = (bf16[12,64,128]{2,1,0:T(8,128)(2,1)S(1)}, bf16[12,64,128]{2,1,0:T(8,128)(2,1)S(1)}, u32[]{:S(2)}, u32[]{:S(2)}) collective-permute-start(bf16[12,64,128]{2,1,0:T(8,128)(2,1)S(1)} %broadcast_select_fusion), channel_id=1, source_target_pairs={{0,1},{1,0},{2,3},{3,2},{4,5},{5,4},{6,7},{7,6},{8,9},{9,8},{10,11... | collective-permute-start | bytes 589832 | tf_op jit(solution)/shard_map/ppermute | solution.py:397
  25.9 1.9 %collective-permute-start.4 = (f32[640,128]{1,0:T(8,128)}, f32[640,128]{1,0:T(8,128)S(1)}, u32[]{:S(2)}, u32[]{:S(2)}) collective-permute-start(f32[640,128]{1,0:T(8,128)} %get-tuple-element.33), channel_id=1, source_target_pairs={{0,1},{1,0},{2,3},{3,2},{4,5},{5,4},{6,7},{7,6},{8,9},{9,8},{10,11... | collective-permute-start | bytes 983048 | tf_op jit(solution)/shard_map/ppermute | solution.py:397
  26.3 5.1 %collective-permute-start.11 = (bf16[24,64,128]{2,1,0:T(8,128)(2,1)}, bf16[24,64,128]{2,1,0:T(8,128)(2,1)S(1)}, u32[]{:S(2)}, u32[]{:S(2)}) collective-permute-start(bf16[24,64,128]{2,1,0:T(8,128)(2,1)} %get-tuple-element.35), channel_id=1, source_target_pairs={{0,1},{1,0},{2,3},{3,2},{4,5},{5,4},{6,7},{7,6},{8,9},{9,8},{10,11... | collective-permute-start | bytes 1179656 | tf_op jit(solution)/shard_map/ppermute | solution.py:397
  27.9 5.8 %collective-permute-start.5 = (bf16[160,128]{1,0:T(8,128)(2,1)S(1)}, bf16[160,128]{1,0:T(8,128)(2,1)S(1)}, u32[]{:S(2)}, u32[]{:S(2)}) collective-permute-start(bf16[160,128]{1,0:T(8,128)(2,1)S(1)} %get-tuple-element.56), channel_id=1, source_target_pairs={{0,2},{1,3},{2,0},{3,1},{4,6},{5,7},{6,4},{7,5},{8,10},{9,11},{10,... | collective-permute-start | bytes 122888 | tf_op jit(solution)/shard_map/ppermute | solution.py:397
  27.9 5.7 %collective-permute-start.6 = (bf16[160,128]{1,0:T(8,128)(2,1)S(1)}, bf16[160,128]{1,0:T(8,128)(2,1)S(1)}, u32[]{:S(2)}, u32[]{:S(2)}) collective-permute-start(bf16[160,128]{1,0:T(8,128)(2,1)S(1)} %get-tuple-element.58), channel_id=1, source_target_pairs={{0,4},{1,5},{2,6},{3,7},{4,0},{5,1},{6,2},{7,3},{8,12},{9,13},{10,... | collective-permute-start | bytes 122888 | tf_op jit(solution)/shard_map/ppermute | solution.py:397
  28.0 8.9 %collective-permute-start.7 = (bf16[160,128]{1,0:T(8,128)(2,1)S(1)}, bf16[160,128]{1,0:T(8,128)(2,1)S(1)}, u32[]{:S(2)}, u32[]{:S(2)}) collective-permute-start(bf16[160,128]{1,0:T(8,128)(2,1)S(1)} %get-tuple-element.57), channel_id=1, source_target_pairs={{0,6},{1,7},{2,4},{3,5},{4,2},{5,3},{6,0},{7,1},{8,14},{9,15},{10,... | collective-permute-start | bytes 122888 | tf_op jit(solution)/shard_map/ppermute | solution.py:397
  31.6 12.4 %collective-permute-start.12 = (bf16[12,64,128]{2,1,0:T(8,128)(2,1)S(1)}, bf16[12,64,128]{2,1,0:T(8,128)(2,1)S(1)}, u32[]{:S(2)}, u32[]{:S(2)}) collective-permute-start(bf16[12,64,128]{2,1,0:T(8,128)(2,1)S(1)} %get-tuple-element.51), channel_id=1, source_target_pairs={{0,30},{1,31},{2,0},{3,1},{4,2},{5,3},{6,4},{7,5},{8,6},{9,7},{10,... | collective-permute-start | bytes 589832 | tf_op jit(solution)/shard_map/ppermute | solution.py:393
  33.6 11.0 %collective-permute-start.13 = (bf16[12,64,128]{2,1,0:T(8,128)(2,1)S(1)}, bf16[12,64,128]{2,1,0:T(8,128)(2,1)S(1)}, u32[]{:S(2)}, u32[]{:S(2)}) collective-permute-start(bf16[12,64,128]{2,1,0:T(8,128)(2,1)S(1)} %get-tuple-element.50), channel_id=1, source_target_pairs={{0,2},{1,3},{2,4},{3,5},{4,6},{5,7},{6,8},{7,9},{8,10},{9,11},{10,... | collective-permute-start | bytes 589832 | tf_op jit(solution)/shard_map/ppermute | solution.py:393
  37.0 7.6 %collective-permute-start.10 = (bf16[160,128]{1,0:T(8,128)(2,1)S(1)}, bf16[160,128]{1,0:T(8,128)(2,1)S(1)}, u32[]{:S(2)}, u32[]{:S(2)}) collective-permute-start(bf16[160,128]{1,0:T(8,128)(2,1)S(1)} %add_convert_fusion), channel_id=1, source_target_pairs={{0,24},{1,25},{2,26},{3,27},{4,28},{5,29},{6,30},{7,31},{8,16},{9,... | collective-permute-start | bytes 122888 | tf_op jit(solution)/shard_map/ppermute | solution.py:397
  37.0 7.6 %collective-permute-start.8 = (bf16[160,128]{1,0:T(8,128)(2,1)S(1)}, bf16[160,128]{1,0:T(8,128)(2,1)S(1)}, u32[]{:S(2)}, u32[]{:S(2)}) collective-permute-start(bf16[160,128]{1,0:T(8,128)(2,1)S(1)} %add_convert_fusion), channel_id=1, source_target_pairs={{0,8},{1,9},{2,10},{3,11},{4,12},{5,13},{6,14},{7,15},{8,0},{9,1},... | collective-permute-start | bytes 122888 | tf_op jit(solution)/shard_map/ppermute | solution.py:397
  37.1 7.5 %collective-permute-start.9 = (bf16[160,128]{1,0:T(8,128)(2,1)S(1)}, bf16[160,128]{1,0:T(8,128)(2,1)S(1)}, u32[]{:S(2)}, u32[]{:S(2)}) collective-permute-start(bf16[160,128]{1,0:T(8,128)(2,1)S(1)} %add_convert_fusion), channel_id=1, source_target_pairs={{0,16},{1,17},{2,18},{3,19},{4,20},{5,21},{6,22},{7,23},{8,24},{9,... | collective-permute-start | bytes 122888 | tf_op jit(solution)/shard_map/ppermute | solution.py:397
  44.6 5.2 %collective-permute-start.14 = (f32[160,128]{1,0:T(8,128)S(1)}, f32[160,128]{1,0:T(8,128)S(1)}, u32[]{:S(2)}, u32[]{:S(2)}) collective-permute-start(f32[160,128]{1,0:T(8,128)S(1)} %add_add_fusion), channel_id=1, source_target_pairs={{0,2},{1,3},{2,0},{3,1},{4,6},{5,7},{6,4},{7,5},{8,10},{9,11},{10,... | collective-permute-start | bytes 245768 | tf_op jit(solution)/shard_map/ppermute | solution.py:397
  44.7 6.3 %collective-permute-start.15 = (f32[160,128]{1,0:T(8,128)S(1)}, f32[160,128]{1,0:T(8,128)S(1)}, u32[]{:S(2)}, u32[]{:S(2)}) collective-permute-start(f32[160,128]{1,0:T(8,128)S(1)} %add_add_fusion), channel_id=1, source_target_pairs={{0,4},{1,5},{2,6},{3,7},{4,0},{5,1},{6,2},{7,3},{8,12},{9,13},{10,... | collective-permute-start | bytes 245768 | tf_op jit(solution)/shard_map/ppermute | solution.py:397
  48.3 5.3 %collective-permute-start.16 = (f32[160,128]{1,0:T(8,128)S(1)}, f32[160,128]{1,0:T(8,128)S(1)}, u32[]{:S(2)}, u32[]{:S(2)}) collective-permute-start(f32[160,128]{1,0:T(8,128)S(1)} %add_add_fusion), channel_id=1, source_target_pairs={{0,6},{1,7},{2,4},{3,5},{4,2},{5,3},{6,0},{7,1},{8,14},{9,15},{10,... | collective-permute-start | bytes 245768 | tf_op jit(solution)/shard_map/ppermute | solution.py:397
  53.7 1.7 %collective-permute-start.17 = (f32[640,128]{1,0:T(8,128)S(1)}, f32[640,128]{1,0:T(8,128)S(1)}, u32[]{:S(2)}, u32[]{:S(2)}) collective-permute-start(f32[640,128]{1,0:T(8,128)S(1)} %pad_maximum_fusion.1.mine_ref), channel_id=1, source_target_pairs={{0,1},{1,0},{2,3},{3,2},{4,5},{5,4},{6,7},{7,6},{8,9},{9,8},{10,11... | collective-permute-start | bytes 983048 | tf_op jit(solution)/shard_map/ppermute | solution.py:397
  (6 other events, 54.4 us)

commit v3 on v2

--- a/solution.py
+++ b/solution.py
@@ -10,6 +10,7 @@
 from jax.sharding import PartitionSpec as P
 
 ROOM = 12
+STEP = 4
 BF = jnp.bfloat16
 F32 = jnp.float32
 
@@ -87,20 +88,46 @@
 
 def spread(ext_ref, wide, length):
     count = length * length
+    size = 2 * length
     column = lax.broadcasted_iota(jnp.int32, (count, 1), 0) & (length - 1)
-    pad = 2 * length
     back = jnp.where(column >= 2, pltpu.roll(wide, 2, 0), 0.0)
     ahead = jnp.where(column < length - 2, pltpu.roll(wide, count - 2, 0), 0.0)
-    ext_ref[pad : pad + count, 0:128] = back.astype(BF)
-    ext_ref[pad : pad + count, 128:256] = wide.astype(BF)
-    ext_ref[pad : pad + count, 256:384] = ahead.astype(BF)
+    for i, part in enumerate((back, wide, ahead)):
+        part = part.astype(BF)
+        lanes = slice(i * 128, (i + 1) * 128)
+        groups = count // (2 * size)
+        for g in range(groups):
+            at = 2 * size * g
+            ext_ref[g, size:, lanes] = part[at : at + size]
+            ext_ref[g + 1, 0:size, lanes] = part[at + size : at + 2 * size]
 
 
 def clear_rows(ext_ref, length):
-    pad = 2 * length
-    empty = jnp.zeros((pad, 384), BF)
-    ext_ref[0:pad, :] = empty
-    ext_ref[pad + length * length :, :] = empty
+    size = 2 * length
+    empty = jnp.zeros((size, 384), BF)
+    ext_ref[0, 0:size, :] = empty
+    ext_ref[ext_ref.shape[0] - 1, size:, :] = empty
+
+
+def pair_taps(rows_of):
+    none = jnp.zeros_like(rows_of[0])
+    left = rows_of + [none]
+    right = [none] + rows_of
+    both = [jnp.concatenate([a, b], axis=1) for a, b in zip(left, right)]
+    return [jnp.concatenate(both[0:2], axis=0), jnp.concatenate(both[2:4], axis=0)]
+
+
+def conv_pairs(ext_ref, weights, first, groups, length):
+    size = 2 * length
+    total = None
+    for half in range(2):
+        rows = ext_ref[first + half : first + half + groups]
+        pixels = jnp.concatenate(
+            [rows[:, 0:size].reshape(groups * size, 384), rows[:, size:].reshape(groups * size, 384)], axis=1
+        )
+        part = dot(pixels, weights[half])
+        total = part if total is None else total + part
+    return total[:, 0:128].reshape(groups, size, 128), total[:, 128:].reshape(groups, size, 128)
 
 
 def begin(source, target, sem):
@@ -114,11 +141,10 @@
         copy.wait()
 
 
-def pack_kernel(x_ref, out_ref, x_vm, out_vm, wide_ref, sems, *, length):
+def pack_kernel(x_ref, out_vm, x_vm, wide_ref, sems, *, length):
     count = length * length
     patches = x_vm.shape[0]
     arriving = [begin(x_ref.at[p], x_vm.at[p], sems.at[p]) for p in range(patches)]
-    leaving = []
     for p in range(patches):
         arriving[p].wait()
         out_vm[4 * p] = x_vm[p, 0 : 2 * length, :]
@@ -126,14 +152,11 @@
         wide_ref[...] = x_vm[p].astype(F32)
         out_vm[4 * p + 2] = column_strip(wide_ref, 0, length).astype(BF)
         out_vm[4 * p + 3] = column_strip(wide_ref, length - 2, length).astype(BF)
-        rows = pl.ds(4 * p, 4)
-        leaving.append(begin(out_vm.at[rows], out_ref.at[rows], sems.at[patches + p]))
-    finish(leaving)
 
 
 def own_kernel(
     me_ref, nb_ref, rot_ref, cor_ref, x_ref, cot_ref, w_ref, bias_in_ref, flip_ref,
-    strips_ref, own_ref, far_ref, near_ref, dw_ref, dx_ref, mid_ref,
+    own_ref, far_ref, near_ref, dw_ref, dx_ref, mid_ref,
     nb_sm, rot_sm, cor_sm, x_vm, cot_vm, w_vm, bias_in_vm, flip_vm,
     strips_vm, near_vm, dw_vm, dx_vm, mid_vm, ext_ref, wide_ref, pool_ref, sems, *, length, devices,
 ):
@@ -141,7 +164,6 @@
     count = length * length
     size = 2 * length
     block = 4 * patches
-    chunk = min(count, 256)
     sources = [nb_ref, rot_ref, cor_ref, w_ref, bias_in_ref, flip_ref]
     targets = [nb_sm, rot_sm, cor_sm, w_vm, bias_in_vm, flip_vm]
     arriving = [begin(a, b, sems.at[i]) for i, (a, b) in enumerate(zip(sources, targets))]
@@ -159,19 +181,19 @@
     taps = [jnp.concatenate([w_vm[a * 3 + b] for a, b in SIDE_TAPS[s]], axis=0) for s in range(4)]
     for p in range(patches):
         cots[p].wait()
+        mine = slice(size * p, size * (p + 1))
+        strips_vm[0, mine, :] = cot_vm[p, 0:size, :]
+        strips_vm[1, mine, :] = cot_vm[p, count - size :, :]
         wide_ref[...] = cot_vm[p].astype(F32)
-        strips = [
-            cot_vm[p, 0:size, :],
-            cot_vm[p, count - size :, :],
-            column_strip(wide_ref, 0, length).astype(BF),
-            column_strip(wide_ref, length - 2, length).astype(BF),
-        ]
-        for s in range(4):
-            strips_vm[s, size * p : size * (p + 1), :] = strips[s]
-            terms = lax.dot_general(strips[s], taps[s], (((1,), (1,)), ((), ())), preferred_element_type=F32)
+        strips_vm[2, mine, :] = column_strip(wide_ref, 0, length).astype(BF)
+        strips_vm[3, mine, :] = column_strip(wide_ref, length - 2, length).astype(BF)
+    sent = []
+    for s in range(4):
+        terms = lax.dot_general(strips_vm[s], taps[s], (((1,), (1,)), ((), ())), preferred_element_type=F32)
+        for p in range(patches):
             side, first, last = [], [], []
             for r in range(2):
-                rows = slice(r * length, (r + 1) * length)
+                rows = slice(size * p + r * length, size * p + (r + 1) * length)
                 ahead = pltpu.roll(terms[rows, 0:128], length - 2, 0)
                 back = pltpu.roll(terms[rows, 256:384], 2, 0)
                 side.append(
@@ -181,74 +203,75 @@
                 )
                 first.append(jnp.where(along >= length - 2, ahead, 0.0))
                 last.append(jnp.where(along < 2, back, 0.0))
-            sent = [(SIDE_DIRECTION[s], side)]
+            sent.append((p, SIDE_DIRECTION[s], side))
             if s < 2:
-                sent += [(SIDE_ENDS[s][0], first), (SIDE_ENDS[s][1], last)]
-            for j, term in sent:
-                where_to, code = place_of(
-                    me, nb_sm[p, j], rot_sm[p, j], wanted_side(*DIRECTIONS[j]), patches, devices
-                )
-                value = dot(flip_vm[code], jnp.concatenate(term, axis=0).astype(BF))
-                value = value * (cor_sm[p, j] > 0).astype(F32)
-                pool_ref[where_to] = pool_ref[where_to] + value
+                sent += [(p, SIDE_ENDS[s][0], first), (p, SIDE_ENDS[s][1], last)]
+    placed = []
+    for p, j, term in sent:
+        where_to, code = place_of(me, nb_sm[p, j], rot_sm[p, j], wanted_side(*DIRECTIONS[j]), patches, devices)
+        value = dot(flip_vm[code], jnp.concatenate(term, axis=0).astype(BF))
+        placed.append((where_to, value * (cor_sm[p, j] > 0).astype(F32)))
+    for where_to, value in placed:
+        pool_ref[where_to] = pool_ref[where_to] + value
     near_vm[...] = pool_ref[3 * block :].astype(BF)
     for source, target in (
-        (strips_vm, strips_ref), (near_vm, near_ref),
+        (near_vm, near_ref),
         (pool_ref.at[pl.ds(0, block)], own_ref), (pool_ref.at[pl.ds(block, 2 * block)], far_ref),
     ):
         leaving.append(begin(source, target, sems.at[used]))
         used += 1
 
     total_bias = jnp.zeros((1, 128), F32)
-    flipped = [
-        jnp.concatenate([w_vm[(2 - a) * 3 + 2], w_vm[(2 - a) * 3 + 1], w_vm[(2 - a) * 3]], axis=1) for a in range(3)
-    ]
-    rows_of = [jnp.concatenate([w_vm[a * 3 + b] for b in range(3)], axis=0) for a in range(3)]
+    flipped = pair_taps(
+        [jnp.concatenate([w_vm[(2 - a) * 3 + 2 - b].T for b in range(3)], axis=0) for a in range(3)]
+    )
+    plain = pair_taps([jnp.concatenate([w_vm[a * 3 + b] for b in range(3)], axis=0) for a in range(3)])
+    groups = count // (2 * size)
+    step = min(groups, STEP)
     for p in range(patches):
         wide = cot_vm[p].astype(F32)
         total_bias = total_bias + jnp.sum(wide, axis=0, keepdims=True)
         spread(ext_ref, wide, length)
         xs[p].wait()
         turned = x_vm[p].T
+        windows = [
+            ext_ref[0:groups].reshape(count, 384),
+            jnp.concatenate([ext_ref[0:groups, size:], ext_ref[1 : groups + 1, 0:size]], axis=1).reshape(count, 384),
+            ext_ref[1 : groups + 1].reshape(count, 384),
+        ]
         for a in range(3):
-            grads = dot(turned, ext_ref[size * a : size * a + count, :])
+            grads = dot(turned, windows[a])
             for b in range(3):
                 tap = (2 - a) * 3 + 2 - b
                 rows = slice(tap * 128, (tap + 1) * 128)
                 part = grads[:, b * 128 : (b + 1) * 128]
                 dw_vm[rows, :] = part if p == 0 else dw_vm[rows, :] + part
-        for start in range(0, count, chunk):
-            total = None
-            for a in range(3):
-                at = start + size * a
-                part = lax.dot_general(
-                    ext_ref[at : at + chunk, :], flipped[a], (((1,), (1,)), ((), ())), preferred_element_type=F32
-                )
-                total = part if total is None else total + part
-            dx_vm[p, start : start + chunk, :] = total.astype(BF)
+        for g in range(0, groups, step):
+            for i, part in enumerate(conv_pairs(ext_ref, flipped, g, step, length)):
+                dx_vm[p, g : g + step, i * size : (i + 1) * size] = part.astype(BF)
         leaving.append(begin(dx_vm.at[p], dx_ref.at[p], sems.at[used]))
         used += 1
-    dw_vm[9 * 128 :, :] = jnp.zeros((dw_vm.shape[0] - 9 * 128, 128), F32)
+    dw_vm[9 * 128 : 10 * 128, :] = jnp.zeros((128, 128), F32)
     dw_vm[9 * 128 : 9 * 128 + 8, :] = jnp.broadcast_to(total_bias, (8, 128))
+    for s in range(4):
+        at = 10 * 128 + s * patches * size
+        dw_vm[at : at + patches * size, :] = strips_vm[s].astype(F32)
     leaving.append(begin(dw_vm, dw_ref, sems.at[used]))
     used += 1
     for p in range(patches):
         spread(ext_ref, x_vm[p].astype(F32), length)
-        for start in range(0, count, chunk):
-            total = jnp.broadcast_to(bias_in_vm[...], (chunk, 128))
-            for a in range(3):
-                at = start + size * a
-                total = total + dot(ext_ref[at : at + chunk, :], rows_of[a])
-            mid_vm[p, start : start + chunk, :] = total
+        for g in range(0, groups, step):
+            for i, part in enumerate(conv_pairs(ext_ref, plain, g, step, length)):
+                mid_vm[p, g : g + step, i * size : (i + 1) * size] = part + bias_in_vm[...]
         leaving.append(begin(mid_vm.at[p], mid_ref.at[p], sems.at[used]))
         used += 1
     finish(leaving)
 
 
 def halo_kernel(
-    me_ref, nb_ref, rot_ref, cor_ref, own_ref, low_ref, high_ref, mate_ref, across_ref, strips_ref, dw_ref,
+    me_ref, nb_ref, rot_ref, cor_ref, own_ref, low_ref, high_ref, mate_ref, across_ref, dw_ref,
     side_ref, end_ref, keep_ref, send_ref, halo_ref,
-    nb_sm, rot_sm, cor_sm, pool_ref, strips_vm, total_ref, side_vm, end_vm, halo_vm, sems, *, length, devices, factor,
+    nb_sm, rot_sm, cor_sm, pool_ref, total_ref, side_vm, end_vm, halo_vm, sems, *, length, devices, factor,
 ):
     block = pool_ref.shape[0] // 5
     patches = block // 4
@@ -256,8 +279,8 @@
     targets = [nb_sm, rot_sm, cor_sm, side_vm, end_vm]
     arriving = [begin(a, b, sems.at[i]) for i, (a, b) in enumerate(zip(sources, targets))]
     used = len(arriving)
-    later = [begin(strips_ref, strips_vm, sems.at[used]), begin(dw_ref, total_ref, sems.at[used + 1])]
-    used += 2
+    later = [begin(dw_ref, total_ref, sems.at[used])]
+    used += 1
     for i, source in enumerate((own_ref, low_ref, high_ref, mate_ref, across_ref)):
         pool_ref[i * block : (i + 1) * block] = source[...]
     me = me_ref[0]
@@ -283,13 +306,15 @@
     leaving = [begin(halo_vm, halo_ref, sems.at[used])]
     finish(later)
     for s in range(4):
+        at = 10 * 128 + s * patches * size
+        strips = total_ref[at : at + patches * size, :].astype(BF)
         grads = lax.dot_general(
-            halo_vm[s], strips_vm[s], (((0,), (0,)), ((), ())), preferred_element_type=F32
+            halo_vm[s], strips, (((0,), (0,)), ((), ())), preferred_element_type=F32
         )
         for i, (a, b) in enumerate(SIDE_TAPS[s]):
             rows = slice((a * 3 + b) * 128, (a * 3 + b + 1) * 128)
             total_ref[rows, :] = total_ref[rows, :] + grads[i * 128 : (i + 1) * 128]
-    half = total_ref.shape[0] // 2
+    half = 5 * 128
     core = lax.rem(me, 2)
     send_ref[...] = total_ref[pl.ds(pl.multiple_of((1 - core) * half, 128), half), :] * factor
     keep_ref[...] = total_ref[pl.ds(pl.multiple_of(core * half, 128), half), :] * factor
@@ -425,6 +450,46 @@
     return whole, swapped(whole, 1)
 
 
+def own_pixels(tables, x, cot, w, bias, flips, devices):
+    patches, count, chans = x.shape
+    length = math.isqrt(count)
+    size = 2 * length
+    block = 4 * patches
+    rows = 10 * chans
+    grouped = (patches, count // (2 * size), 2 * size, chans)
+    shape = jax.ShapeDtypeStruct
+    scratch = pltpu.VMEM
+    table_scratch = [pltpu.SMEM(tables[1].shape, jnp.int32)] * 3
+    return call(
+        functools.partial(own_kernel, length=length, devices=devices), "own_pixels", "shhhhhhhh",
+        [
+            shape((block, size, chans), F32),
+            shape((2 * block, size, chans), F32),
+            shape((2 * block, size, chans), BF),
+            shape((rows + block * size, chans), F32),
+            shape(grouped, BF),
+            shape(grouped, F32),
+        ],
+        table_scratch
+        + [
+            scratch(x.shape, BF),
+            scratch(x.shape, BF),
+            scratch(w.shape, BF),
+            scratch((1, chans), F32),
+            scratch(flips.shape, BF),
+            scratch((4, patches * size, chans), BF),
+            scratch((2 * block, size, chans), BF),
+            scratch((rows + block * size, chans), F32),
+            scratch(grouped, BF),
+            scratch(grouped, F32),
+            scratch((count // (2 * size) + 1, 2 * size, 3 * chans), BF),
+            scratch((count, chans), F32),
+            scratch((5 * block, size, chans), F32),
+        ],
+        6 + 4 * patches + 4,
+    )(*tables, x, cot, w, bias, flips)
+
+
 def body(inputs, cotangent, weights, bias_vector, neighbours, rotations, corners):
     patches, length, _, chans = inputs.shape
     devices = lax.axis_size("patch")
@@ -446,41 +511,14 @@
 
     (edges,) = call(
         functools.partial(pack_kernel, length=length), "pack_edges", "h", [shape((block, size, chans), BF)],
-        [scratch(x.shape, BF), scratch((block, size, chans), BF), scratch((count, chans), F32)], 2 * patches,
+        [scratch(x.shape, BF), scratch((count, chans), F32)], patches, small=(0,), room=ROOM,
     )(x)
     from_low = shifted(edges, 2)
     from_high = shifted(edges, -2)
     from_mate = swapped(edges, 1)
 
-    strips, own, far, near, dw, dx, mid = call(
-        functools.partial(own_kernel, length=length, devices=devices), "own_pixels", "shhhhhhhh",
-        [
-            shape((4, patches * size, chans), BF),
-            shape((block, size, chans), F32),
-            shape((2 * block, size, chans), F32),
-            shape((2 * block, size, chans), BF),
-            shape((rows, chans), F32),
-            shape(x.shape, BF),
-            shape(x.shape, F32),
-        ],
-        table_scratch
-        + [
-            scratch(x.shape, BF),
-            scratch(x.shape, BF),
-            scratch(w.shape, BF),
-            scratch((1, chans), F32),
-            scratch(flips.shape, BF),
-            scratch((4, patches * size, chans), BF),
-            scratch((2 * block, size, chans), BF),
-            scratch((rows, chans), F32),
-            scratch(x.shape, BF),
-            scratch(x.shape, F32),
-            scratch((count + 2 * size, 3 * chans), BF),
-            scratch((count, chans), F32),
-            scratch((5 * block, size, chans), F32),
-        ],
-        6 + 4 * patches + 5,
-    )(*tables, x, cot, w, bias_vector.reshape(1, chans), flips)
+    own, far, near, dw, dx, mid = own_pixels(tables, x, cot, w, bias_vector.reshape(1, chans), flips, devices)
+    dx, mid = dx.reshape(x.shape), mid.reshape(x.shape)
     near_in = swapped(near, 1)
 
     from_low, from_high, dw = lax.optimization_barrier((from_low, from_high, dw))
@@ -493,7 +531,7 @@
     factor = 1.0 / (length * math.sqrt(patches * devices))
     keep, send, halo = call(
         functools.partial(halo_kernel, length=length, devices=devices, factor=factor), "halo_kernel_grad",
-        "shhhvvvvvaahh",
+        "shhhvvvvvahh",
         [
             shape((rows // 2, chans), F32),
             shape((rows // 2, chans), F32),
@@ -502,14 +540,13 @@
         table_scratch
         + [
             scratch((5 * block, size, chans), BF),
-            scratch(strips.shape, BF),
-            scratch((rows, chans), F32),
+            scratch(dw.shape, F32),
             scratch(sides.shape, BF),
             scratch(ends.shape, BF),
             scratch((4, patches * size, 3 * chans), BF),
         ],
-        8, small=(0, 1), room=ROOM,
-    )(*tables, edges, from_low, from_high, from_mate, from_across, strips, dw, sides, ends)
+        7, small=(0, 1), room=ROOM,
+    )(*tables, edges, from_low, from_high, from_mate, from_across, dw, sides, ends)
 
     (outputs,) = call(
         functools.partial(forward_kernel, length=length), "add_halo_outputs", "aha", [shape(x.shape, BF)],

time: 57 us -> 50.5 us (0.89)
  Pallas kernels: 20.8 us -> 15.5 us
  waiting for transfers between devices: 11.8 us -> 10 us
    pallas_call x1, Pallas kernels: 10.5 us -> 7.68 us  [own_pixels(): call(functools.partial(own_kernel, length=length, devices=devices), 'own_...]
    ppermute x14, waiting for transfers between devices: 11.1 us -> 9.25 us  [swapped(): lax.ppermute(value, 'patch', [(d, d ^ mask) for d in range(lax.axis_size(...]
    pallas_call x1, Pallas kernels: 1.93 us -> 0.28 us  [body(): call(functools.partial(pack_kernel, length=length), 'pack_edges', 'h', [s...]
    pallas_call x1, Pallas kernels: 3.04 us -> 2.23 us  [body(): call(functools.partial(halo_kernel, length=length, devices=devices, facto...]
    unnamed x24 -> x22, local copies, waits for them, and re-layouts: 0.98 us -> 1.18 us
  transfers between devices with their start and end apart: 18 -> 18, of which waited for: 7 -> 7; matrix products, arithmetic and copies ran while one was open for 0% -> 0% of each run, Pallas kernels for 25% -> 23%
where the time goes in v3:
time: 50.5 us; the launch traced here: 50.3 us
  starting transfers between devices  22.4 us (44%)
  Pallas kernels  15.5 us (31%)
  waiting for transfers between devices  10 us (20%)
  local copies, waits for them, and re-layouts  1.24 us (2%)
  between operations  0.87 us (2%)
    ppermute x14, starting transfers between devices, swapped(): lax.ppermute(value, 'patch', [(d, d ^ mask) for d in range(lax.axis_size(...  12.8 us
    ppermute x4, starting transfers between devices, shifted(): lax.ppermute(value, 'patch', [(d, (d + steps) % count) for d in range(cou...  9.59 us
    ppermute x14, waiting for transfers between devices, swapped(): lax.ppermute(value, 'patch', [(d, d ^ mask) for d in range(lax.axis_size(...  9.25 us
    pallas_call x1, Pallas kernels, own_pixels(): call(functools.partial(own_kernel, length=length, devices=devices), 'own_...  7.68 us
    pallas_call x1, Pallas kernels, body(): call(functools.partial(forward_kernel, length=length), 'add_halo_outputs'...  2.52 us
    pallas_call x1, Pallas kernels, body(): call(functools.partial(halo_kernel, length=length, devices=devices, facto...  2.23 us
    pallas_call x1, Pallas kernels, last(): call(functools.partial(join_kernel, length=length), 'join_input_grad', 'a...  1.49 us
    pallas_call x1, Pallas kernels, body(): call(functools.partial(result_kernel, taps=9 * chans), 'order_kernel_grad...  1.34 us
  transfers between devices with their start and end apart: 18, of which 7 were waited for; matrix products, arithmetic and copies ran while one was open for 0% of the time, Pallas kernels for 23%

profile of v3, /device:TPU:0, one launch (start us, length us, event | category | flops | bytes accessed | tf_op | source)
XLA Modules:
  0.0 50.3 jit_solution(6676890392523158962)
XLA Ops:
  0.6 1.1 %copy-done = bf16[3,32,32,128]{3,2,1,0:T(8,128)(2,1)S(1)} copy-done((bf16[3,32,32,128]{3,2,1,0:T(8,128)(2,1)S(1)}, bf16[3,32,32,128]{3,2,1,0:T(8,128)(2,1)}, u32[]{:S(2)}) %copy-start) | copy-done | bytes 786456
  1.8 0.3 pack_edges.1.own_ref
  2.1 3.0 %collective-permute-start = (bf16[12,64,128]{2,1,0:T(8,128)(2,1)S(1)}, bf16[12,64,128]{2,1,0:T(8,128)(2,1)S(1)}, u32[]{:S(2)}, u32[]{:S(2)}) collective-permute-start(bf16[12,64,128]{2,1,0:T(8,128)(2,1)S(1)} %pack_edges.1.own_ref), channel_id=1, source_target_pairs={{0,2},{1,3},{2,4},{3,5},{4,6},{5,7},{6,8},{7,9},{8,10},{9,11},{10,... | collective-permute-start | bytes 589832 | tf_op jit(solution)/shard_map/ppermute | solution.py:418
  5.1 4.1 %collective-permute-start.1 = (bf16[12,64,128]{2,1,0:T(8,128)(2,1)S(1)}, bf16[12,64,128]{2,1,0:T(8,128)(2,1)S(1)}, u32[]{:S(2)}, u32[]{:S(2)}) collective-permute-start(bf16[12,64,128]{2,1,0:T(8,128)(2,1)S(1)} %pack_edges.1.own_ref), channel_id=1, source_target_pairs={{0,30},{1,31},{2,0},{3,1},{4,2},{5,3},{6,4},{7,5},{8,6},{9,7},{10,... | collective-permute-start | bytes 589832 | tf_op jit(solution)/shard_map/ppermute | solution.py:418
  9.1 7.7 %own_pixels.1 = (f32[12,64,128]{2,1,0:T(8,128)}, f32[24,64,128]{2,1,0:T(8,128)}, bf16[24,64,128]{2,1,0:T(8,128)(2,1)}, f32[2048,128]{1,0:T(8,128)}, bf16[3,8,128...) custom-call(s32[1]{0:T(128)} %bitcast.me_ref, s32[3,8]{1,0:T(4,128)} %nb_ref.3, s32[3,8]{1,0:T(4,128)} %rot_ref.3, ...), custom_call_target="tpu_custom_call" | custom-call | tf_op jit(solution)/shard_map/own_pixels/pallas_call | solution.py:463
  16.9 0.6 %collective-permute-start.3 = (bf16[12,64,128]{2,1,0:T(8,128)(2,1)S(1)}, bf16[12,64,128]{2,1,0:T(8,128)(2,1)S(1)}, u32[]{:S(2)}, u32[]{:S(2)}) collective-permute-start(bf16[12,64,128]{2,1,0:T(8,128)(2,1)S(1)} %broadcast_select_fusion), channel_id=1, source_target_pairs={{0,1},{1,0},{2,3},{3,2},{4,5},{5,4},{6,7},{7,6},{8,9},{9,8},{10,11... | collective-permute-start | bytes 589832 | tf_op jit(solution)/shard_map/ppermute | solution.py:422
  17.5 1.1 %collective-permute-done.3.across_ref = bf16[12,64,128]{2,1,0:T(8,128)(2,1)S(1)} collective-permute-done((bf16[12,64,128]{2,1,0:T(8,128)(2,1)S(1)}, bf16[12,64,128]{2,1,0:T(8,128)(2,1)S(1)}, u32[]{:S(2)}, u32[]{:S(2)}) %collective-permute-start.3) | collective-permute-done | bytes 196640 | tf_op jit(solution)/shard_map/ppermute | solution.py:422
  18.5 2.2 %halo_kernel_grad.1 = (f32[640,128]{1,0:T(8,128)S(1)}, f32[640,128]{1,0:T(8,128)S(1)}, bf16[4,192,384]{2,1,0:T(8,128)(2,1)}) custom-call(s32[1]{0:T(128)} %bitcast.me_ref, s32[3,8]{1,0:T(4,128)S(1)} %copy-done.7, s32[3,8]{1,0:T(4,128)S(1)} %copy-done.8, s32[3,8]{1,0:T(4,128)S(1)} %copy-done.9, bf16[12,64,128]{2,1,0:T(8,128)(2,1)S(1)} %pack_edges.1.own_ref, ...), custom_call_target="tpu_custom_call" | custom-call | tf_op jit(solution)/shard_map/halo_kernel_grad/pallas_call | solution.py:532
  20.8 0.4 collective-permute-start.4
  21.4 1.1 %collective-permute-done.4 = f32[640,128]{1,0:T(8,128)S(1)} collective-permute-done((f32[640,128]{1,0:T(8,128)S(1)}, f32[640,128]{1,0:T(8,128)S(1)}, u32[]{:S(2)}, u32[]{:S(2)}) %collective-permute-start.4) | collective-permute-done | bytes 327712 | tf_op jit(solution)/shard_map/ppermute | solution.py:422
  22.7 0.3 collective-permute-start.6
  22.9 3.2 %collective-permute-start.7 = (bf16[160,128]{1,0:T(8,128)(2,1)S(1)}, bf16[160,128]{1,0:T(8,128)(2,1)S(1)}, u32[]{:S(2)}, u32[]{:S(2)}) collective-permute-start(bf16[160,128]{1,0:T(8,128)(2,1)S(1)} %get-tuple-element.55), channel_id=1, source_target_pairs={{0,6},{1,7},{2,4},{3,5},{4,2},{5,3},{6,0},{7,1},{8,14},{9,15},{10,... | collective-permute-start | bytes 122888 | tf_op jit(solution)/shard_map/ppermute | solution.py:422
  26.3 2.5 %collective-permute-start.12 = (bf16[12,64,128]{2,1,0:T(8,128)(2,1)S(1)}, bf16[12,64,128]{2,1,0:T(8,128)(2,1)S(1)}, u32[]{:S(2)}, u32[]{:S(2)}) collective-permute-start(bf16[12,64,128]{2,1,0:T(8,128)(2,1)S(1)} %get-tuple-element.49), channel_id=1, source_target_pairs={{0,30},{1,31},{2,0},{3,1},{4,2},{5,3},{6,4},{7,5},{8,6},{9,7},{10,... | collective-permute-start | bytes 589832 | tf_op jit(solution)/shard_map/ppermute | solution.py:418
  28.8 3.2 %collective-permute-done.7 = bf16[160,128]{1,0:T(8,128)(2,1)S(1)} collective-permute-done((bf16[160,128]{1,0:T(8,128)(2,1)S(1)}, bf16[160,128]{1,0:T(8,128)(2,1)S(1)}, u32[]{:S(2)}, u32[]{:S(2)}) %collective-permute-start.7) | collective-permute-done | bytes 40992 | tf_op jit(solution)/shard_map/ppermute | solution.py:422
  32.2 4.3 %collective-permute-start.9 = (bf16[160,128]{1,0:T(8,128)(2,1)S(1)}, bf16[160,128]{1,0:T(8,128)(2,1)S(1)}, u32[]{:S(2)}, u32[]{:S(2)}) collective-permute-start(bf16[160,128]{1,0:T(8,128)(2,1)S(1)} %add_convert_fusion), channel_id=1, source_target_pairs={{0,16},{1,17},{2,18},{3,19},{4,20},{5,21},{6,22},{7,23},{8,24},{9,... | collective-permute-start | bytes 122888 | tf_op jit(solution)/shard_map/ppermute | solution.py:422
  36.5 2.5 %add_halo_outputs.1 = bf16[3,1024,128]{2,1,0:T(8,128)(2,1)} custom-call(f32[3,1024,128]{2,1,0:T(8,128)} %bitcast.28, bf16[9,128,128]{2,1,0:T(8,128)(2,1)S(1)} %bitcast.26, bf16[4,192,384]{2,1,0:T(8,128)(2,1)S(1)} %copy-done.3), custom_call_target="tpu_custom_call" | custom-call | tf_op jit(solution)/shard_map/add_halo_outputs/pallas_call | solution.py:551
  39.0 0.7 %collective-permute-done.13.low_ref = bf16[12,64,128]{2,1,0:T(8,128)(2,1)S(1)} collective-permute-done((bf16[12,64,128]{2,1,0:T(8,128)(2,1)S(1)}, bf16[12,64,128]{2,1,0:T(8,128)(2,1)S(1)}, u32[]{:S(2)}, u32[]{:S(2)}) %collective-permute-start.13) | collective-permute-done | bytes 196640 | tf_op jit(solution)/shard_map/ppermute | solution.py:418
  39.8 2.9 %collective-permute-start.16 = (f32[160,128]{1,0:T(8,128)S(1)}, f32[160,128]{1,0:T(8,128)S(1)}, u32[]{:S(2)}, u32[]{:S(2)}) collective-permute-start(f32[160,128]{1,0:T(8,128)S(1)} %add_add_fusion), channel_id=1, source_target_pairs={{0,6},{1,7},{2,4},{3,5},{4,2},{5,3},{6,0},{7,1},{8,14},{9,15},{10,... | collective-permute-start | bytes 245768 | tf_op jit(solution)/shard_map/ppermute | solution.py:422
  42.7 0.7 %collective-permute-start.15 = (f32[160,128]{1,0:T(8,128)S(1)}, f32[160,128]{1,0:T(8,128)S(1)}, u32[]{:S(2)}, u32[]{:S(2)}) collective-permute-start(f32[160,128]{1,0:T(8,128)S(1)} %add_add_fusion), channel_id=1, source_target_pairs={{0,4},{1,5},{2,6},{3,7},{4,0},{5,1},{6,2},{7,3},{8,12},{9,13},{10,... | collective-permute-start | bytes 245768 | tf_op jit(solution)/shard_map/ppermute | solution.py:422
  43.4 1.5 %join_input_grad.1 = bf16[3,1024,128]{2,1,0:T(8,128)(2,1)} custom-call(bf16[3,1024,128]{2,1,0:T(8,128)(2,1)S(1)} %bitcast.27, f32[12,64,128]{2,1,0:T(8,128)S(1)} %copy-done.4, bf16[24,64,128]{2,1,0:T(8,128)(2,1)S(1)} %collective-permute-done.11.near_ref, bf16[12,64,128]{2,1,0:T(8,128)(2,1)S(1)} %collective-permute-done.13.low_ref, ...), custom_call_target="tpu_custom_call" | custom-call | tf_op jit(solution)/shard_map/join_input_grad/pallas_call | solution.py:567
  44.9 0.3 collective-permute-done.16
  45.2 1.9 %collective-permute-done.14 = f32[160,128]{1,0:T(8,128)S(1)} collective-permute-done((f32[160,128]{1,0:T(8,128)S(1)}, f32[160,128]{1,0:T(8,128)S(1)}, u32[]{:S(2)}, u32[]{:S(2)}) %collective-permute-start.14) | collective-permute-done | bytes 81952 | tf_op jit(solution)/shard_map/ppermute | solution.py:422
  47.3 1.6 %collective-permute-done.17.other_ref = f32[640,128]{1,0:T(8,128)S(1)} collective-permute-done((f32[640,128]{1,0:T(8,128)S(1)}, f32[640,128]{1,0:T(8,128)S(1)}, u32[]{:S(2)}, u32[]{:S(2)}) %collective-permute-start.17) | collective-permute-done | bytes 327712 | tf_op jit(solution)/shard_map/ppermute | solution.py:422
  48.9 1.3 %order_kernel_grad.1 = (f32[1152,128]{1,0:T(8,128)}, f32[1,128]{1,0:T(1,128)}) custom-call(s32[1]{0:T(128)} %bitcast.me_ref, f32[640,128]{1,0:T(8,128)S(1)} %pad_maximum_fusion.1.mine_ref, f32[640,128]{1,0:T(8,128)S(1)} %collective-permute-done.17.other_ref), custom_call_target="tpu_custom_call" | custom-call | tf_op jit(solution)/shard_map/order_kernel_grad/pallas_call | solution.py:581
  (49 shorter events, 0.8 us)
Async XLA Ops:
  1.8 16.8 %copy-start.5 = (bf16[4,192,64]{2,1,0:T(8,128)(2,1)S(1)}, bf16[4,192,64]{2,1,0:T(8,128)(2,1)}, u32[]{:S(2)}) copy-start(bf16[4,192,64]{2,1,0:T(8,128)(2,1)} %constant.64.clone.side_ref) | copy-start | bytes 294916
  1.8 16.8 %copy-start.6 = (bf16[4,128,64]{2,1,0:T(8,128)(2,1)S(1)}, bf16[4,128,64]{2,1,0:T(8,128)(2,1)}, u32[]{:S(2)}) copy-start(bf16[4,128,64]{2,1,0:T(8,128)(2,1)} %constant.65.clone.end_ref) | copy-start | bytes 196612
  1.8 16.8 %copy-start.7 = (s32[3,8]{1,0:T(4,128)S(1)}, s32[3,8]{1,0:T(4,128)}, u32[]{:S(2)}) copy-start(s32[3,8]{1,0:T(4,128)} %nb_ref.3) | copy-start | bytes 292
  1.8 16.8 %copy-start.8 = (s32[3,8]{1,0:T(4,128)S(1)}, s32[3,8]{1,0:T(4,128)}, u32[]{:S(2)}) copy-start(s32[3,8]{1,0:T(4,128)} %rot_ref.3) | copy-start | bytes 292
  1.8 16.8 %copy-start.9 = (s32[3,8]{1,0:T(4,128)S(1)}, s32[3,8]{1,0:T(4,128)}, u32[]{:S(2)}) copy-start(s32[3,8]{1,0:T(4,128)} %cor_ref.3) | copy-start | bytes 292
  2.1 14.7 %collective-permute-start = (bf16[12,64,128]{2,1,0:T(8,128)(2,1)S(1)}, bf16[12,64,128]{2,1,0:T(8,128)(2,1)S(1)}, u32[]{:S(2)}, u32[]{:S(2)}) collective-permute-start(bf16[12,64,128]{2,1,0:T(8,128)(2,1)S(1)} %pack_edges.1.own_ref), channel_id=1, source_target_pairs={{0,2},{1,3},{2,4},{3,5},{4,6},{5,7},{6,8},{7,9},{8,10},{9,11},{10,... | collective-permute-start | bytes 589832 | tf_op jit(solution)/shard_map/ppermute | solution.py:418
  5.1 11.8 %collective-permute-start.1 = (bf16[12,64,128]{2,1,0:T(8,128)(2,1)S(1)}, bf16[12,64,128]{2,1,0:T(8,128)(2,1)S(1)}, u32[]{:S(2)}, u32[]{:S(2)}) collective-permute-start(bf16[12,64,128]{2,1,0:T(8,128)(2,1)S(1)} %pack_edges.1.own_ref), channel_id=1, source_target_pairs={{0,30},{1,31},{2,0},{3,1},{4,2},{5,3},{6,4},{7,5},{8,6},{9,7},{10,... | collective-permute-start | bytes 589832 | tf_op jit(solution)/shard_map/ppermute | solution.py:418
  9.1 8.3 %collective-permute-start.2 = (bf16[12,64,128]{2,1,0:T(8,128)(2,1)S(1)}, bf16[12,64,128]{2,1,0:T(8,128)(2,1)S(1)}, u32[]{:S(2)}, u32[]{:S(2)}) collective-permute-start(bf16[12,64,128]{2,1,0:T(8,128)(2,1)S(1)} %pack_edges.1.own_ref), channel_id=1, source_target_pairs={{0,1},{1,0},{2,3},{3,2},{4,5},{5,4},{6,7},{7,6},{8,9},{9,8},{10,11... | collective-permute-start | bytes 589832 | tf_op jit(solution)/shard_map/ppermute | solution.py:422
  16.9 1.6 %collective-permute-start.3 = (bf16[12,64,128]{2,1,0:T(8,128)(2,1)S(1)}, bf16[12,64,128]{2,1,0:T(8,128)(2,1)S(1)}, u32[]{:S(2)}, u32[]{:S(2)}) collective-permute-start(bf16[12,64,128]{2,1,0:T(8,128)(2,1)S(1)} %broadcast_select_fusion), channel_id=1, source_target_pairs={{0,1},{1,0},{2,3},{3,2},{4,5},{5,4},{6,7},{7,6},{8,9},{9,8},{10,11... | collective-permute-start | bytes 589832 | tf_op jit(solution)/shard_map/ppermute | solution.py:422
  20.8 15.7 %copy-start.1 = (bf16[3,3,128,128]{3,2,1,0:T(8,128)(2,1)S(1)}, bf16[3,3,128,128]{3,2,1,0:T(8,128)(2,1)}, u32[]{:S(2)}) copy-start(bf16[3,3,128,128]{3,2,1,0:T(8,128)(2,1)} %param.12) | copy-start | bytes 884740
  20.8 1.7 %collective-permute-start.4 = (f32[640,128]{1,0:T(8,128)S(1)}, f32[640,128]{1,0:T(8,128)S(1)}, u32[]{:S(2)}, u32[]{:S(2)}) collective-permute-start(f32[640,128]{1,0:T(8,128)S(1)} %get-tuple-element.31), channel_id=1, source_target_pairs={{0,1},{1,0},{2,3},{3,2},{4,5},{5,4},{6,7},{7,6},{8,9},{9,8},{10,11... | collective-permute-start | bytes 983048 | tf_op jit(solution)/shard_map/ppermute | solution.py:422
  21.2 4.9 %collective-permute-start.11 = (bf16[24,64,128]{2,1,0:T(8,128)(2,1)}, bf16[24,64,128]{2,1,0:T(8,128)(2,1)S(1)}, u32[]{:S(2)}, u32[]{:S(2)}) collective-permute-start(bf16[24,64,128]{2,1,0:T(8,128)(2,1)} %get-tuple-element.33), channel_id=1, source_target_pairs={{0,1},{1,0},{2,3},{3,2},{4,5},{5,4},{6,7},{7,6},{8,9},{9,8},{10,11... | collective-permute-start | bytes 1179656 | tf_op jit(solution)/shard_map/ppermute | solution.py:422
  22.6 6.2 %collective-permute-start.5 = (bf16[160,128]{1,0:T(8,128)(2,1)S(1)}, bf16[160,128]{1,0:T(8,128)(2,1)S(1)}, u32[]{:S(2)}, u32[]{:S(2)}) collective-permute-start(bf16[160,128]{1,0:T(8,128)(2,1)S(1)} %get-tuple-element.54), channel_id=1, source_target_pairs={{0,2},{1,3},{2,0},{3,1},{4,6},{5,7},{6,4},{7,5},{8,10},{9,11},{10,... | collective-permute-start | bytes 122888 | tf_op jit(solution)/shard_map/ppermute | solution.py:422
  22.7 6.2 %collective-permute-start.6 = (bf16[160,128]{1,0:T(8,128)(2,1)S(1)}, bf16[160,128]{1,0:T(8,128)(2,1)S(1)}, u32[]{:S(2)}, u32[]{:S(2)}) collective-permute-start(bf16[160,128]{1,0:T(8,128)(2,1)S(1)} %get-tuple-element.56), channel_id=1, source_target_pairs={{0,4},{1,5},{2,6},{3,7},{4,0},{5,1},{6,2},{7,3},{8,12},{9,13},{10,... | collective-permute-start | bytes 122888 | tf_op jit(solution)/shard_map/ppermute | solution.py:422
  22.9 9.1 %collective-permute-start.7 = (bf16[160,128]{1,0:T(8,128)(2,1)S(1)}, bf16[160,128]{1,0:T(8,128)(2,1)S(1)}, u32[]{:S(2)}, u32[]{:S(2)}) collective-permute-start(bf16[160,128]{1,0:T(8,128)(2,1)S(1)} %get-tuple-element.55), channel_id=1, source_target_pairs={{0,6},{1,7},{2,4},{3,5},{4,2},{5,3},{6,0},{7,1},{8,14},{9,15},{10,... | collective-permute-start | bytes 122888 | tf_op jit(solution)/shard_map/ppermute | solution.py:422
  26.3 12.7 %collective-permute-start.12 = (bf16[12,64,128]{2,1,0:T(8,128)(2,1)S(1)}, bf16[12,64,128]{2,1,0:T(8,128)(2,1)S(1)}, u32[]{:S(2)}, u32[]{:S(2)}) collective-permute-start(bf16[12,64,128]{2,1,0:T(8,128)(2,1)S(1)} %get-tuple-element.49), channel_id=1, source_target_pairs={{0,30},{1,31},{2,0},{3,1},{4,2},{5,3},{6,4},{7,5},{8,6},{9,7},{10,... | collective-permute-start | bytes 589832 | tf_op jit(solution)/shard_map/ppermute | solution.py:418
  28.8 11.0 %collective-permute-start.13 = (bf16[12,64,128]{2,1,0:T(8,128)(2,1)S(1)}, bf16[12,64,128]{2,1,0:T(8,128)(2,1)S(1)}, u32[]{:S(2)}, u32[]{:S(2)}) collective-permute-start(bf16[12,64,128]{2,1,0:T(8,128)(2,1)S(1)} %get-tuple-element.48), channel_id=1, source_target_pairs={{0,2},{1,3},{2,4},{3,5},{4,6},{5,7},{6,8},{7,9},{8,10},{9,11},{10,... | collective-permute-start | bytes 589832 | tf_op jit(solution)/shard_map/ppermute | solution.py:418
  32.0 7.7 %collective-permute-start.10 = (bf16[160,128]{1,0:T(8,128)(2,1)S(1)}, bf16[160,128]{1,0:T(8,128)(2,1)S(1)}, u32[]{:S(2)}, u32[]{:S(2)}) collective-permute-start(bf16[160,128]{1,0:T(8,128)(2,1)S(1)} %add_convert_fusion), channel_id=1, source_target_pairs={{0,24},{1,25},{2,26},{3,27},{4,28},{5,29},{6,30},{7,31},{8,16},{9,... | collective-permute-start | bytes 122888 | tf_op jit(solution)/shard_map/ppermute | solution.py:422
  32.1 7.7 %collective-permute-start.8 = (bf16[160,128]{1,0:T(8,128)(2,1)S(1)}, bf16[160,128]{1,0:T(8,128)(2,1)S(1)}, u32[]{:S(2)}, u32[]{:S(2)}) collective-permute-start(bf16[160,128]{1,0:T(8,128)(2,1)S(1)} %add_convert_fusion), channel_id=1, source_target_pairs={{0,8},{1,9},{2,10},{3,11},{4,12},{5,13},{6,14},{7,15},{8,0},{9,1},... | collective-permute-start | bytes 122888 | tf_op jit(solution)/shard_map/ppermute | solution.py:422
  32.2 7.6 %collective-permute-start.9 = (bf16[160,128]{1,0:T(8,128)(2,1)S(1)}, bf16[160,128]{1,0:T(8,128)(2,1)S(1)}, u32[]{:S(2)}, u32[]{:S(2)}) collective-permute-start(bf16[160,128]{1,0:T(8,128)(2,1)S(1)} %add_convert_fusion), channel_id=1, source_target_pairs={{0,16},{1,17},{2,18},{3,19},{4,20},{5,21},{6,22},{7,23},{8,24},{9,... | collective-permute-start | bytes 122888 | tf_op jit(solution)/shard_map/ppermute | solution.py:422
  39.8 5.4 %collective-permute-start.16 = (f32[160,128]{1,0:T(8,128)S(1)}, f32[160,128]{1,0:T(8,128)S(1)}, u32[]{:S(2)}, u32[]{:S(2)}) collective-permute-start(f32[160,128]{1,0:T(8,128)S(1)} %add_add_fusion), channel_id=1, source_target_pairs={{0,6},{1,7},{2,4},{3,5},{4,2},{5,3},{6,0},{7,1},{8,14},{9,15},{10,... | collective-permute-start | bytes 245768 | tf_op jit(solution)/shard_map/ppermute | solution.py:422
  42.7 4.4 %collective-permute-start.14 = (f32[160,128]{1,0:T(8,128)S(1)}, f32[160,128]{1,0:T(8,128)S(1)}, u32[]{:S(2)}, u32[]{:S(2)}) collective-permute-start(f32[160,128]{1,0:T(8,128)S(1)} %add_add_fusion), channel_id=1, source_target_pairs={{0,2},{1,3},{2,0},{3,1},{4,6},{5,7},{6,4},{7,5},{8,10},{9,11},{10,... | collective-permute-start | bytes 245768 | tf_op jit(solution)/shard_map/ppermute | solution.py:422
  42.7 4.4 %collective-permute-start.15 = (f32[160,128]{1,0:T(8,128)S(1)}, f32[160,128]{1,0:T(8,128)S(1)}, u32[]{:S(2)}, u32[]{:S(2)}) collective-permute-start(f32[160,128]{1,0:T(8,128)S(1)} %add_add_fusion), channel_id=1, source_target_pairs={{0,4},{1,5},{2,6},{3,7},{4,0},{5,1},{6,2},{7,3},{8,12},{9,13},{10,... | collective-permute-start | bytes 245768 | tf_op jit(solution)/shard_map/ppermute | solution.py:422
  47.2 1.7 %collective-permute-start.17 = (f32[640,128]{1,0:T(8,128)S(1)}, f32[640,128]{1,0:T(8,128)S(1)}, u32[]{:S(2)}, u32[]{:S(2)}) collective-permute-start(f32[640,128]{1,0:T(8,128)S(1)} %pad_maximum_fusion.1.mine_ref), channel_id=1, source_target_pairs={{0,1},{1,0},{2,3},{3,2},{4,5},{5,4},{6,7},{7,6},{8,9},{9,8},{10,11... | collective-permute-start | bytes 983048 | tf_op jit(solution)/shard_map/ppermute | solution.py:422
  (5 other events, 39.9 us)

commit v4 on v3

--- a/solution.py
+++ b/solution.py
@@ -314,10 +314,12 @@
         for i, (a, b) in enumerate(SIDE_TAPS[s]):
             rows = slice((a * 3 + b) * 128, (a * 3 + b + 1) * 128)
             total_ref[rows, :] = total_ref[rows, :] + grads[i * 128 : (i + 1) * 128]
-    half = 5 * 128
+    taps = 9 * 128
+    half = taps // 2
     core = lax.rem(me, 2)
-    send_ref[...] = total_ref[pl.ds(pl.multiple_of((1 - core) * half, 128), half), :] * factor
-    keep_ref[...] = total_ref[pl.ds(pl.multiple_of(core * half, 128), half), :] * factor
+    for target, which in ((send_ref, 1 - core), (keep_ref, core)):
+        target[0:half, :] = total_ref[pl.ds(pl.multiple_of(which * half, 64), half), :] * factor
+        target[half:, :] = total_ref[taps : taps + target.shape[0] - half, :] * factor
     finish(leaving)
 
 
@@ -376,35 +378,26 @@
     finish(leaving)
 
 
-def result_kernel(me_ref, mine_ref, other_ref, grad_ref, bias_ref, sems, *, taps):
+def half_kernel(me_ref, half_ref, *refs, mates):
+    grad_ref, sem = refs[1 if mates else 0], refs[-1]
+    half = grad_ref.shape[0] // 2
     core = lax.rem(me_ref[0], 2)
-    half = mine_ref.shape[0]
-    rest = taps - half
-
-    def write(low_ref, high_ref):
-        leaving = [
-            begin(low_ref, grad_ref.at[pl.ds(0, half)], sems.at[0]),
-            begin(high_ref.at[pl.ds(0, rest)], grad_ref.at[pl.ds(half, rest)], sems.at[1]),
-        ]
-        bias_ref[...] = high_ref[rest : rest + 1, :]
-        finish(leaving)
-
-    @pl.when(core == 0)
-    def _():
-        write(mine_ref, other_ref)
-
-    @pl.when(core == 1)
-    def _():
-        write(other_ref, mine_ref)
-
-
-def call(kernel, name, operands, outs, scratch, copies, small=(), room=4):
+    at = (1 - core) * half if mates else core * half
+    copy = begin(half_ref.at[pl.ds(0, half)], grad_ref.at[pl.ds(pl.multiple_of(at, 64), half)], sem.at[0])
+    if not mates:
+        bias_ref = refs[1]
+        bias_ref[...] = half_ref[half : half + 1, :]
+    copy.wait()
+
+
+def call(kernel, name, operands, outs, scratch, copies, small=(), room=4, aliases=None):
     spaces = {"s": pltpu.SMEM, "h": pltpu.HBM, "a": pl.ANY, "v": pltpu.VMEM}
     out_specs = [pl.BlockSpec(memory_space=pltpu.VMEM if i in small else pl.ANY) for i in range(len(outs))]
     return pl.pallas_call(
         kernel,
         name=name,
         out_shape=list(outs),
+        input_output_aliases=aliases or {},
         in_specs=[pl.BlockSpec(memory_space=spaces[o]) for o in operands],
         out_specs=out_specs,
         scratch_shapes=list(scratch) + [pltpu.SemaphoreType.DMA((copies,))],
@@ -430,7 +423,7 @@
     mine = keep + swapped(send, 1)
     quarter = mine.shape[0] // 4
     at = (me // 2) % 4
-    arrived = [swapped(part_of(mine, at ^ k, quarter).astype(BF), 2 * k) for k in range(1, 4)]
+    arrived = [swapped(part_of(mine, at ^ k, quarter).astype(BF), 2 * k) for k in (3, 2, 1)]
     mine = part_of(mine, at, quarter)
     for a in arrived:
         mine = mine + a.astype(F32)
@@ -578,10 +571,14 @@
         return value
 
     mine, other = summed(keep, send, me, devices, between, last)
+    grad_shapes = [shape((9 * chans, chans), F32), shape((1, chans), F32)]
     weight_grad, bias_grad = call(
-        functools.partial(result_kernel, taps=9 * chans), "order_kernel_grad", "svv",
-        [shape((9 * chans, chans), F32), shape((1, chans), F32)], [], 2, small=(1,), room=ROOM,
-    )(me_arr, mine, other)
+        functools.partial(half_kernel, mates=False), "place_own_half", "sv", grad_shapes, [], 1, small=(1,), room=ROOM,
+    )(me_arr, mine)
+    (weight_grad,) = call(
+        functools.partial(half_kernel, mates=True), "place_mates_half", "sva", grad_shapes[:1], [], 1, room=ROOM,
+        aliases={2: 0},
+    )(me_arr, other, weight_grad)
     return (
         results["out"].reshape(inputs.shape),
         results["in"].reshape(inputs.shape),

time: 50.5 us -> 49.4 us (0.978)
  waiting for transfers between devices: 10 us -> 8.27 us
  Pallas kernels: 15.5 us -> 16.2 us
    ppermute x14, waiting for transfers between devices: 9.25 us -> 7.56 us  [swapped(): lax.ppermute(value, 'patch', [(d, d ^ mask) for d in range(lax.axis_size(...]
    pallas_call x1 -> x2, Pallas kernels: 1.34 us -> 1.96 us  [the longest x1 1.24 us: body(): call(functools.partial(half_kernel, mates=False), 'place_own_half', 'sv',...]
  transfers between devices with their start and end apart: 18 -> 18, of which waited for: 7 -> 8; matrix products, arithmetic and copies ran while one was open for 0% -> 0% of each run, Pallas kernels for 23% -> 26%
where the time goes in v4:
time: 49.4 us; the launch traced here: 49.2 us
  starting transfers between devices  22.4 us (45%)
  Pallas kernels  16.2 us (33%)
  waiting for transfers between devices  8.27 us (17%)
  local copies, waits for them, and re-layouts  1.24 us (3%)
  between operations  0.87 us (2%)
    ppermute x14, starting transfers between devices, swapped(): lax.ppermute(value, 'patch', [(d, d ^ mask) for d in range(lax.axis_size(...  12.8 us
    ppermute x4, starting transfers between devices, shifted(): lax.ppermute(value, 'patch', [(d, (d + steps) % count) for d in range(cou...  9.58 us
    pallas_call x1, Pallas kernels, own_pixels(): call(functools.partial(own_kernel, length=length, devices=devices), 'own_...  7.68 us
    ppermute x14, waiting for transfers between devices, swapped(): lax.ppermute(value, 'patch', [(d, d ^ mask) for d in range(lax.axis_size(...  7.56 us
    pallas_call x1, Pallas kernels, body(): call(functools.partial(forward_kernel, length=length), 'add_halo_outputs'...  2.52 us
    pallas_call x1, Pallas kernels, body(): call(functools.partial(halo_kernel, length=length, devices=devices, facto...  2.22 us
    pallas_call x1, Pallas kernels, last(): call(functools.partial(join_kernel, length=length), 'join_input_grad', 'a...  1.49 us
    pallas_call x1, Pallas kernels, body(): call(functools.partial(half_kernel, mates=False), 'place_own_half', 'sv',...  1.24 us
  transfers between devices with their start and end apart: 18, of which 8 were waited for; matrix products, arithmetic and copies ran while one was open for 0% of the time, Pallas kernels for 26%

profile of v4, /device:TPU:0, one launch (start us, length us, event | category | flops | bytes accessed | tf_op | source)
XLA Modules:
  0.0 49.2 jit_solution(1247794156207163961)
XLA Ops:
  0.6 1.1 %copy-done = bf16[3,32,32,128]{3,2,1,0:T(8,128)(2,1)S(1)} copy-done((bf16[3,32,32,128]{3,2,1,0:T(8,128)(2,1)S(1)}, bf16[3,32,32,128]{3,2,1,0:T(8,128)(2,1)}, u32[]{:S(2)}) %copy-start) | copy-done | bytes 786456
  2.1 3.0 %collective-permute-start = (bf16[12,64,128]{2,1,0:T(8,128)(2,1)S(1)}, bf16[12,64,128]{2,1,0:T(8,128)(2,1)S(1)}, u32[]{:S(2)}, u32[]{:S(2)}) collective-permute-start(bf16[12,64,128]{2,1,0:T(8,128)(2,1)S(1)} %pack_edges.1.own_ref), channel_id=1, source_target_pairs={{0,2},{1,3},{2,4},{3,5},{4,6},{5,7},{6,8},{7,9},{8,10},{9,11},{10,... | collective-permute-start | bytes 589832 | tf_op jit(solution)/shard_map/ppermute | solution.py:411
  5.1 4.1 %collective-permute-start.1 = (bf16[12,64,128]{2,1,0:T(8,128)(2,1)S(1)}, bf16[12,64,128]{2,1,0:T(8,128)(2,1)S(1)}, u32[]{:S(2)}, u32[]{:S(2)}) collective-permute-start(bf16[12,64,128]{2,1,0:T(8,128)(2,1)S(1)} %pack_edges.1.own_ref), channel_id=1, source_target_pairs={{0,30},{1,31},{2,0},{3,1},{4,2},{5,3},{6,4},{7,5},{8,6},{9,7},{10,... | collective-permute-start | bytes 589832 | tf_op jit(solution)/shard_map/ppermute | solution.py:411
  9.1 7.7 %own_pixels.1 = (f32[12,64,128]{2,1,0:T(8,128)}, f32[24,64,128]{2,1,0:T(8,128)}, bf16[24,64,128]{2,1,0:T(8,128)(2,1)}, f32[2048,128]{1,0:T(8,128)}, bf16[3,8,128...) custom-call(s32[1]{0:T(128)} %bitcast.me_ref, s32[3,8]{1,0:T(4,128)} %nb_ref.3, s32[3,8]{1,0:T(4,128)} %rot_ref.3, ...), custom_call_target="tpu_custom_call" | custom-call | tf_op jit(solution)/shard_map/own_pixels/pallas_call | solution.py:456
  16.9 0.6 %collective-permute-start.3 = (bf16[12,64,128]{2,1,0:T(8,128)(2,1)S(1)}, bf16[12,64,128]{2,1,0:T(8,128)(2,1)S(1)}, u32[]{:S(2)}, u32[]{:S(2)}) collective-permute-start(bf16[12,64,128]{2,1,0:T(8,128)(2,1)S(1)} %broadcast_select_fusion), channel_id=1, source_target_pairs={{0,1},{1,0},{2,3},{3,2},{4,5},{5,4},{6,7},{7,6},{8,9},{9,8},{10,11... | collective-permute-start | bytes 589832 | tf_op jit(solution)/shard_map/ppermute | solution.py:415
  17.5 1.1 %collective-permute-done.3.across_ref = bf16[12,64,128]{2,1,0:T(8,128)(2,1)S(1)} collective-permute-done((bf16[12,64,128]{2,1,0:T(8,128)(2,1)S(1)}, bf16[12,64,128]{2,1,0:T(8,128)(2,1)S(1)}, u32[]{:S(2)}, u32[]{:S(2)}) %collective-permute-start.3) | collective-permute-done | bytes 196640 | tf_op jit(solution)/shard_map/ppermute | solution.py:415
  18.5 2.2 %halo_kernel_grad.1 = (f32[640,128]{1,0:T(8,128)S(1)}, f32[640,128]{1,0:T(8,128)S(1)}, bf16[4,192,384]{2,1,0:T(8,128)(2,1)}) custom-call(s32[1]{0:T(128)} %bitcast.me_ref, s32[3,8]{1,0:T(4,128)S(1)} %copy-done.7, s32[3,8]{1,0:T(4,128)S(1)} %copy-done.8, s32[3,8]{1,0:T(4,128)S(1)} %copy-done.9, bf16[12,64,128]{2,1,0:T(8,128)(2,1)S(1)} %pack_edges.1.own_ref, ...), custom_call_target="tpu_custom_call" | custom-call | tf_op jit(solution)/shard_map/halo_kernel_grad/pallas_call | solution.py:525
  20.8 0.4 collective-permute-start.4
  21.4 1.1 %collective-permute-done.4 = f32[640,128]{1,0:T(8,128)S(1)} collective-permute-done((f32[640,128]{1,0:T(8,128)S(1)}, f32[640,128]{1,0:T(8,128)S(1)}, u32[]{:S(2)}, u32[]{:S(2)}) %collective-permute-start.4) | collective-permute-done | bytes 327712 | tf_op jit(solution)/shard_map/ppermute | solution.py:415
  22.7 1.4 %collective-permute-start.6 = (bf16[160,128]{1,0:T(8,128)(2,1)S(1)}, bf16[160,128]{1,0:T(8,128)(2,1)S(1)}, u32[]{:S(2)}, u32[]{:S(2)}) collective-permute-start(bf16[160,128]{1,0:T(8,128)(2,1)S(1)} %get-tuple-element.56), channel_id=1, source_target_pairs={{0,4},{1,5},{2,6},{3,7},{4,0},{5,1},{6,2},{7,3},{8,12},{9,13},{10,... | collective-permute-start | bytes 122888 | tf_op jit(solution)/shard_map/ppermute | solution.py:415
  24.0 2.1 %collective-permute-start.7 = (bf16[160,128]{1,0:T(8,128)(2,1)S(1)}, bf16[160,128]{1,0:T(8,128)(2,1)S(1)}, u32[]{:S(2)}, u32[]{:S(2)}) collective-permute-start(bf16[160,128]{1,0:T(8,128)(2,1)S(1)} %get-tuple-element.55), channel_id=1, source_target_pairs={{0,2},{1,3},{2,0},{3,1},{4,6},{5,7},{6,4},{7,5},{8,10},{9,11},{10,... | collective-permute-start | bytes 122888 | tf_op jit(solution)/shard_map/ppermute | solution.py:415
  26.3 2.5 %collective-permute-start.12 = (bf16[12,64,128]{2,1,0:T(8,128)(2,1)S(1)}, bf16[12,64,128]{2,1,0:T(8,128)(2,1)S(1)}, u32[]{:S(2)}, u32[]{:S(2)}) collective-permute-start(bf16[12,64,128]{2,1,0:T(8,128)(2,1)S(1)} %get-tuple-element.49), channel_id=1, source_target_pairs={{0,30},{1,31},{2,0},{3,1},{4,2},{5,3},{6,4},{7,5},{8,6},{9,7},{10,... | collective-permute-start | bytes 589832 | tf_op jit(solution)/shard_map/ppermute | solution.py:411
  28.8 3.2 %collective-permute-done.7 = bf16[160,128]{1,0:T(8,128)(2,1)S(1)} collective-permute-done((bf16[160,128]{1,0:T(8,128)(2,1)S(1)}, bf16[160,128]{1,0:T(8,128)(2,1)S(1)}, u32[]{:S(2)}, u32[]{:S(2)}) %collective-permute-start.7) | collective-permute-done | bytes 40992 | tf_op jit(solution)/shard_map/ppermute | solution.py:415
  32.2 4.3 %collective-permute-start.9 = (bf16[160,128]{1,0:T(8,128)(2,1)S(1)}, bf16[160,128]{1,0:T(8,128)(2,1)S(1)}, u32[]{:S(2)}, u32[]{:S(2)}) collective-permute-start(bf16[160,128]{1,0:T(8,128)(2,1)S(1)} %add_convert_fusion), channel_id=1, source_target_pairs={{0,16},{1,17},{2,18},{3,19},{4,20},{5,21},{6,22},{7,23},{8,24},{9,... | collective-permute-start | bytes 122888 | tf_op jit(solution)/shard_map/ppermute | solution.py:415
  36.5 2.5 %add_halo_outputs.1 = bf16[3,1024,128]{2,1,0:T(8,128)(2,1)} custom-call(f32[3,1024,128]{2,1,0:T(8,128)} %bitcast.28, bf16[9,128,128]{2,1,0:T(8,128)(2,1)S(1)} %bitcast.26, bf16[4,192,384]{2,1,0:T(8,128)(2,1)S(1)} %copy-done.3), custom_call_target="tpu_custom_call" | custom-call | tf_op jit(solution)/shard_map/add_halo_outputs/pallas_call | solution.py:544
  39.1 0.7 %collective-permute-done.13.low_ref = bf16[12,64,128]{2,1,0:T(8,128)(2,1)S(1)} collective-permute-done((bf16[12,64,128]{2,1,0:T(8,128)(2,1)S(1)}, bf16[12,64,128]{2,1,0:T(8,128)(2,1)S(1)}, u32[]{:S(2)}, u32[]{:S(2)}) %collective-permute-start.13) | collective-permute-done | bytes 196640 | tf_op jit(solution)/shard_map/ppermute | solution.py:411
  39.8 2.0 %collective-permute-start.16 = (f32[160,128]{1,0:T(8,128)S(1)}, f32[160,128]{1,0:T(8,128)S(1)}, u32[]{:S(2)}, u32[]{:S(2)}) collective-permute-start(f32[160,128]{1,0:T(8,128)S(1)} %add_add_fusion), channel_id=1, source_target_pairs={{0,6},{1,7},{2,4},{3,5},{4,2},{5,3},{6,0},{7,1},{8,14},{9,15},{10,... | collective-permute-start | bytes 245768 | tf_op jit(solution)/shard_map/ppermute | solution.py:415
  41.9 1.5 %collective-permute-start.15 = (f32[160,128]{1,0:T(8,128)S(1)}, f32[160,128]{1,0:T(8,128)S(1)}, u32[]{:S(2)}, u32[]{:S(2)}) collective-permute-start(f32[160,128]{1,0:T(8,128)S(1)} %add_add_fusion), channel_id=1, source_target_pairs={{0,4},{1,5},{2,6},{3,7},{4,0},{5,1},{6,2},{7,3},{8,12},{9,13},{10,... | collective-permute-start | bytes 245768 | tf_op jit(solution)/shard_map/ppermute | solution.py:415
  43.4 1.5 %join_input_grad.1 = bf16[3,1024,128]{2,1,0:T(8,128)(2,1)} custom-call(bf16[3,1024,128]{2,1,0:T(8,128)(2,1)S(1)} %bitcast.27, f32[12,64,128]{2,1,0:T(8,128)S(1)} %copy-done.4, bf16[24,64,128]{2,1,0:T(8,128)(2,1)S(1)} %collective-permute-done.11.near_ref, bf16[12,64,128]{2,1,0:T(8,128)(2,1)S(1)} %collective-permute-done.13.low_ref, ...), custom_call_target="tpu_custom_call" | custom-call | tf_op jit(solution)/shard_map/join_input_grad/pallas_call | solution.py:560
  44.9 0.5 collective-permute-done.16
  45.3 0.9 %collective-permute-done.14 = f32[160,128]{1,0:T(8,128)S(1)} collective-permute-done((f32[160,128]{1,0:T(8,128)S(1)}, f32[160,128]{1,0:T(8,128)S(1)}, u32[]{:S(2)}, u32[]{:S(2)}) %collective-permute-start.14) | collective-permute-done | bytes 81952 | tf_op jit(solution)/shard_map/ppermute | solution.py:415
  46.3 0.4 collective-permute-done.15
  46.8 1.2 %place_own_half.1 = (f32[1152,128]{1,0:T(8,128)}, f32[1,128]{1,0:T(1,128)}) custom-call(s32[1]{0:T(128)} %bitcast.me_ref, f32[640,128]{1,0:T(8,128)S(1)} %pad_maximum_fusion.1.half_ref), custom_call_target="tpu_custom_call" | custom-call | tf_op jit(solution)/shard_map/place_own_half/pallas_call | solution.py:575
  48.4 0.7 %place_mates_half.1 = f32[1152,128]{1,0:T(8,128)} custom-call(s32[1]{0:T(128)} %bitcast.me_ref, f32[640,128]{1,0:T(8,128)S(1)} %collective-permute-done.17.half_ref, f32[1152,128]{1,0:T(8,128)} %get-tuple-element.46.refs_0_), custom_call_target="tpu_custom_call", output_to_operand_aliasing={{}: (2, {})} | custom-call | tf_op jit(solution)/shard_map/place_mates_half/pallas_call | solution.py:578
  (50 shorter events, 1.6 us)
Async XLA Ops:
  1.8 16.8 %copy-start.5 = (bf16[4,192,64]{2,1,0:T(8,128)(2,1)S(1)}, bf16[4,192,64]{2,1,0:T(8,128)(2,1)}, u32[]{:S(2)}) copy-start(bf16[4,192,64]{2,1,0:T(8,128)(2,1)} %constant.64.clone.side_ref) | copy-start | bytes 294916
  1.8 16.8 %copy-start.6 = (bf16[4,128,64]{2,1,0:T(8,128)(2,1)S(1)}, bf16[4,128,64]{2,1,0:T(8,128)(2,1)}, u32[]{:S(2)}) copy-start(bf16[4,128,64]{2,1,0:T(8,128)(2,1)} %constant.65.clone.end_ref) | copy-start | bytes 196612
  1.8 16.8 %copy-start.7 = (s32[3,8]{1,0:T(4,128)S(1)}, s32[3,8]{1,0:T(4,128)}, u32[]{:S(2)}) copy-start(s32[3,8]{1,0:T(4,128)} %nb_ref.3) | copy-start | bytes 292
  1.8 16.8 %copy-start.8 = (s32[3,8]{1,0:T(4,128)S(1)}, s32[3,8]{1,0:T(4,128)}, u32[]{:S(2)}) copy-start(s32[3,8]{1,0:T(4,128)} %rot_ref.3) | copy-start | bytes 292
  1.8 16.8 %copy-start.9 = (s32[3,8]{1,0:T(4,128)S(1)}, s32[3,8]{1,0:T(4,128)}, u32[]{:S(2)}) copy-start(s32[3,8]{1,0:T(4,128)} %cor_ref.3) | copy-start | bytes 292
  2.1 14.7 %collective-permute-start = (bf16[12,64,128]{2,1,0:T(8,128)(2,1)S(1)}, bf16[12,64,128]{2,1,0:T(8,128)(2,1)S(1)}, u32[]{:S(2)}, u32[]{:S(2)}) collective-permute-start(bf16[12,64,128]{2,1,0:T(8,128)(2,1)S(1)} %pack_edges.1.own_ref), channel_id=1, source_target_pairs={{0,2},{1,3},{2,4},{3,5},{4,6},{5,7},{6,8},{7,9},{8,10},{9,11},{10,... | collective-permute-start | bytes 589832 | tf_op jit(solution)/shard_map/ppermute | solution.py:411
  5.1 11.8 %collective-permute-start.1 = (bf16[12,64,128]{2,1,0:T(8,128)(2,1)S(1)}, bf16[12,64,128]{2,1,0:T(8,128)(2,1)S(1)}, u32[]{:S(2)}, u32[]{:S(2)}) collective-permute-start(bf16[12,64,128]{2,1,0:T(8,128)(2,1)S(1)} %pack_edges.1.own_ref), channel_id=1, source_target_pairs={{0,30},{1,31},{2,0},{3,1},{4,2},{5,3},{6,4},{7,5},{8,6},{9,7},{10,... | collective-permute-start | bytes 589832 | tf_op jit(solution)/shard_map/ppermute | solution.py:411
  9.1 8.3 %collective-permute-start.2 = (bf16[12,64,128]{2,1,0:T(8,128)(2,1)S(1)}, bf16[12,64,128]{2,1,0:T(8,128)(2,1)S(1)}, u32[]{:S(2)}, u32[]{:S(2)}) collective-permute-start(bf16[12,64,128]{2,1,0:T(8,128)(2,1)S(1)} %pack_edges.1.own_ref), channel_id=1, source_target_pairs={{0,1},{1,0},{2,3},{3,2},{4,5},{5,4},{6,7},{7,6},{8,9},{9,8},{10,11... | collective-permute-start | bytes 589832 | tf_op jit(solution)/shard_map/ppermute | solution.py:415
  16.9 1.6 %collective-permute-start.3 = (bf16[12,64,128]{2,1,0:T(8,128)(2,1)S(1)}, bf16[12,64,128]{2,1,0:T(8,128)(2,1)S(1)}, u32[]{:S(2)}, u32[]{:S(2)}) collective-permute-start(bf16[12,64,128]{2,1,0:T(8,128)(2,1)S(1)} %broadcast_select_fusion), channel_id=1, source_target_pairs={{0,1},{1,0},{2,3},{3,2},{4,5},{5,4},{6,7},{7,6},{8,9},{9,8},{10,11... | collective-permute-start | bytes 589832 | tf_op jit(solution)/shard_map/ppermute | solution.py:415
  20.8 15.8 %copy-start.1 = (bf16[3,3,128,128]{3,2,1,0:T(8,128)(2,1)S(1)}, bf16[3,3,128,128]{3,2,1,0:T(8,128)(2,1)}, u32[]{:S(2)}) copy-start(bf16[3,3,128,128]{3,2,1,0:T(8,128)(2,1)} %param.12) | copy-start | bytes 884740
  20.8 1.7 %collective-permute-start.4 = (f32[640,128]{1,0:T(8,128)S(1)}, f32[640,128]{1,0:T(8,128)S(1)}, u32[]{:S(2)}, u32[]{:S(2)}) collective-permute-start(f32[640,128]{1,0:T(8,128)S(1)} %get-tuple-element.31), channel_id=1, source_target_pairs={{0,1},{1,0},{2,3},{3,2},{4,5},{5,4},{6,7},{7,6},{8,9},{9,8},{10,11... | collective-permute-start | bytes 983048 | tf_op jit(solution)/shard_map/ppermute | solution.py:415
  21.2 4.9 %collective-permute-start.11 = (bf16[24,64,128]{2,1,0:T(8,128)(2,1)}, bf16[24,64,128]{2,1,0:T(8,128)(2,1)S(1)}, u32[]{:S(2)}, u32[]{:S(2)}) collective-permute-start(bf16[24,64,128]{2,1,0:T(8,128)(2,1)} %get-tuple-element.33), channel_id=1, source_target_pairs={{0,1},{1,0},{2,3},{3,2},{4,5},{5,4},{6,7},{7,6},{8,9},{9,8},{10,11... | collective-permute-start | bytes 1179656 | tf_op jit(solution)/shard_map/ppermute | solution.py:415
  22.6 6.2 %collective-permute-start.5 = (bf16[160,128]{1,0:T(8,128)(2,1)S(1)}, bf16[160,128]{1,0:T(8,128)(2,1)S(1)}, u32[]{:S(2)}, u32[]{:S(2)}) collective-permute-start(bf16[160,128]{1,0:T(8,128)(2,1)S(1)} %get-tuple-element.54), channel_id=1, source_target_pairs={{0,6},{1,7},{2,4},{3,5},{4,2},{5,3},{6,0},{7,1},{8,14},{9,15},{10,... | collective-permute-start | bytes 122888 | tf_op jit(solution)/shard_map/ppermute | solution.py:415
  22.7 6.2 %collective-permute-start.6 = (bf16[160,128]{1,0:T(8,128)(2,1)S(1)}, bf16[160,128]{1,0:T(8,128)(2,1)S(1)}, u32[]{:S(2)}, u32[]{:S(2)}) collective-permute-start(bf16[160,128]{1,0:T(8,128)(2,1)S(1)} %get-tuple-element.56), channel_id=1, source_target_pairs={{0,4},{1,5},{2,6},{3,7},{4,0},{5,1},{6,2},{7,3},{8,12},{9,13},{10,... | collective-permute-start | bytes 122888 | tf_op jit(solution)/shard_map/ppermute | solution.py:415
  24.0 8.1 %collective-permute-start.7 = (bf16[160,128]{1,0:T(8,128)(2,1)S(1)}, bf16[160,128]{1,0:T(8,128)(2,1)S(1)}, u32[]{:S(2)}, u32[]{:S(2)}) collective-permute-start(bf16[160,128]{1,0:T(8,128)(2,1)S(1)} %get-tuple-element.55), channel_id=1, source_target_pairs={{0,2},{1,3},{2,0},{3,1},{4,6},{5,7},{6,4},{7,5},{8,10},{9,11},{10,... | collective-permute-start | bytes 122888 | tf_op jit(solution)/shard_map/ppermute | solution.py:415
  26.3 12.8 %collective-permute-start.12 = (bf16[12,64,128]{2,1,0:T(8,128)(2,1)S(1)}, bf16[12,64,128]{2,1,0:T(8,128)(2,1)S(1)}, u32[]{:S(2)}, u32[]{:S(2)}) collective-permute-start(bf16[12,64,128]{2,1,0:T(8,128)(2,1)S(1)} %get-tuple-element.49), channel_id=1, source_target_pairs={{0,30},{1,31},{2,0},{3,1},{4,2},{5,3},{6,4},{7,5},{8,6},{9,7},{10,... | collective-permute-start | bytes 589832 | tf_op jit(solution)/shard_map/ppermute | solution.py:411
  28.8 11.0 %collective-permute-start.13 = (bf16[12,64,128]{2,1,0:T(8,128)(2,1)S(1)}, bf16[12,64,128]{2,1,0:T(8,128)(2,1)S(1)}, u32[]{:S(2)}, u32[]{:S(2)}) collective-permute-start(bf16[12,64,128]{2,1,0:T(8,128)(2,1)S(1)} %get-tuple-element.48), channel_id=1, source_target_pairs={{0,2},{1,3},{2,4},{3,5},{4,6},{5,7},{6,8},{7,9},{8,10},{9,11},{10,... | collective-permute-start | bytes 589832 | tf_op jit(solution)/shard_map/ppermute | solution.py:411
  32.1 7.7 %collective-permute-start.10 = (bf16[160,128]{1,0:T(8,128)(2,1)S(1)}, bf16[160,128]{1,0:T(8,128)(2,1)S(1)}, u32[]{:S(2)}, u32[]{:S(2)}) collective-permute-start(bf16[160,128]{1,0:T(8,128)(2,1)S(1)} %add_convert_fusion), channel_id=1, source_target_pairs={{0,24},{1,25},{2,26},{3,27},{4,28},{5,29},{6,30},{7,31},{8,16},{9,... | collective-permute-start | bytes 122888 | tf_op jit(solution)/shard_map/ppermute | solution.py:415
  32.2 7.6 %collective-permute-start.8 = (bf16[160,128]{1,0:T(8,128)(2,1)S(1)}, bf16[160,128]{1,0:T(8,128)(2,1)S(1)}, u32[]{:S(2)}, u32[]{:S(2)}) collective-permute-start(bf16[160,128]{1,0:T(8,128)(2,1)S(1)} %add_convert_fusion), channel_id=1, source_target_pairs={{0,8},{1,9},{2,10},{3,11},{4,12},{5,13},{6,14},{7,15},{8,0},{9,1},... | collective-permute-start | bytes 122888 | tf_op jit(solution)/shard_map/ppermute | solution.py:415
  32.2 7.6 %collective-permute-start.9 = (bf16[160,128]{1,0:T(8,128)(2,1)S(1)}, bf16[160,128]{1,0:T(8,128)(2,1)S(1)}, u32[]{:S(2)}, u32[]{:S(2)}) collective-permute-start(bf16[160,128]{1,0:T(8,128)(2,1)S(1)} %add_convert_fusion), channel_id=1, source_target_pairs={{0,16},{1,17},{2,18},{3,19},{4,20},{5,21},{6,22},{7,23},{8,24},{9,... | collective-permute-start | bytes 122888 | tf_op jit(solution)/shard_map/ppermute | solution.py:415
  39.8 5.5 %collective-permute-start.16 = (f32[160,128]{1,0:T(8,128)S(1)}, f32[160,128]{1,0:T(8,128)S(1)}, u32[]{:S(2)}, u32[]{:S(2)}) collective-permute-start(f32[160,128]{1,0:T(8,128)S(1)} %add_add_fusion), channel_id=1, source_target_pairs={{0,6},{1,7},{2,4},{3,5},{4,2},{5,3},{6,0},{7,1},{8,14},{9,15},{10,... | collective-permute-start | bytes 245768 | tf_op jit(solution)/shard_map/ppermute | solution.py:415
  41.8 4.4 %collective-permute-start.14 = (f32[160,128]{1,0:T(8,128)S(1)}, f32[160,128]{1,0:T(8,128)S(1)}, u32[]{:S(2)}, u32[]{:S(2)}) collective-permute-start(f32[160,128]{1,0:T(8,128)S(1)} %add_add_fusion), channel_id=1, source_target_pairs={{0,2},{1,3},{2,0},{3,1},{4,6},{5,7},{6,4},{7,5},{8,10},{9,11},{10,... | collective-permute-start | bytes 245768 | tf_op jit(solution)/shard_map/ppermute | solution.py:415
  41.9 4.7 %collective-permute-start.15 = (f32[160,128]{1,0:T(8,128)S(1)}, f32[160,128]{1,0:T(8,128)S(1)}, u32[]{:S(2)}, u32[]{:S(2)}) collective-permute-start(f32[160,128]{1,0:T(8,128)S(1)} %add_add_fusion), channel_id=1, source_target_pairs={{0,4},{1,5},{2,6},{3,7},{4,0},{5,1},{6,2},{7,3},{8,12},{9,13},{10,... | collective-permute-start | bytes 245768 | tf_op jit(solution)/shard_map/ppermute | solution.py:415
  46.7 1.7 %collective-permute-start.17 = (f32[640,128]{1,0:T(8,128)S(1)}, f32[640,128]{1,0:T(8,128)S(1)}, u32[]{:S(2)}, u32[]{:S(2)}) collective-permute-start(f32[640,128]{1,0:T(8,128)S(1)} %pad_maximum_fusion.1.half_ref), channel_id=1, source_target_pairs={{0,1},{1,0},{2,3},{3,2},{4,5},{5,4},{6,7},{7,6},{8,9},{9,8},{10,11... | collective-permute-start | bytes 983048 | tf_op jit(solution)/shard_map/ppermute | solution.py:415
  (5 other events, 39.9 us)

commit v5 on v4

--- a/solution.py
+++ b/solution.py
@@ -270,13 +270,13 @@
 
 def halo_kernel(
     me_ref, nb_ref, rot_ref, cor_ref, own_ref, low_ref, high_ref, mate_ref, across_ref, dw_ref,
-    side_ref, end_ref, keep_ref, send_ref, halo_ref,
-    nb_sm, rot_sm, cor_sm, pool_ref, total_ref, side_vm, end_vm, halo_vm, sems, *, length, devices, factor,
+    side_vm, end_vm, keep_ref, send_ref, halo_ref,
+    nb_sm, rot_sm, cor_sm, pool_ref, total_ref, halo_vm, sems, *, length, devices, factor,
 ):
     block = pool_ref.shape[0] // 5
     patches = block // 4
-    sources = [nb_ref, rot_ref, cor_ref, side_ref, end_ref]
-    targets = [nb_sm, rot_sm, cor_sm, side_vm, end_vm]
+    sources = [nb_ref, rot_ref, cor_ref]
+    targets = [nb_sm, rot_sm, cor_sm]
     arriving = [begin(a, b, sems.at[i]) for i, (a, b) in enumerate(zip(sources, targets))]
     used = len(arriving)
     later = [begin(dw_ref, total_ref, sems.at[used])]
@@ -524,7 +524,7 @@
     factor = 1.0 / (length * math.sqrt(patches * devices))
     keep, send, halo = call(
         functools.partial(halo_kernel, length=length, devices=devices, factor=factor), "halo_kernel_grad",
-        "shhhvvvvvahh",
+        "shhhvvvvvavv",
         [
             shape((rows // 2, chans), F32),
             shape((rows // 2, chans), F32),
@@ -534,11 +534,9 @@
         + [
             scratch((5 * block, size, chans), BF),
             scratch(dw.shape, F32),
-            scratch(sides.shape, BF),
-            scratch(ends.shape, BF),
             scratch((4, patches * size, 3 * chans), BF),
         ],
-        7, small=(0, 1), room=ROOM,
+        5, small=(0, 1), room=ROOM,
     )(*tables, edges, from_low, from_high, from_mate, from_across, dw, sides, ends)
 
     (outputs,) = call(
@@ -551,9 +549,8 @@
     results = {}
 
     def between(value):
-        value, results["high"], results["low"], results["out"] = lax.optimization_barrier(
-            (value, terms_high, terms_low, outputs)
-        )
+        value, results["low"], results["out"] = lax.optimization_barrier((value, terms_low, outputs))
+        results["high"] = terms_high
         return value
 
     def last(value):

time: 49.4 us -> 48.8 us (0.988)
  waiting for transfers between devices: 8.27 us -> 5.58 us
  starting transfers between devices: 22.4 us -> 24.7 us
    ppermute x4, starting transfers between devices: 9.58 us -> 11.7 us  [shifted(): lax.ppermute(value, 'patch', [(d, (d + steps) % count) for d in range(cou...]
    ppermute x14, waiting for transfers between devices: 7.56 us -> 5.57 us  [swapped(): lax.ppermute(value, 'patch', [(d, d ^ mask) for d in range(lax.axis_size(...]
    ppermute x4, waiting for transfers between devices: 0.71 us -> 0.01 us  [shifted(): lax.ppermute(value, 'patch', [(d, (d + steps) % count) for d in range(cou...]
  transfers between devices with their start and end apart: 18 -> 18, of which waited for: 8 -> 7; matrix products, arithmetic and copies ran while one was open for 0% -> 1% of each run, Pallas kernels for 26% -> 27%
where the time goes in v5:
time: 48.8 us; the launch traced here: 48.5 us
  starting transfers between devices  24.7 us (51%)
  Pallas kernels  15.9 us (33%)
  waiting for transfers between devices  5.58 us (11%)
  local copies, waits for them, and re-layouts  1.24 us (3%)
  between operations  0.89 us (2%)
    ppermute x14, starting transfers between devices, swapped(): lax.ppermute(value, 'patch', [(d, d ^ mask) for d in range(lax.axis_size(...  13 us
    ppermute x4, starting transfers between devices, shifted(): lax.ppermute(value, 'patch', [(d, (d + steps) % count) for d in range(cou...  11.7 us
    pallas_call x1, Pallas kernels, own_pixels(): call(functools.partial(own_kernel, length=length, devices=devices), 'own_...  7.68 us
    ppermute x14, waiting for transfers between devices, swapped(): lax.ppermute(value, 'patch', [(d, d ^ mask) for d in range(lax.axis_size(...  5.57 us
    pallas_call x1, Pallas kernels, body(): call(functools.partial(forward_kernel, length=length), 'add_halo_outputs'...  2.52 us
    pallas_call x1, Pallas kernels, body(): call(functools.partial(halo_kernel, length=length, devices=devices, facto...  1.95 us
    pallas_call x1, Pallas kernels, last(): call(functools.partial(join_kernel, length=length), 'join_input_grad', 'a...  1.5 us
    pallas_call x1, Pallas kernels, body(): call(functools.partial(half_kernel, mates=False), 'place_own_half', 'sv',...  1.24 us
  transfers between devices with their start and end apart: 18, of which 7 were waited for; matrix products, arithmetic and copies ran while one was open for 1% of the time, Pallas kernels for 27%

profile of v5, /device:TPU:0, one launch (start us, length us, event | category | flops | bytes accessed | tf_op | source)
XLA Modules:
  0.0 48.5 jit_solution(11249191034087024146)
XLA Ops:
  0.6 1.1 %copy-done = bf16[3,32,32,128]{3,2,1,0:T(8,128)(2,1)S(1)} copy-done((bf16[3,32,32,128]{3,2,1,0:T(8,128)(2,1)S(1)}, bf16[3,32,32,128]{3,2,1,0:T(8,128)(2,1)}, u32[]{:S(2)}) %copy-start) | copy-done | bytes 786456
  2.1 3.0 %collective-permute-start = (bf16[12,64,128]{2,1,0:T(8,128)(2,1)S(1)}, bf16[12,64,128]{2,1,0:T(8,128)(2,1)S(1)}, u32[]{:S(2)}, u32[]{:S(2)}) collective-permute-start(bf16[12,64,128]{2,1,0:T(8,128)(2,1)S(1)} %pack_edges.1.own_ref), channel_id=1, source_target_pairs={{0,2},{1,3},{2,4},{3,5},{4,6},{5,7},{6,8},{7,9},{8,10},{9,11},{10,... | collective-permute-start | bytes 589832 | tf_op jit(solution)/shard_map/ppermute | solution.py:411
  5.1 4.1 %collective-permute-start.1 = (bf16[12,64,128]{2,1,0:T(8,128)(2,1)S(1)}, bf16[12,64,128]{2,1,0:T(8,128)(2,1)S(1)}, u32[]{:S(2)}, u32[]{:S(2)}) collective-permute-start(bf16[12,64,128]{2,1,0:T(8,128)(2,1)S(1)} %pack_edges.1.own_ref), channel_id=1, source_target_pairs={{0,30},{1,31},{2,0},{3,1},{4,2},{5,3},{6,4},{7,5},{8,6},{9,7},{10,... | collective-permute-start | bytes 589832 | tf_op jit(solution)/shard_map/ppermute | solution.py:411
  9.1 7.7 %own_pixels.1 = (f32[12,64,128]{2,1,0:T(8,128)}, f32[24,64,128]{2,1,0:T(8,128)}, bf16[24,64,128]{2,1,0:T(8,128)(2,1)}, f32[2048,128]{1,0:T(8,128)}, bf16[3,8,128...) custom-call(s32[1]{0:T(128)} %bitcast.me_ref, s32[3,8]{1,0:T(4,128)} %nb_ref.3, s32[3,8]{1,0:T(4,128)} %rot_ref.3, ...), custom_call_target="tpu_custom_call" | custom-call | tf_op jit(solution)/shard_map/own_pixels/pallas_call | solution.py:456
  16.9 0.6 %collective-permute-start.3 = (bf16[12,64,128]{2,1,0:T(8,128)(2,1)S(1)}, bf16[12,64,128]{2,1,0:T(8,128)(2,1)S(1)}, u32[]{:S(2)}, u32[]{:S(2)}) collective-permute-start(bf16[12,64,128]{2,1,0:T(8,128)(2,1)S(1)} %broadcast_select_fusion), channel_id=1, source_target_pairs={{0,1},{1,0},{2,3},{3,2},{4,5},{5,4},{6,7},{7,6},{8,9},{9,8},{10,11... | collective-permute-start | bytes 589832 | tf_op jit(solution)/shard_map/ppermute | solution.py:415
  17.5 1.1 %collective-permute-done.3.across_ref = bf16[12,64,128]{2,1,0:T(8,128)(2,1)S(1)} collective-permute-done((bf16[12,64,128]{2,1,0:T(8,128)(2,1)S(1)}, bf16[12,64,128]{2,1,0:T(8,128)(2,1)S(1)}, u32[]{:S(2)}, u32[]{:S(2)}) %collective-permute-start.3) | collective-permute-done | bytes 196640 | tf_op jit(solution)/shard_map/ppermute | solution.py:415
  18.5 1.9 %halo_kernel_grad.1 = (f32[640,128]{1,0:T(8,128)S(1)}, f32[640,128]{1,0:T(8,128)S(1)}, bf16[4,192,384]{2,1,0:T(8,128)(2,1)}) custom-call(s32[1]{0:T(128)} %bitcast.me_ref, s32[3,8]{1,0:T(4,128)S(1)} %copy-done.7, s32[3,8]{1,0:T(4,128)S(1)} %copy-done.8, s32[3,8]{1,0:T(4,128)S(1)} %copy-done.9, bf16[12,64,128]{2,1,0:T(8,128)(2,1)S(1)} %pack_edges.1.own_ref, ...), custom_call_target="tpu_custom_call" | custom-call | tf_op jit(solution)/shard_map/halo_kernel_grad/pallas_call | solution.py:525
  20.5 0.4 collective-permute-start.4
  21.1 1.1 %collective-permute-done.4 = f32[640,128]{1,0:T(8,128)S(1)} collective-permute-done((f32[640,128]{1,0:T(8,128)S(1)}, f32[640,128]{1,0:T(8,128)S(1)}, u32[]{:S(2)}, u32[]{:S(2)}) %collective-permute-start.4) | collective-permute-done | bytes 327712 | tf_op jit(solution)/shard_map/ppermute | solution.py:415
  22.4 1.4 %collective-permute-start.6 = (bf16[160,128]{1,0:T(8,128)(2,1)S(1)}, bf16[160,128]{1,0:T(8,128)(2,1)S(1)}, u32[]{:S(2)}, u32[]{:S(2)}) collective-permute-start(bf16[160,128]{1,0:T(8,128)(2,1)S(1)} %get-tuple-element.54), channel_id=1, source_target_pairs={{0,4},{1,5},{2,6},{3,7},{4,0},{5,1},{6,2},{7,3},{8,12},{9,13},{10,... | collective-permute-start | bytes 122888 | tf_op jit(solution)/shard_map/ppermute | solution.py:415
  23.7 2.1 %collective-permute-start.7 = (bf16[160,128]{1,0:T(8,128)(2,1)S(1)}, bf16[160,128]{1,0:T(8,128)(2,1)S(1)}, u32[]{:S(2)}, u32[]{:S(2)}) collective-permute-start(bf16[160,128]{1,0:T(8,128)(2,1)S(1)} %get-tuple-element.53), channel_id=1, source_target_pairs={{0,2},{1,3},{2,0},{3,1},{4,6},{5,7},{6,4},{7,5},{8,10},{9,11},{10,... | collective-permute-start | bytes 122888 | tf_op jit(solution)/shard_map/ppermute | solution.py:415
  26.1 1.5 %collective-permute-done.5 = bf16[160,128]{1,0:T(8,128)(2,1)S(1)} collective-permute-done((bf16[160,128]{1,0:T(8,128)(2,1)S(1)}, bf16[160,128]{1,0:T(8,128)(2,1)S(1)}, u32[]{:S(2)}, u32[]{:S(2)}) %collective-permute-start.5) | collective-permute-done | bytes 40992 | tf_op jit(solution)/shard_map/ppermute | solution.py:415
  27.9 4.0 %collective-permute-start.10 = (bf16[160,128]{1,0:T(8,128)(2,1)S(1)}, bf16[160,128]{1,0:T(8,128)(2,1)S(1)}, u32[]{:S(2)}, u32[]{:S(2)}) collective-permute-start(bf16[160,128]{1,0:T(8,128)(2,1)S(1)} %add_convert_fusion), channel_id=1, source_target_pairs={{0,24},{1,25},{2,26},{3,27},{4,28},{5,29},{6,30},{7,31},{8,16},{9,... | collective-permute-start | bytes 122888 | tf_op jit(solution)/shard_map/ppermute | solution.py:415
  31.9 0.6 %collective-permute-start.9 = (bf16[160,128]{1,0:T(8,128)(2,1)S(1)}, bf16[160,128]{1,0:T(8,128)(2,1)S(1)}, u32[]{:S(2)}, u32[]{:S(2)}) collective-permute-start(bf16[160,128]{1,0:T(8,128)(2,1)S(1)} %add_convert_fusion), channel_id=1, source_target_pairs={{0,16},{1,17},{2,18},{3,19},{4,20},{5,21},{6,22},{7,23},{8,24},{9,... | collective-permute-start | bytes 122888 | tf_op jit(solution)/shard_map/ppermute | solution.py:415
  32.5 4.6 %collective-permute-start.16 = (bf16[12,64,128]{2,1,0:T(8,128)(2,1)S(1)}, bf16[12,64,128]{2,1,0:T(8,128)(2,1)S(1)}, u32[]{:S(2)}, u32[]{:S(2)}) collective-permute-start(bf16[12,64,128]{2,1,0:T(8,128)(2,1)S(1)} %get-tuple-element.46), channel_id=1, source_target_pairs={{0,30},{1,31},{2,0},{3,1},{4,2},{5,3},{6,4},{7,5},{8,6},{9,7},{10,... | collective-permute-start | bytes 589832 | tf_op jit(solution)/shard_map/ppermute | solution.py:411
  37.1 2.5 %add_halo_outputs.1 = bf16[3,1024,128]{2,1,0:T(8,128)(2,1)} custom-call(f32[3,1024,128]{2,1,0:T(8,128)} %bitcast.28, bf16[9,128,128]{2,1,0:T(8,128)(2,1)S(1)} %bitcast.26, bf16[4,192,384]{2,1,0:T(8,128)(2,1)S(1)} %copy-done.3), custom_call_target="tpu_custom_call" | custom-call | tf_op jit(solution)/shard_map/add_halo_outputs/pallas_call | solution.py:542
  39.8 0.6 %collective-permute-start.13 = (f32[160,128]{1,0:T(8,128)S(1)}, f32[160,128]{1,0:T(8,128)S(1)}, u32[]{:S(2)}, u32[]{:S(2)}) collective-permute-start(f32[160,128]{1,0:T(8,128)S(1)} %add_add_fusion), channel_id=1, source_target_pairs={{0,2},{1,3},{2,0},{3,1},{4,6},{5,7},{6,4},{7,5},{8,10},{9,11},{10,... | collective-permute-start | bytes 245768 | tf_op jit(solution)/shard_map/ppermute | solution.py:415
  40.4 2.9 %collective-permute-start.14 = (f32[160,128]{1,0:T(8,128)S(1)}, f32[160,128]{1,0:T(8,128)S(1)}, u32[]{:S(2)}, u32[]{:S(2)}) collective-permute-start(f32[160,128]{1,0:T(8,128)S(1)} %add_add_fusion), channel_id=1, source_target_pairs={{0,4},{1,5},{2,6},{3,7},{4,0},{5,1},{6,2},{7,3},{8,12},{9,13},{10,... | collective-permute-start | bytes 245768 | tf_op jit(solution)/shard_map/ppermute | solution.py:415
  43.3 1.5 %join_input_grad.1 = bf16[3,1024,128]{2,1,0:T(8,128)(2,1)} custom-call(bf16[3,1024,128]{2,1,0:T(8,128)(2,1)S(1)} %bitcast.27, f32[12,64,128]{2,1,0:T(8,128)S(1)} %copy-done.4, bf16[24,64,128]{2,1,0:T(8,128)(2,1)S(1)} %collective-permute-done.11.near_ref, bf16[12,64,128]{2,1,0:T(8,128)(2,1)S(1)} %collective-permute-done.12.low_ref, ...), custom_call_target="tpu_custom_call" | custom-call | tf_op jit(solution)/shard_map/join_input_grad/pallas_call | solution.py:557
  44.8 0.4 collective-permute-done.15
  45.2 0.8 %collective-permute-done.14 = f32[160,128]{1,0:T(8,128)S(1)} collective-permute-done((f32[160,128]{1,0:T(8,128)S(1)}, f32[160,128]{1,0:T(8,128)S(1)}, u32[]{:S(2)}, u32[]{:S(2)}) %collective-permute-start.14) | collective-permute-done | bytes 81952 | tf_op jit(solution)/shard_map/ppermute | solution.py:415
  46.2 1.2 %place_own_half.1 = (f32[1152,128]{1,0:T(8,128)}, f32[1,128]{1,0:T(1,128)}) custom-call(s32[1]{0:T(128)} %bitcast.me_ref, f32[640,128]{1,0:T(8,128)S(1)} %pad_maximum_fusion.1.half_ref), custom_call_target="tpu_custom_call" | custom-call | tf_op jit(solution)/shard_map/place_own_half/pallas_call | solution.py:572
  47.4 0.4 collective-permute-done.17.half_ref
  47.8 0.7 %place_mates_half.1 = f32[1152,128]{1,0:T(8,128)} custom-call(s32[1]{0:T(128)} %bitcast.me_ref, f32[640,128]{1,0:T(8,128)S(1)} %collective-permute-done.17.half_ref, f32[1152,128]{1,0:T(8,128)} %get-tuple-element.44.refs_0_), custom_call_target="tpu_custom_call", output_to_operand_aliasing={{}: (2, {})} | custom-call | tf_op jit(solution)/shard_map/place_mates_half/pallas_call | solution.py:575
  (50 shorter events, 1.4 us)
Async XLA Ops:
  1.8 16.8 %copy-start.5 = (bf16[4,192,64]{2,1,0:T(8,128)(2,1)S(1)}, bf16[4,192,64]{2,1,0:T(8,128)(2,1)}, u32[]{:S(2)}) copy-start(bf16[4,192,64]{2,1,0:T(8,128)(2,1)} %constant.64.clone.side_vm) | copy-start | bytes 294916
  1.8 16.8 %copy-start.6 = (bf16[4,128,64]{2,1,0:T(8,128)(2,1)S(1)}, bf16[4,128,64]{2,1,0:T(8,128)(2,1)}, u32[]{:S(2)}) copy-start(bf16[4,128,64]{2,1,0:T(8,128)(2,1)} %constant.65.clone.end_vm) | copy-start | bytes 196612
  1.8 16.8 %copy-start.7 = (s32[3,8]{1,0:T(4,128)S(1)}, s32[3,8]{1,0:T(4,128)}, u32[]{:S(2)}) copy-start(s32[3,8]{1,0:T(4,128)} %nb_ref.3) | copy-start | bytes 292
  1.8 16.8 %copy-start.8 = (s32[3,8]{1,0:T(4,128)S(1)}, s32[3,8]{1,0:T(4,128)}, u32[]{:S(2)}) copy-start(s32[3,8]{1,0:T(4,128)} %rot_ref.3) | copy-start | bytes 292
  1.8 16.8 %copy-start.9 = (s32[3,8]{1,0:T(4,128)S(1)}, s32[3,8]{1,0:T(4,128)}, u32[]{:S(2)}) copy-start(s32[3,8]{1,0:T(4,128)} %cor_ref.3) | copy-start | bytes 292
  2.1 14.7 %collective-permute-start = (bf16[12,64,128]{2,1,0:T(8,128)(2,1)S(1)}, bf16[12,64,128]{2,1,0:T(8,128)(2,1)S(1)}, u32[]{:S(2)}, u32[]{:S(2)}) collective-permute-start(bf16[12,64,128]{2,1,0:T(8,128)(2,1)S(1)} %pack_edges.1.own_ref), channel_id=1, source_target_pairs={{0,2},{1,3},{2,4},{3,5},{4,6},{5,7},{6,8},{7,9},{8,10},{9,11},{10,... | collective-permute-start | bytes 589832 | tf_op jit(solution)/shard_map/ppermute | solution.py:411
  5.1 11.8 %collective-permute-start.1 = (bf16[12,64,128]{2,1,0:T(8,128)(2,1)S(1)}, bf16[12,64,128]{2,1,0:T(8,128)(2,1)S(1)}, u32[]{:S(2)}, u32[]{:S(2)}) collective-permute-start(bf16[12,64,128]{2,1,0:T(8,128)(2,1)S(1)} %pack_edges.1.own_ref), channel_id=1, source_target_pairs={{0,30},{1,31},{2,0},{3,1},{4,2},{5,3},{6,4},{7,5},{8,6},{9,7},{10,... | collective-permute-start | bytes 589832 | tf_op jit(solution)/shard_map/ppermute | solution.py:411
  9.1 8.3 %collective-permute-start.2 = (bf16[12,64,128]{2,1,0:T(8,128)(2,1)S(1)}, bf16[12,64,128]{2,1,0:T(8,128)(2,1)S(1)}, u32[]{:S(2)}, u32[]{:S(2)}) collective-permute-start(bf16[12,64,128]{2,1,0:T(8,128)(2,1)S(1)} %pack_edges.1.own_ref), channel_id=1, source_target_pairs={{0,1},{1,0},{2,3},{3,2},{4,5},{5,4},{6,7},{7,6},{8,9},{9,8},{10,11... | collective-permute-start | bytes 589832 | tf_op jit(solution)/shard_map/ppermute | solution.py:415
  16.9 1.6 %collective-permute-start.3 = (bf16[12,64,128]{2,1,0:T(8,128)(2,1)S(1)}, bf16[12,64,128]{2,1,0:T(8,128)(2,1)S(1)}, u32[]{:S(2)}, u32[]{:S(2)}) collective-permute-start(bf16[12,64,128]{2,1,0:T(8,128)(2,1)S(1)} %broadcast_select_fusion), channel_id=1, source_target_pairs={{0,1},{1,0},{2,3},{3,2},{4,5},{5,4},{6,7},{7,6},{8,9},{9,8},{10,11... | collective-permute-start | bytes 589832 | tf_op jit(solution)/shard_map/ppermute | solution.py:415
  20.5 16.6 %copy-start.1 = (bf16[3,3,128,128]{3,2,1,0:T(8,128)(2,1)S(1)}, bf16[3,3,128,128]{3,2,1,0:T(8,128)(2,1)}, u32[]{:S(2)}) copy-start(bf16[3,3,128,128]{3,2,1,0:T(8,128)(2,1)} %param.12) | copy-start | bytes 884740
  20.5 1.7 %collective-permute-start.4 = (f32[640,128]{1,0:T(8,128)S(1)}, f32[640,128]{1,0:T(8,128)S(1)}, u32[]{:S(2)}, u32[]{:S(2)}) collective-permute-start(f32[640,128]{1,0:T(8,128)S(1)} %get-tuple-element.30), channel_id=1, source_target_pairs={{0,1},{1,0},{2,3},{3,2},{4,5},{5,4},{6,7},{7,6},{8,9},{9,8},{10,11... | collective-permute-start | bytes 983048 | tf_op jit(solution)/shard_map/ppermute | solution.py:415
  21.0 4.9 %collective-permute-start.11 = (bf16[24,64,128]{2,1,0:T(8,128)(2,1)}, bf16[24,64,128]{2,1,0:T(8,128)(2,1)S(1)}, u32[]{:S(2)}, u32[]{:S(2)}) collective-permute-start(bf16[24,64,128]{2,1,0:T(8,128)(2,1)} %get-tuple-element.32), channel_id=1, source_target_pairs={{0,1},{1,0},{2,3},{3,2},{4,5},{5,4},{6,7},{7,6},{8,9},{9,8},{10,11... | collective-permute-start | bytes 1179656 | tf_op jit(solution)/shard_map/ppermute | solution.py:415
  22.3 5.2 %collective-permute-start.5 = (bf16[160,128]{1,0:T(8,128)(2,1)S(1)}, bf16[160,128]{1,0:T(8,128)(2,1)S(1)}, u32[]{:S(2)}, u32[]{:S(2)}) collective-permute-start(bf16[160,128]{1,0:T(8,128)(2,1)S(1)} %get-tuple-element.52), channel_id=1, source_target_pairs={{0,6},{1,7},{2,4},{3,5},{4,2},{5,3},{6,0},{7,1},{8,14},{9,15},{10,... | collective-permute-start | bytes 122888 | tf_op jit(solution)/shard_map/ppermute | solution.py:415
  22.4 5.2 %collective-permute-start.6 = (bf16[160,128]{1,0:T(8,128)(2,1)S(1)}, bf16[160,128]{1,0:T(8,128)(2,1)S(1)}, u32[]{:S(2)}, u32[]{:S(2)}) collective-permute-start(bf16[160,128]{1,0:T(8,128)(2,1)S(1)} %get-tuple-element.54), channel_id=1, source_target_pairs={{0,4},{1,5},{2,6},{3,7},{4,0},{5,1},{6,2},{7,3},{8,12},{9,13},{10,... | collective-permute-start | bytes 122888 | tf_op jit(solution)/shard_map/ppermute | solution.py:415
  23.7 4.1 %collective-permute-start.7 = (bf16[160,128]{1,0:T(8,128)(2,1)S(1)}, bf16[160,128]{1,0:T(8,128)(2,1)S(1)}, u32[]{:S(2)}, u32[]{:S(2)}) collective-permute-start(bf16[160,128]{1,0:T(8,128)(2,1)S(1)} %get-tuple-element.53), channel_id=1, source_target_pairs={{0,2},{1,3},{2,0},{3,1},{4,6},{5,7},{6,4},{7,5},{8,10},{9,11},{10,... | collective-permute-start | bytes 122888 | tf_op jit(solution)/shard_map/ppermute | solution.py:415
  26.0 13.7 %collective-permute-start.12 = (bf16[12,64,128]{2,1,0:T(8,128)(2,1)S(1)}, bf16[12,64,128]{2,1,0:T(8,128)(2,1)S(1)}, u32[]{:S(2)}, u32[]{:S(2)}) collective-permute-start(bf16[12,64,128]{2,1,0:T(8,128)(2,1)S(1)} %get-tuple-element.47), channel_id=1, source_target_pairs={{0,2},{1,3},{2,4},{3,5},{4,6},{5,7},{6,8},{7,9},{8,10},{9,11},{10,... | collective-permute-start | bytes 589832 | tf_op jit(solution)/shard_map/ppermute | solution.py:411
  27.9 11.8 %collective-permute-start.10 = (bf16[160,128]{1,0:T(8,128)(2,1)S(1)}, bf16[160,128]{1,0:T(8,128)(2,1)S(1)}, u32[]{:S(2)}, u32[]{:S(2)}) collective-permute-start(bf16[160,128]{1,0:T(8,128)(2,1)S(1)} %add_convert_fusion), channel_id=1, source_target_pairs={{0,24},{1,25},{2,26},{3,27},{4,28},{5,29},{6,30},{7,31},{8,16},{9,... | collective-permute-start | bytes 122888 | tf_op jit(solution)/shard_map/ppermute | solution.py:415
  31.9 7.8 %collective-permute-start.8 = (bf16[160,128]{1,0:T(8,128)(2,1)S(1)}, bf16[160,128]{1,0:T(8,128)(2,1)S(1)}, u32[]{:S(2)}, u32[]{:S(2)}) collective-permute-start(bf16[160,128]{1,0:T(8,128)(2,1)S(1)} %add_convert_fusion), channel_id=1, source_target_pairs={{0,8},{1,9},{2,10},{3,11},{4,12},{5,13},{6,14},{7,15},{8,0},{9,1},... | collective-permute-start | bytes 122888 | tf_op jit(solution)/shard_map/ppermute | solution.py:415
  31.9 7.8 %collective-permute-start.9 = (bf16[160,128]{1,0:T(8,128)(2,1)S(1)}, bf16[160,128]{1,0:T(8,128)(2,1)S(1)}, u32[]{:S(2)}, u32[]{:S(2)}) collective-permute-start(bf16[160,128]{1,0:T(8,128)(2,1)S(1)} %add_convert_fusion), channel_id=1, source_target_pairs={{0,16},{1,17},{2,18},{3,19},{4,20},{5,21},{6,22},{7,23},{8,24},{9,... | collective-permute-start | bytes 122888 | tf_op jit(solution)/shard_map/ppermute | solution.py:415
  32.5 10.8 %collective-permute-start.16 = (bf16[12,64,128]{2,1,0:T(8,128)(2,1)S(1)}, bf16[12,64,128]{2,1,0:T(8,128)(2,1)S(1)}, u32[]{:S(2)}, u32[]{:S(2)}) collective-permute-start(bf16[12,64,128]{2,1,0:T(8,128)(2,1)S(1)} %get-tuple-element.46), channel_id=1, source_target_pairs={{0,30},{1,31},{2,0},{3,1},{4,2},{5,3},{6,4},{7,5},{8,6},{9,7},{10,... | collective-permute-start | bytes 589832 | tf_op jit(solution)/shard_map/ppermute | solution.py:411
  39.7 5.4 %collective-permute-start.15 = (f32[160,128]{1,0:T(8,128)S(1)}, f32[160,128]{1,0:T(8,128)S(1)}, u32[]{:S(2)}, u32[]{:S(2)}) collective-permute-start(f32[160,128]{1,0:T(8,128)S(1)} %add_add_fusion), channel_id=1, source_target_pairs={{0,6},{1,7},{2,4},{3,5},{4,2},{5,3},{6,0},{7,1},{8,14},{9,15},{10,... | collective-permute-start | bytes 245768 | tf_op jit(solution)/shard_map/ppermute | solution.py:415
  39.8 5.4 %collective-permute-start.13 = (f32[160,128]{1,0:T(8,128)S(1)}, f32[160,128]{1,0:T(8,128)S(1)}, u32[]{:S(2)}, u32[]{:S(2)}) collective-permute-start(f32[160,128]{1,0:T(8,128)S(1)} %add_add_fusion), channel_id=1, source_target_pairs={{0,2},{1,3},{2,0},{3,1},{4,6},{5,7},{6,4},{7,5},{8,10},{9,11},{10,... | collective-permute-start | bytes 245768 | tf_op jit(solution)/shard_map/ppermute | solution.py:415
  40.4 5.6 %collective-permute-start.14 = (f32[160,128]{1,0:T(8,128)S(1)}, f32[160,128]{1,0:T(8,128)S(1)}, u32[]{:S(2)}, u32[]{:S(2)}) collective-permute-start(f32[160,128]{1,0:T(8,128)S(1)} %add_add_fusion), channel_id=1, source_target_pairs={{0,4},{1,5},{2,6},{3,7},{4,0},{5,1},{6,2},{7,3},{8,12},{9,13},{10,... | collective-permute-start | bytes 245768 | tf_op jit(solution)/shard_map/ppermute | solution.py:415
  46.1 1.7 %collective-permute-start.17 = (f32[640,128]{1,0:T(8,128)S(1)}, f32[640,128]{1,0:T(8,128)S(1)}, u32[]{:S(2)}, u32[]{:S(2)}) collective-permute-start(f32[640,128]{1,0:T(8,128)S(1)} %pad_maximum_fusion.1.half_ref), channel_id=1, source_target_pairs={{0,1},{1,0},{2,3},{3,2},{4,5},{5,4},{6,7},{7,6},{8,9},{9,8},{10,11... | collective-permute-start | bytes 983048 | tf_op jit(solution)/shard_map/ppermute | solution.py:415
  (5 other events, 39.1 us)

commit v6 on v5

--- a/solution.py
+++ b/solution.py
@@ -549,7 +549,7 @@
     results = {}
 
     def between(value):
-        value, results["low"], results["out"] = lax.optimization_barrier((value, terms_low, outputs))
+        value, results["low"] = lax.optimization_barrier((value, terms_low))
         results["high"] = terms_high
         return value
 
@@ -564,7 +564,7 @@
             ],
             1 + 2 * patches, room=ROOM,
         )(dx, own, near_in, results["low"], results["high"])
-        value, results["in"] = lax.optimization_barrier((value, input_grad))
+        value, results["in"], results["out"] = lax.optimization_barrier((value, input_grad, outputs))
         return value
 
     mine, other = summed(keep, send, me, devices, between, last)

time: 48.8 us -> 47.9 us (0.982)
  waiting for transfers between devices: 5.58 us -> 4.72 us
    ppermute x14, waiting for transfers between devices: 5.57 us -> 4.51 us  [swapped(): lax.ppermute(value, 'patch', [(d, d ^ mask) for d in range(lax.axis_size(...]
    unnamed x22 -> x24, local copies, waits for them, and re-layouts: 1.18 us -> 1.18 us
where the time goes in v6:
time: 47.9 us; the launch traced here: 47.7 us
  starting transfers between devices  24.7 us (52%)
  Pallas kernels  15.9 us (33%)
  waiting for transfers between devices  4.72 us (10%)
  local copies, waits for them, and re-layouts  1.24 us (3%)
  between operations  0.89 us (2%)
    ppermute x14, starting transfers between devices, swapped(): lax.ppermute(value, 'patch', [(d, d ^ mask) for d in range(lax.axis_size(...  12.9 us
    ppermute x4, starting transfers between devices, shifted(): lax.ppermute(value, 'patch', [(d, (d + steps) % count) for d in range(cou...  11.7 us
    pallas_call x1, Pallas kernels, own_pixels(): call(functools.partial(own_kernel, length=length, devices=devices), 'own_...  7.68 us
    ppermute x14, waiting for transfers between devices, swapped(): lax.ppermute(value, 'patch', [(d, d ^ mask) for d in range(lax.axis_size(...  4.51 us
    pallas_call x1, Pallas kernels, body(): call(functools.partial(forward_kernel, length=length), 'add_halo_outputs'...  2.52 us
    pallas_call x1, Pallas kernels, body(): call(functools.partial(halo_kernel, length=length, devices=devices, facto...  1.95 us
    pallas_call x1, Pallas kernels, last(): call(functools.partial(join_kernel, length=length), 'join_input_grad', 'a...  1.5 us
    pallas_call x1, Pallas kernels, body(): call(functools.partial(half_kernel, mates=False), 'place_own_half', 'sv',...  1.24 us
  transfers between devices with their start and end apart: 18, of which 7 were waited for; matrix products, arithmetic and copies ran while one was open for 1% of the time, Pallas kernels for 27%

profile of v6, /device:TPU:0, one launch (start us, length us, event | category | flops | bytes accessed | tf_op | source)
XLA Modules:
  0.0 47.7 jit_solution(11891369457385270506)
XLA Ops:
  0.6 1.1 %copy-done = bf16[3,32,32,128]{3,2,1,0:T(8,128)(2,1)S(1)} copy-done((bf16[3,32,32,128]{3,2,1,0:T(8,128)(2,1)S(1)}, bf16[3,32,32,128]{3,2,1,0:T(8,128)(2,1)}, u32[]{:S(2)}) %copy-start) | copy-done | bytes 786456
  1.8 0.3 pack_edges.1.own_ref
  2.1 3.0 %collective-permute-start = (bf16[12,64,128]{2,1,0:T(8,128)(2,1)S(1)}, bf16[12,64,128]{2,1,0:T(8,128)(2,1)S(1)}, u32[]{:S(2)}, u32[]{:S(2)}) collective-permute-start(bf16[12,64,128]{2,1,0:T(8,128)(2,1)S(1)} %pack_edges.1.own_ref), channel_id=1, source_target_pairs={{0,2},{1,3},{2,4},{3,5},{4,6},{5,7},{6,8},{7,9},{8,10},{9,11},{10,... | collective-permute-start | bytes 589832 | tf_op jit(solution)/shard_map/ppermute | solution.py:411
  5.1 4.1 %collective-permute-start.1 = (bf16[12,64,128]{2,1,0:T(8,128)(2,1)S(1)}, bf16[12,64,128]{2,1,0:T(8,128)(2,1)S(1)}, u32[]{:S(2)}, u32[]{:S(2)}) collective-permute-start(bf16[12,64,128]{2,1,0:T(8,128)(2,1)S(1)} %pack_edges.1.own_ref), channel_id=1, source_target_pairs={{0,30},{1,31},{2,0},{3,1},{4,2},{5,3},{6,4},{7,5},{8,6},{9,7},{10,... | collective-permute-start | bytes 589832 | tf_op jit(solution)/shard_map/ppermute | solution.py:411
  9.1 7.7 %own_pixels.1 = (f32[12,64,128]{2,1,0:T(8,128)}, f32[24,64,128]{2,1,0:T(8,128)}, bf16[24,64,128]{2,1,0:T(8,128)(2,1)}, f32[2048,128]{1,0:T(8,128)}, bf16[3,8,128...) custom-call(s32[1]{0:T(128)} %bitcast.me_ref, s32[3,8]{1,0:T(4,128)} %nb_ref.3, s32[3,8]{1,0:T(4,128)} %rot_ref.3, ...), custom_call_target="tpu_custom_call" | custom-call | tf_op jit(solution)/shard_map/own_pixels/pallas_call | solution.py:456
  16.9 0.6 %collective-permute-start.3 = (bf16[12,64,128]{2,1,0:T(8,128)(2,1)S(1)}, bf16[12,64,128]{2,1,0:T(8,128)(2,1)S(1)}, u32[]{:S(2)}, u32[]{:S(2)}) collective-permute-start(bf16[12,64,128]{2,1,0:T(8,128)(2,1)S(1)} %broadcast_select_fusion), channel_id=1, source_target_pairs={{0,1},{1,0},{2,3},{3,2},{4,5},{5,4},{6,7},{7,6},{8,9},{9,8},{10,11... | collective-permute-start | bytes 589832 | tf_op jit(solution)/shard_map/ppermute | solution.py:415
  17.5 1.1 %collective-permute-done.3.across_ref = bf16[12,64,128]{2,1,0:T(8,128)(2,1)S(1)} collective-permute-done((bf16[12,64,128]{2,1,0:T(8,128)(2,1)S(1)}, bf16[12,64,128]{2,1,0:T(8,128)(2,1)S(1)}, u32[]{:S(2)}, u32[]{:S(2)}) %collective-permute-start.3) | collective-permute-done | bytes 196640 | tf_op jit(solution)/shard_map/ppermute | solution.py:415
  18.6 1.9 %halo_kernel_grad.1 = (f32[640,128]{1,0:T(8,128)S(1)}, f32[640,128]{1,0:T(8,128)S(1)}, bf16[4,192,384]{2,1,0:T(8,128)(2,1)}) custom-call(s32[1]{0:T(128)} %bitcast.me_ref, s32[3,8]{1,0:T(4,128)S(1)} %copy-done.7, s32[3,8]{1,0:T(4,128)S(1)} %copy-done.8, s32[3,8]{1,0:T(4,128)S(1)} %copy-done.9, bf16[12,64,128]{2,1,0:T(8,128)(2,1)S(1)} %pack_edges.1.own_ref, ...), custom_call_target="tpu_custom_call" | custom-call | tf_op jit(solution)/shard_map/halo_kernel_grad/pallas_call | solution.py:525
  20.5 0.4 collective-permute-start.4
  21.1 1.1 %collective-permute-done.4 = f32[640,128]{1,0:T(8,128)S(1)} collective-permute-done((f32[640,128]{1,0:T(8,128)S(1)}, f32[640,128]{1,0:T(8,128)S(1)}, u32[]{:S(2)}, u32[]{:S(2)}) %collective-permute-start.4) | collective-permute-done | bytes 327712 | tf_op jit(solution)/shard_map/ppermute | solution.py:415
  22.4 1.3 %collective-permute-start.6 = (bf16[160,128]{1,0:T(8,128)(2,1)S(1)}, bf16[160,128]{1,0:T(8,128)(2,1)S(1)}, u32[]{:S(2)}, u32[]{:S(2)}) collective-permute-start(bf16[160,128]{1,0:T(8,128)(2,1)S(1)} %get-tuple-element.54), channel_id=1, source_target_pairs={{0,4},{1,5},{2,6},{3,7},{4,0},{5,1},{6,2},{7,3},{8,12},{9,13},{10,... | collective-permute-start | bytes 122888 | tf_op jit(solution)/shard_map/ppermute | solution.py:415
  23.7 2.1 %collective-permute-start.7 = (bf16[160,128]{1,0:T(8,128)(2,1)S(1)}, bf16[160,128]{1,0:T(8,128)(2,1)S(1)}, u32[]{:S(2)}, u32[]{:S(2)}) collective-permute-start(bf16[160,128]{1,0:T(8,128)(2,1)S(1)} %get-tuple-element.53), channel_id=1, source_target_pairs={{0,2},{1,3},{2,0},{3,1},{4,6},{5,7},{6,4},{7,5},{8,10},{9,11},{10,... | collective-permute-start | bytes 122888 | tf_op jit(solution)/shard_map/ppermute | solution.py:415
  26.0 1.5 %collective-permute-done.5 = bf16[160,128]{1,0:T(8,128)(2,1)S(1)} collective-permute-done((bf16[160,128]{1,0:T(8,128)(2,1)S(1)}, bf16[160,128]{1,0:T(8,128)(2,1)S(1)}, u32[]{:S(2)}, u32[]{:S(2)}) %collective-permute-start.5) | collective-permute-done | bytes 40992 | tf_op jit(solution)/shard_map/ppermute | solution.py:415
  27.5 0.3 collective-permute-done.7
  27.9 4.0 %collective-permute-start.10 = (bf16[160,128]{1,0:T(8,128)(2,1)S(1)}, bf16[160,128]{1,0:T(8,128)(2,1)S(1)}, u32[]{:S(2)}, u32[]{:S(2)}) collective-permute-start(bf16[160,128]{1,0:T(8,128)(2,1)S(1)} %add_convert_fusion), channel_id=1, source_target_pairs={{0,24},{1,25},{2,26},{3,27},{4,28},{5,29},{6,30},{7,31},{8,16},{9,... | collective-permute-start | bytes 122888 | tf_op jit(solution)/shard_map/ppermute | solution.py:415
  31.8 0.6 %collective-permute-start.9 = (bf16[160,128]{1,0:T(8,128)(2,1)S(1)}, bf16[160,128]{1,0:T(8,128)(2,1)S(1)}, u32[]{:S(2)}, u32[]{:S(2)}) collective-permute-start(bf16[160,128]{1,0:T(8,128)(2,1)S(1)} %add_convert_fusion), channel_id=1, source_target_pairs={{0,16},{1,17},{2,18},{3,19},{4,20},{5,21},{6,22},{7,23},{8,24},{9,... | collective-permute-start | bytes 122888 | tf_op jit(solution)/shard_map/ppermute | solution.py:415
  32.5 4.6 %collective-permute-start.16 = (bf16[12,64,128]{2,1,0:T(8,128)(2,1)S(1)}, bf16[12,64,128]{2,1,0:T(8,128)(2,1)S(1)}, u32[]{:S(2)}, u32[]{:S(2)}) collective-permute-start(bf16[12,64,128]{2,1,0:T(8,128)(2,1)S(1)} %get-tuple-element.46), channel_id=1, source_target_pairs={{0,30},{1,31},{2,0},{3,1},{4,2},{5,3},{6,4},{7,5},{8,6},{9,7},{10,... | collective-permute-start | bytes 589832 | tf_op jit(solution)/shard_map/ppermute | solution.py:411
  37.4 2.4 %collective-permute-start.14 = (f32[160,128]{1,0:T(8,128)S(1)}, f32[160,128]{1,0:T(8,128)S(1)}, u32[]{:S(2)}, u32[]{:S(2)}) collective-permute-start(f32[160,128]{1,0:T(8,128)S(1)} %add_add_fusion), channel_id=1, source_target_pairs={{0,4},{1,5},{2,6},{3,7},{4,0},{5,1},{6,2},{7,3},{8,12},{9,13},{10,... | collective-permute-start | bytes 245768 | tf_op jit(solution)/shard_map/ppermute | solution.py:415
  39.8 1.1 %collective-permute-start.15 = (f32[160,128]{1,0:T(8,128)S(1)}, f32[160,128]{1,0:T(8,128)S(1)}, u32[]{:S(2)}, u32[]{:S(2)}) collective-permute-start(f32[160,128]{1,0:T(8,128)S(1)} %add_add_fusion), channel_id=1, source_target_pairs={{0,6},{1,7},{2,4},{3,5},{4,2},{5,3},{6,0},{7,1},{8,14},{9,15},{10,... | collective-permute-start | bytes 245768 | tf_op jit(solution)/shard_map/ppermute | solution.py:415
  40.9 2.5 %add_halo_outputs.1 = bf16[3,1024,128]{2,1,0:T(8,128)(2,1)} custom-call(f32[3,1024,128]{2,1,0:T(8,128)} %bitcast.28, bf16[9,128,128]{2,1,0:T(8,128)(2,1)S(1)} %bitcast.26, bf16[4,192,384]{2,1,0:T(8,128)(2,1)S(1)} %copy-done.3), custom_call_target="tpu_custom_call" | custom-call | tf_op jit(solution)/shard_map/add_halo_outputs/pallas_call | solution.py:542
  43.5 1.5 %join_input_grad.1 = bf16[3,1024,128]{2,1,0:T(8,128)(2,1)} custom-call(bf16[3,1024,128]{2,1,0:T(8,128)(2,1)S(1)} %bitcast.27, f32[12,64,128]{2,1,0:T(8,128)S(1)} %copy-done.4, bf16[24,64,128]{2,1,0:T(8,128)(2,1)S(1)} %collective-permute-done.11.near_ref, bf16[12,64,128]{2,1,0:T(8,128)(2,1)S(1)} %collective-permute-done.12.low_ref, ...), custom_call_target="tpu_custom_call" | custom-call | tf_op jit(solution)/shard_map/join_input_grad/pallas_call | solution.py:557
  45.3 1.2 %place_own_half.1 = (f32[1152,128]{1,0:T(8,128)}, f32[1,128]{1,0:T(1,128)}) custom-call(s32[1]{0:T(128)} %bitcast.me_ref, f32[640,128]{1,0:T(8,128)S(1)} %pad_maximum_fusion.1.half_ref), custom_call_target="tpu_custom_call" | custom-call | tf_op jit(solution)/shard_map/place_own_half/pallas_call | solution.py:572
  46.6 0.4 collective-permute-done.17.half_ref
  46.9 0.7 %place_mates_half.1 = f32[1152,128]{1,0:T(8,128)} custom-call(s32[1]{0:T(128)} %bitcast.me_ref, f32[640,128]{1,0:T(8,128)S(1)} %collective-permute-done.17.half_ref, f32[1152,128]{1,0:T(8,128)} %get-tuple-element.44.refs_0_), custom_call_target="tpu_custom_call", output_to_operand_aliasing={{}: (2, {})} | custom-call | tf_op jit(solution)/shard_map/place_mates_half/pallas_call | solution.py:575
  (52 shorter events, 1.2 us)
Async XLA Ops:
  1.8 16.8 %copy-start.6 = (bf16[4,128,64]{2,1,0:T(8,128)(2,1)S(1)}, bf16[4,128,64]{2,1,0:T(8,128)(2,1)}, u32[]{:S(2)}) copy-start(bf16[4,128,64]{2,1,0:T(8,128)(2,1)} %constant.65.clone.end_vm) | copy-start | bytes 196612
  1.8 16.8 %copy-start.7 = (s32[3,8]{1,0:T(4,128)S(1)}, s32[3,8]{1,0:T(4,128)}, u32[]{:S(2)}) copy-start(s32[3,8]{1,0:T(4,128)} %nb_ref.3) | copy-start | bytes 292
  1.8 16.8 %copy-start.8 = (s32[3,8]{1,0:T(4,128)S(1)}, s32[3,8]{1,0:T(4,128)}, u32[]{:S(2)}) copy-start(s32[3,8]{1,0:T(4,128)} %rot_ref.3) | copy-start | bytes 292
  1.8 16.8 %copy-start.9 = (s32[3,8]{1,0:T(4,128)S(1)}, s32[3,8]{1,0:T(4,128)}, u32[]{:S(2)}) copy-start(s32[3,8]{1,0:T(4,128)} %cor_ref.3) | copy-start | bytes 292
  2.1 14.8 %collective-permute-start = (bf16[12,64,128]{2,1,0:T(8,128)(2,1)S(1)}, bf16[12,64,128]{2,1,0:T(8,128)(2,1)S(1)}, u32[]{:S(2)}, u32[]{:S(2)}) collective-permute-start(bf16[12,64,128]{2,1,0:T(8,128)(2,1)S(1)} %pack_edges.1.own_ref), channel_id=1, source_target_pairs={{0,2},{1,3},{2,4},{3,5},{4,6},{5,7},{6,8},{7,9},{8,10},{9,11},{10,... | collective-permute-start | bytes 589832 | tf_op jit(solution)/shard_map/ppermute | solution.py:411
  5.1 11.8 %collective-permute-start.1 = (bf16[12,64,128]{2,1,0:T(8,128)(2,1)S(1)}, bf16[12,64,128]{2,1,0:T(8,128)(2,1)S(1)}, u32[]{:S(2)}, u32[]{:S(2)}) collective-permute-start(bf16[12,64,128]{2,1,0:T(8,128)(2,1)S(1)} %pack_edges.1.own_ref), channel_id=1, source_target_pairs={{0,30},{1,31},{2,0},{3,1},{4,2},{5,3},{6,4},{7,5},{8,6},{9,7},{10,... | collective-permute-start | bytes 589832 | tf_op jit(solution)/shard_map/ppermute | solution.py:411
  9.1 8.3 %collective-permute-start.2 = (bf16[12,64,128]{2,1,0:T(8,128)(2,1)S(1)}, bf16[12,64,128]{2,1,0:T(8,128)(2,1)S(1)}, u32[]{:S(2)}, u32[]{:S(2)}) collective-permute-start(bf16[12,64,128]{2,1,0:T(8,128)(2,1)S(1)} %pack_edges.1.own_ref), channel_id=1, source_target_pairs={{0,1},{1,0},{2,3},{3,2},{4,5},{5,4},{6,7},{7,6},{8,9},{9,8},{10,11... | collective-permute-start | bytes 589832 | tf_op jit(solution)/shard_map/ppermute | solution.py:415
  16.9 1.6 %collective-permute-start.3 = (bf16[12,64,128]{2,1,0:T(8,128)(2,1)S(1)}, bf16[12,64,128]{2,1,0:T(8,128)(2,1)S(1)}, u32[]{:S(2)}, u32[]{:S(2)}) collective-permute-start(bf16[12,64,128]{2,1,0:T(8,128)(2,1)S(1)} %broadcast_select_fusion), channel_id=1, source_target_pairs={{0,1},{1,0},{2,3},{3,2},{4,5},{5,4},{6,7},{7,6},{8,9},{9,8},{10,11... | collective-permute-start | bytes 589832 | tf_op jit(solution)/shard_map/ppermute | solution.py:415
  20.5 1.7 %collective-permute-start.4 = (f32[640,128]{1,0:T(8,128)S(1)}, f32[640,128]{1,0:T(8,128)S(1)}, u32[]{:S(2)}, u32[]{:S(2)}) collective-permute-start(f32[640,128]{1,0:T(8,128)S(1)} %get-tuple-element.30), channel_id=1, source_target_pairs={{0,1},{1,0},{2,3},{3,2},{4,5},{5,4},{6,7},{7,6},{8,9},{9,8},{10,11... | collective-permute-start | bytes 983048 | tf_op jit(solution)/shard_map/ppermute | solution.py:415
  21.0 4.9 %collective-permute-start.11 = (bf16[24,64,128]{2,1,0:T(8,128)(2,1)S(1)}, bf16[24,64,128]{2,1,0:T(8,128)(2,1)S(1)}, u32[]{:S(2)}, u32[]{:S(2)}) collective-permute-start(bf16[24,64,128]{2,1,0:T(8,128)(2,1)S(1)} %copy-done.11), channel_id=1, source_target_pairs={{0,1},{1,0},{2,3},{3,2},{4,5},{5,4},{6,7},{7,6},{8,9},{9,8},{10,11... | collective-permute-start | bytes 1179656 | tf_op jit(solution)/shard_map/ppermute | solution.py:415
  21.1 19.8 %copy-start.1 = (bf16[3,3,128,128]{3,2,1,0:T(8,128)(2,1)S(1)}, bf16[3,3,128,128]{3,2,1,0:T(8,128)(2,1)}, u32[]{:S(2)}) copy-start(bf16[3,3,128,128]{3,2,1,0:T(8,128)(2,1)} %param.12) | copy-start | bytes 884740
  21.1 19.8 %copy-start.3 = (bf16[4,192,384]{2,1,0:T(8,128)(2,1)S(1)}, bf16[4,192,384]{2,1,0:T(8,128)(2,1)}, u32[]{:S(2)}) copy-start(bf16[4,192,384]{2,1,0:T(8,128)(2,1)} %get-tuple-element.40.halo_ref) | copy-start | bytes 1769476
  22.3 5.2 %collective-permute-start.5 = (bf16[160,128]{1,0:T(8,128)(2,1)S(1)}, bf16[160,128]{1,0:T(8,128)(2,1)S(1)}, u32[]{:S(2)}, u32[]{:S(2)}) collective-permute-start(bf16[160,128]{1,0:T(8,128)(2,1)S(1)} %get-tuple-element.52), channel_id=1, source_target_pairs={{0,6},{1,7},{2,4},{3,5},{4,2},{5,3},{6,0},{7,1},{8,14},{9,15},{10,... | collective-permute-start | bytes 122888 | tf_op jit(solution)/shard_map/ppermute | solution.py:415
  22.4 5.2 %collective-permute-start.6 = (bf16[160,128]{1,0:T(8,128)(2,1)S(1)}, bf16[160,128]{1,0:T(8,128)(2,1)S(1)}, u32[]{:S(2)}, u32[]{:S(2)}) collective-permute-start(bf16[160,128]{1,0:T(8,128)(2,1)S(1)} %get-tuple-element.54), channel_id=1, source_target_pairs={{0,4},{1,5},{2,6},{3,7},{4,0},{5,1},{6,2},{7,3},{8,12},{9,13},{10,... | collective-permute-start | bytes 122888 | tf_op jit(solution)/shard_map/ppermute | solution.py:415
  23.7 4.1 %collective-permute-start.7 = (bf16[160,128]{1,0:T(8,128)(2,1)S(1)}, bf16[160,128]{1,0:T(8,128)(2,1)S(1)}, u32[]{:S(2)}, u32[]{:S(2)}) collective-permute-start(bf16[160,128]{1,0:T(8,128)(2,1)S(1)} %get-tuple-element.53), channel_id=1, source_target_pairs={{0,2},{1,3},{2,0},{3,1},{4,6},{5,7},{6,4},{7,5},{8,10},{9,11},{10,... | collective-permute-start | bytes 122888 | tf_op jit(solution)/shard_map/ppermute | solution.py:415
  26.0 11.3 %collective-permute-start.12 = (bf16[12,64,128]{2,1,0:T(8,128)(2,1)S(1)}, bf16[12,64,128]{2,1,0:T(8,128)(2,1)S(1)}, u32[]{:S(2)}, u32[]{:S(2)}) collective-permute-start(bf16[12,64,128]{2,1,0:T(8,128)(2,1)S(1)} %get-tuple-element.47), channel_id=1, source_target_pairs={{0,2},{1,3},{2,4},{3,5},{4,6},{5,7},{6,8},{7,9},{8,10},{9,11},{10,... | collective-permute-start | bytes 589832 | tf_op jit(solution)/shard_map/ppermute | solution.py:411
  27.9 9.4 %collective-permute-start.10 = (bf16[160,128]{1,0:T(8,128)(2,1)S(1)}, bf16[160,128]{1,0:T(8,128)(2,1)S(1)}, u32[]{:S(2)}, u32[]{:S(2)}) collective-permute-start(bf16[160,128]{1,0:T(8,128)(2,1)S(1)} %add_convert_fusion), channel_id=1, source_target_pairs={{0,24},{1,25},{2,26},{3,27},{4,28},{5,29},{6,30},{7,31},{8,16},{9,... | collective-permute-start | bytes 122888 | tf_op jit(solution)/shard_map/ppermute | solution.py:415
  31.8 5.5 %collective-permute-start.8 = (bf16[160,128]{1,0:T(8,128)(2,1)S(1)}, bf16[160,128]{1,0:T(8,128)(2,1)S(1)}, u32[]{:S(2)}, u32[]{:S(2)}) collective-permute-start(bf16[160,128]{1,0:T(8,128)(2,1)S(1)} %add_convert_fusion), channel_id=1, source_target_pairs={{0,8},{1,9},{2,10},{3,11},{4,12},{5,13},{6,14},{7,15},{8,0},{9,1},... | collective-permute-start | bytes 122888 | tf_op jit(solution)/shard_map/ppermute | solution.py:415
  31.8 5.5 %collective-permute-start.9 = (bf16[160,128]{1,0:T(8,128)(2,1)S(1)}, bf16[160,128]{1,0:T(8,128)(2,1)S(1)}, u32[]{:S(2)}, u32[]{:S(2)}) collective-permute-start(bf16[160,128]{1,0:T(8,128)(2,1)S(1)} %add_convert_fusion), channel_id=1, source_target_pairs={{0,16},{1,17},{2,18},{3,19},{4,20},{5,21},{6,22},{7,23},{8,24},{9,... | collective-permute-start | bytes 122888 | tf_op jit(solution)/shard_map/ppermute | solution.py:415
  32.5 11.0 %collective-permute-start.16 = (bf16[12,64,128]{2,1,0:T(8,128)(2,1)S(1)}, bf16[12,64,128]{2,1,0:T(8,128)(2,1)S(1)}, u32[]{:S(2)}, u32[]{:S(2)}) collective-permute-start(bf16[12,64,128]{2,1,0:T(8,128)(2,1)S(1)} %get-tuple-element.46), channel_id=1, source_target_pairs={{0,30},{1,31},{2,0},{3,1},{4,2},{5,3},{6,4},{7,5},{8,6},{9,7},{10,... | collective-permute-start | bytes 589832 | tf_op jit(solution)/shard_map/ppermute | solution.py:411
  37.3 7.6 %collective-permute-start.13 = (f32[160,128]{1,0:T(8,128)S(1)}, f32[160,128]{1,0:T(8,128)S(1)}, u32[]{:S(2)}, u32[]{:S(2)}) collective-permute-start(f32[160,128]{1,0:T(8,128)S(1)} %add_add_fusion), channel_id=1, source_target_pairs={{0,2},{1,3},{2,0},{3,1},{4,6},{5,7},{6,4},{7,5},{8,10},{9,11},{10,... | collective-permute-start | bytes 245768 | tf_op jit(solution)/shard_map/ppermute | solution.py:415
  37.4 7.6 %collective-permute-start.14 = (f32[160,128]{1,0:T(8,128)S(1)}, f32[160,128]{1,0:T(8,128)S(1)}, u32[]{:S(2)}, u32[]{:S(2)}) collective-permute-start(f32[160,128]{1,0:T(8,128)S(1)} %add_add_fusion), channel_id=1, source_target_pairs={{0,4},{1,5},{2,6},{3,7},{4,0},{5,1},{6,2},{7,3},{8,12},{9,13},{10,... | collective-permute-start | bytes 245768 | tf_op jit(solution)/shard_map/ppermute | solution.py:415
  39.8 5.3 %collective-permute-start.15 = (f32[160,128]{1,0:T(8,128)S(1)}, f32[160,128]{1,0:T(8,128)S(1)}, u32[]{:S(2)}, u32[]{:S(2)}) collective-permute-start(f32[160,128]{1,0:T(8,128)S(1)} %add_add_fusion), channel_id=1, source_target_pairs={{0,6},{1,7},{2,4},{3,5},{4,2},{5,3},{6,0},{7,1},{8,14},{9,15},{10,... | collective-permute-start | bytes 245768 | tf_op jit(solution)/shard_map/ppermute | solution.py:415
  45.2 1.7 %collective-permute-start.17 = (f32[640,128]{1,0:T(8,128)S(1)}, f32[640,128]{1,0:T(8,128)S(1)}, u32[]{:S(2)}, u32[]{:S(2)}) collective-permute-start(f32[640,128]{1,0:T(8,128)S(1)} %pad_maximum_fusion.1.half_ref), channel_id=1, source_target_pairs={{0,1},{1,0},{2,3},{3,2},{4,5},{5,4},{6,7},{7,6},{8,9},{9,8},{10,11... | collective-permute-start | bytes 983048 | tf_op jit(solution)/shard_map/ppermute | solution.py:415
  (6 other events, 36.1 us)

commit v7 on v6

--- a/solution.py
+++ b/solution.py
@@ -430,7 +430,7 @@
     step = 8
     while step < devices:
         sent = mine.astype(BF)
-        arrived = [swapped(sent, k * step) for k in range(1, 4 if 2 * step < devices else 2)]
+        arrived = [swapped(sent, k * step) for k in ((3, 2, 1) if 2 * step < devices else (1,))][::-1]
         if 4 * step >= devices:
             arrived = between(arrived)
         mine = sent.astype(F32) + arrived[0].astype(F32)

time: 47.9 us -> 47.9 us (level)
  no operation moved by 1% of the time
where the time goes in v7:
time: 47.9 us; the launch traced here: 47.7 us
  starting transfers between devices  24.7 us (52%)
  Pallas kernels  15.9 us (33%)
  waiting for transfers between devices  4.72 us (10%)
  local copies, waits for them, and re-layouts  1.24 us (3%)
  between operations  0.89 us (2%)
    ppermute x14, starting transfers between devices, swapped(): lax.ppermute(value, 'patch', [(d, d ^ mask) for d in range(lax.axis_size(...  12.9 us
    ppermute x4, starting transfers between devices, shifted(): lax.ppermute(value, 'patch', [(d, (d + steps) % count) for d in range(cou...  11.7 us
    pallas_call x1, Pallas kernels, own_pixels(): call(functools.partial(own_kernel, length=length, devices=devices), 'own_...  7.68 us
    ppermute x14, waiting for transfers between devices, swapped(): lax.ppermute(value, 'patch', [(d, d ^ mask) for d in range(lax.axis_size(...  4.51 us
    pallas_call x1, Pallas kernels, body(): call(functools.partial(forward_kernel, length=length), 'add_halo_outputs'...  2.52 us
    pallas_call x1, Pallas kernels, body(): call(functools.partial(halo_kernel, length=length, devices=devices, facto...  1.94 us
    pallas_call x1, Pallas kernels, last(): call(functools.partial(join_kernel, length=length), 'join_input_grad', 'a...  1.5 us
    pallas_call x1, Pallas kernels, body(): call(functools.partial(half_kernel, mates=False), 'place_own_half', 'sv',...  1.24 us
  transfers between devices with their start and end apart: 18, of which 7 were waited for; matrix products, arithmetic and copies ran while one was open for 1% of the time, Pallas kernels for 27%

profile of v7, /device:TPU:0, one launch (start us, length us, event | category | flops | bytes accessed | tf_op | source)
XLA Modules:
  0.0 47.7 jit_solution(11891369457385270506)
XLA Ops:
  0.6 1.1 %copy-done = bf16[3,32,32,128]{3,2,1,0:T(8,128)(2,1)S(1)} copy-done((bf16[3,32,32,128]{3,2,1,0:T(8,128)(2,1)S(1)}, bf16[3,32,32,128]{3,2,1,0:T(8,128)(2,1)}, u32[]{:S(2)}) %copy-start) | copy-done | bytes 786456
  1.8 0.3 pack_edges.1.own_ref
  2.1 3.0 %collective-permute-start = (bf16[12,64,128]{2,1,0:T(8,128)(2,1)S(1)}, bf16[12,64,128]{2,1,0:T(8,128)(2,1)S(1)}, u32[]{:S(2)}, u32[]{:S(2)}) collective-permute-start(bf16[12,64,128]{2,1,0:T(8,128)(2,1)S(1)} %pack_edges.1.own_ref), channel_id=1, source_target_pairs={{0,2},{1,3},{2,4},{3,5},{4,6},{5,7},{6,8},{7,9},{8,10},{9,11},{10,... | collective-permute-start | bytes 589832 | tf_op jit(solution)/shard_map/ppermute | solution.py:411
  5.1 4.1 %collective-permute-start.1 = (bf16[12,64,128]{2,1,0:T(8,128)(2,1)S(1)}, bf16[12,64,128]{2,1,0:T(8,128)(2,1)S(1)}, u32[]{:S(2)}, u32[]{:S(2)}) collective-permute-start(bf16[12,64,128]{2,1,0:T(8,128)(2,1)S(1)} %pack_edges.1.own_ref), channel_id=1, source_target_pairs={{0,30},{1,31},{2,0},{3,1},{4,2},{5,3},{6,4},{7,5},{8,6},{9,7},{10,... | collective-permute-start | bytes 589832 | tf_op jit(solution)/shard_map/ppermute | solution.py:411
  9.1 7.7 %own_pixels.1 = (f32[12,64,128]{2,1,0:T(8,128)}, f32[24,64,128]{2,1,0:T(8,128)}, bf16[24,64,128]{2,1,0:T(8,128)(2,1)}, f32[2048,128]{1,0:T(8,128)}, bf16[3,8,128...) custom-call(s32[1]{0:T(128)} %bitcast.me_ref, s32[3,8]{1,0:T(4,128)} %nb_ref.3, s32[3,8]{1,0:T(4,128)} %rot_ref.3, ...), custom_call_target="tpu_custom_call" | custom-call | tf_op jit(solution)/shard_map/own_pixels/pallas_call | solution.py:456
  16.9 0.6 %collective-permute-start.3 = (bf16[12,64,128]{2,1,0:T(8,128)(2,1)S(1)}, bf16[12,64,128]{2,1,0:T(8,128)(2,1)S(1)}, u32[]{:S(2)}, u32[]{:S(2)}) collective-permute-start(bf16[12,64,128]{2,1,0:T(8,128)(2,1)S(1)} %broadcast_select_fusion), channel_id=1, source_target_pairs={{0,1},{1,0},{2,3},{3,2},{4,5},{5,4},{6,7},{7,6},{8,9},{9,8},{10,11... | collective-permute-start | bytes 589832 | tf_op jit(solution)/shard_map/ppermute | solution.py:415
  17.5 1.1 %collective-permute-done.3.across_ref = bf16[12,64,128]{2,1,0:T(8,128)(2,1)S(1)} collective-permute-done((bf16[12,64,128]{2,1,0:T(8,128)(2,1)S(1)}, bf16[12,64,128]{2,1,0:T(8,128)(2,1)S(1)}, u32[]{:S(2)}, u32[]{:S(2)}) %collective-permute-start.3) | collective-permute-done | bytes 196640 | tf_op jit(solution)/shard_map/ppermute | solution.py:415
  18.6 1.9 %halo_kernel_grad.1 = (f32[640,128]{1,0:T(8,128)S(1)}, f32[640,128]{1,0:T(8,128)S(1)}, bf16[4,192,384]{2,1,0:T(8,128)(2,1)}) custom-call(s32[1]{0:T(128)} %bitcast.me_ref, s32[3,8]{1,0:T(4,128)S(1)} %copy-done.7, s32[3,8]{1,0:T(4,128)S(1)} %copy-done.8, s32[3,8]{1,0:T(4,128)S(1)} %copy-done.9, bf16[12,64,128]{2,1,0:T(8,128)(2,1)S(1)} %pack_edges.1.own_ref, ...), custom_call_target="tpu_custom_call" | custom-call | tf_op jit(solution)/shard_map/halo_kernel_grad/pallas_call | solution.py:525
  20.5 0.4 collective-permute-start.4
  21.1 1.1 %collective-permute-done.4 = f32[640,128]{1,0:T(8,128)S(1)} collective-permute-done((f32[640,128]{1,0:T(8,128)S(1)}, f32[640,128]{1,0:T(8,128)S(1)}, u32[]{:S(2)}, u32[]{:S(2)}) %collective-permute-start.4) | collective-permute-done | bytes 327712 | tf_op jit(solution)/shard_map/ppermute | solution.py:415
  22.4 1.3 %collective-permute-start.6 = (bf16[160,128]{1,0:T(8,128)(2,1)S(1)}, bf16[160,128]{1,0:T(8,128)(2,1)S(1)}, u32[]{:S(2)}, u32[]{:S(2)}) collective-permute-start(bf16[160,128]{1,0:T(8,128)(2,1)S(1)} %get-tuple-element.54), channel_id=1, source_target_pairs={{0,4},{1,5},{2,6},{3,7},{4,0},{5,1},{6,2},{7,3},{8,12},{9,13},{10,... | collective-permute-start | bytes 122888 | tf_op jit(solution)/shard_map/ppermute | solution.py:415
  23.7 2.1 %collective-permute-start.7 = (bf16[160,128]{1,0:T(8,128)(2,1)S(1)}, bf16[160,128]{1,0:T(8,128)(2,1)S(1)}, u32[]{:S(2)}, u32[]{:S(2)}) collective-permute-start(bf16[160,128]{1,0:T(8,128)(2,1)S(1)} %get-tuple-element.53), channel_id=1, source_target_pairs={{0,2},{1,3},{2,0},{3,1},{4,6},{5,7},{6,4},{7,5},{8,10},{9,11},{10,... | collective-permute-start | bytes 122888 | tf_op jit(solution)/shard_map/ppermute | solution.py:415
  26.0 1.5 %collective-permute-done.5 = bf16[160,128]{1,0:T(8,128)(2,1)S(1)} collective-permute-done((bf16[160,128]{1,0:T(8,128)(2,1)S(1)}, bf16[160,128]{1,0:T(8,128)(2,1)S(1)}, u32[]{:S(2)}, u32[]{:S(2)}) %collective-permute-start.5) | collective-permute-done | bytes 40992 | tf_op jit(solution)/shard_map/ppermute | solution.py:415
  27.5 0.3 collective-permute-done.7
  27.9 4.0 %collective-permute-start.10 = (bf16[160,128]{1,0:T(8,128)(2,1)S(1)}, bf16[160,128]{1,0:T(8,128)(2,1)S(1)}, u32[]{:S(2)}, u32[]{:S(2)}) collective-permute-start(bf16[160,128]{1,0:T(8,128)(2,1)S(1)} %add_convert_fusion), channel_id=1, source_target_pairs={{0,24},{1,25},{2,26},{3,27},{4,28},{5,29},{6,30},{7,31},{8,16},{9,... | collective-permute-start | bytes 122888 | tf_op jit(solution)/shard_map/ppermute | solution.py:415
  31.8 0.6 %collective-permute-start.9 = (bf16[160,128]{1,0:T(8,128)(2,1)S(1)}, bf16[160,128]{1,0:T(8,128)(2,1)S(1)}, u32[]{:S(2)}, u32[]{:S(2)}) collective-permute-start(bf16[160,128]{1,0:T(8,128)(2,1)S(1)} %add_convert_fusion), channel_id=1, source_target_pairs={{0,16},{1,17},{2,18},{3,19},{4,20},{5,21},{6,22},{7,23},{8,24},{9,... | collective-permute-start | bytes 122888 | tf_op jit(solution)/shard_map/ppermute | solution.py:415
  32.5 4.6 %collective-permute-start.16 = (bf16[12,64,128]{2,1,0:T(8,128)(2,1)S(1)}, bf16[12,64,128]{2,1,0:T(8,128)(2,1)S(1)}, u32[]{:S(2)}, u32[]{:S(2)}) collective-permute-start(bf16[12,64,128]{2,1,0:T(8,128)(2,1)S(1)} %get-tuple-element.46), channel_id=1, source_target_pairs={{0,30},{1,31},{2,0},{3,1},{4,2},{5,3},{6,4},{7,5},{8,6},{9,7},{10,... | collective-permute-start | bytes 589832 | tf_op jit(solution)/shard_map/ppermute | solution.py:411
  37.4 2.4 %collective-permute-start.14 = (f32[160,128]{1,0:T(8,128)S(1)}, f32[160,128]{1,0:T(8,128)S(1)}, u32[]{:S(2)}, u32[]{:S(2)}) collective-permute-start(f32[160,128]{1,0:T(8,128)S(1)} %add_add_fusion), channel_id=1, source_target_pairs={{0,4},{1,5},{2,6},{3,7},{4,0},{5,1},{6,2},{7,3},{8,12},{9,13},{10,... | collective-permute-start | bytes 245768 | tf_op jit(solution)/shard_map/ppermute | solution.py:415
  39.8 1.1 %collective-permute-start.15 = (f32[160,128]{1,0:T(8,128)S(1)}, f32[160,128]{1,0:T(8,128)S(1)}, u32[]{:S(2)}, u32[]{:S(2)}) collective-permute-start(f32[160,128]{1,0:T(8,128)S(1)} %add_add_fusion), channel_id=1, source_target_pairs={{0,6},{1,7},{2,4},{3,5},{4,2},{5,3},{6,0},{7,1},{8,14},{9,15},{10,... | collective-permute-start | bytes 245768 | tf_op jit(solution)/shard_map/ppermute | solution.py:415
  40.9 2.5 %add_halo_outputs.1 = bf16[3,1024,128]{2,1,0:T(8,128)(2,1)} custom-call(f32[3,1024,128]{2,1,0:T(8,128)} %bitcast.28, bf16[9,128,128]{2,1,0:T(8,128)(2,1)S(1)} %bitcast.26, bf16[4,192,384]{2,1,0:T(8,128)(2,1)S(1)} %copy-done.3), custom_call_target="tpu_custom_call" | custom-call | tf_op jit(solution)/shard_map/add_halo_outputs/pallas_call | solution.py:542
  43.5 1.5 %join_input_grad.1 = bf16[3,1024,128]{2,1,0:T(8,128)(2,1)} custom-call(bf16[3,1024,128]{2,1,0:T(8,128)(2,1)S(1)} %bitcast.27, f32[12,64,128]{2,1,0:T(8,128)S(1)} %copy-done.4, bf16[24,64,128]{2,1,0:T(8,128)(2,1)S(1)} %collective-permute-done.11.near_ref, bf16[12,64,128]{2,1,0:T(8,128)(2,1)S(1)} %collective-permute-done.12.low_ref, ...), custom_call_target="tpu_custom_call" | custom-call | tf_op jit(solution)/shard_map/join_input_grad/pallas_call | solution.py:557
  45.3 1.2 %place_own_half.1 = (f32[1152,128]{1,0:T(8,128)}, f32[1,128]{1,0:T(1,128)}) custom-call(s32[1]{0:T(128)} %bitcast.me_ref, f32[640,128]{1,0:T(8,128)S(1)} %pad_maximum_fusion.1.half_ref), custom_call_target="tpu_custom_call" | custom-call | tf_op jit(solution)/shard_map/place_own_half/pallas_call | solution.py:572
  46.6 0.4 collective-permute-done.17.half_ref
  46.9 0.7 %place_mates_half.1 = f32[1152,128]{1,0:T(8,128)} custom-call(s32[1]{0:T(128)} %bitcast.me_ref, f32[640,128]{1,0:T(8,128)S(1)} %collective-permute-done.17.half_ref, f32[1152,128]{1,0:T(8,128)} %get-tuple-element.44.refs_0_), custom_call_target="tpu_custom_call", output_to_operand_aliasing={{}: (2, {})} | custom-call | tf_op jit(solution)/shard_map/place_mates_half/pallas_call | solution.py:575
  (52 shorter events, 1.2 us)
Async XLA Ops:
  1.8 16.8 %copy-start.6 = (bf16[4,128,64]{2,1,0:T(8,128)(2,1)S(1)}, bf16[4,128,64]{2,1,0:T(8,128)(2,1)}, u32[]{:S(2)}) copy-start(bf16[4,128,64]{2,1,0:T(8,128)(2,1)} %constant.65.clone.end_vm) | copy-start | bytes 196612
  1.8 16.8 %copy-start.7 = (s32[3,8]{1,0:T(4,128)S(1)}, s32[3,8]{1,0:T(4,128)}, u32[]{:S(2)}) copy-start(s32[3,8]{1,0:T(4,128)} %nb_ref.3) | copy-start | bytes 292
  1.8 16.8 %copy-start.8 = (s32[3,8]{1,0:T(4,128)S(1)}, s32[3,8]{1,0:T(4,128)}, u32[]{:S(2)}) copy-start(s32[3,8]{1,0:T(4,128)} %rot_ref.3) | copy-start | bytes 292
  1.8 16.8 %copy-start.9 = (s32[3,8]{1,0:T(4,128)S(1)}, s32[3,8]{1,0:T(4,128)}, u32[]{:S(2)}) copy-start(s32[3,8]{1,0:T(4,128)} %cor_ref.3) | copy-start | bytes 292
  2.1 14.8 %collective-permute-start = (bf16[12,64,128]{2,1,0:T(8,128)(2,1)S(1)}, bf16[12,64,128]{2,1,0:T(8,128)(2,1)S(1)}, u32[]{:S(2)}, u32[]{:S(2)}) collective-permute-start(bf16[12,64,128]{2,1,0:T(8,128)(2,1)S(1)} %pack_edges.1.own_ref), channel_id=1, source_target_pairs={{0,2},{1,3},{2,4},{3,5},{4,6},{5,7},{6,8},{7,9},{8,10},{9,11},{10,... | collective-permute-start | bytes 589832 | tf_op jit(solution)/shard_map/ppermute | solution.py:411
  5.1 11.8 %collective-permute-start.1 = (bf16[12,64,128]{2,1,0:T(8,128)(2,1)S(1)}, bf16[12,64,128]{2,1,0:T(8,128)(2,1)S(1)}, u32[]{:S(2)}, u32[]{:S(2)}) collective-permute-start(bf16[12,64,128]{2,1,0:T(8,128)(2,1)S(1)} %pack_edges.1.own_ref), channel_id=1, source_target_pairs={{0,30},{1,31},{2,0},{3,1},{4,2},{5,3},{6,4},{7,5},{8,6},{9,7},{10,... | collective-permute-start | bytes 589832 | tf_op jit(solution)/shard_map/ppermute | solution.py:411
  9.1 8.3 %collective-permute-start.2 = (bf16[12,64,128]{2,1,0:T(8,128)(2,1)S(1)}, bf16[12,64,128]{2,1,0:T(8,128)(2,1)S(1)}, u32[]{:S(2)}, u32[]{:S(2)}) collective-permute-start(bf16[12,64,128]{2,1,0:T(8,128)(2,1)S(1)} %pack_edges.1.own_ref), channel_id=1, source_target_pairs={{0,1},{1,0},{2,3},{3,2},{4,5},{5,4},{6,7},{7,6},{8,9},{9,8},{10,11... | collective-permute-start | bytes 589832 | tf_op jit(solution)/shard_map/ppermute | solution.py:415
  16.9 1.6 %collective-permute-start.3 = (bf16[12,64,128]{2,1,0:T(8,128)(2,1)S(1)}, bf16[12,64,128]{2,1,0:T(8,128)(2,1)S(1)}, u32[]{:S(2)}, u32[]{:S(2)}) collective-permute-start(bf16[12,64,128]{2,1,0:T(8,128)(2,1)S(1)} %broadcast_select_fusion), channel_id=1, source_target_pairs={{0,1},{1,0},{2,3},{3,2},{4,5},{5,4},{6,7},{7,6},{8,9},{9,8},{10,11... | collective-permute-start | bytes 589832 | tf_op jit(solution)/shard_map/ppermute | solution.py:415
  20.5 1.7 %collective-permute-start.4 = (f32[640,128]{1,0:T(8,128)S(1)}, f32[640,128]{1,0:T(8,128)S(1)}, u32[]{:S(2)}, u32[]{:S(2)}) collective-permute-start(f32[640,128]{1,0:T(8,128)S(1)} %get-tuple-element.30), channel_id=1, source_target_pairs={{0,1},{1,0},{2,3},{3,2},{4,5},{5,4},{6,7},{7,6},{8,9},{9,8},{10,11... | collective-permute-start | bytes 983048 | tf_op jit(solution)/shard_map/ppermute | solution.py:415
  21.0 4.9 %collective-permute-start.11 = (bf16[24,64,128]{2,1,0:T(8,128)(2,1)S(1)}, bf16[24,64,128]{2,1,0:T(8,128)(2,1)S(1)}, u32[]{:S(2)}, u32[]{:S(2)}) collective-permute-start(bf16[24,64,128]{2,1,0:T(8,128)(2,1)S(1)} %copy-done.11), channel_id=1, source_target_pairs={{0,1},{1,0},{2,3},{3,2},{4,5},{5,4},{6,7},{7,6},{8,9},{9,8},{10,11... | collective-permute-start | bytes 1179656 | tf_op jit(solution)/shard_map/ppermute | solution.py:415
  21.1 19.8 %copy-start.1 = (bf16[3,3,128,128]{3,2,1,0:T(8,128)(2,1)S(1)}, bf16[3,3,128,128]{3,2,1,0:T(8,128)(2,1)}, u32[]{:S(2)}) copy-start(bf16[3,3,128,128]{3,2,1,0:T(8,128)(2,1)} %param.12) | copy-start | bytes 884740
  21.1 19.8 %copy-start.3 = (bf16[4,192,384]{2,1,0:T(8,128)(2,1)S(1)}, bf16[4,192,384]{2,1,0:T(8,128)(2,1)}, u32[]{:S(2)}) copy-start(bf16[4,192,384]{2,1,0:T(8,128)(2,1)} %get-tuple-element.40.halo_ref) | copy-start | bytes 1769476
  22.3 5.2 %collective-permute-start.5 = (bf16[160,128]{1,0:T(8,128)(2,1)S(1)}, bf16[160,128]{1,0:T(8,128)(2,1)S(1)}, u32[]{:S(2)}, u32[]{:S(2)}) collective-permute-start(bf16[160,128]{1,0:T(8,128)(2,1)S(1)} %get-tuple-element.52), channel_id=1, source_target_pairs={{0,6},{1,7},{2,4},{3,5},{4,2},{5,3},{6,0},{7,1},{8,14},{9,15},{10,... | collective-permute-start | bytes 122888 | tf_op jit(solution)/shard_map/ppermute | solution.py:415
  22.4 5.2 %collective-permute-start.6 = (bf16[160,128]{1,0:T(8,128)(2,1)S(1)}, bf16[160,128]{1,0:T(8,128)(2,1)S(1)}, u32[]{:S(2)}, u32[]{:S(2)}) collective-permute-start(bf16[160,128]{1,0:T(8,128)(2,1)S(1)} %get-tuple-element.54), channel_id=1, source_target_pairs={{0,4},{1,5},{2,6},{3,7},{4,0},{5,1},{6,2},{7,3},{8,12},{9,13},{10,... | collective-permute-start | bytes 122888 | tf_op jit(solution)/shard_map/ppermute | solution.py:415
  23.7 4.1 %collective-permute-start.7 = (bf16[160,128]{1,0:T(8,128)(2,1)S(1)}, bf16[160,128]{1,0:T(8,128)(2,1)S(1)}, u32[]{:S(2)}, u32[]{:S(2)}) collective-permute-start(bf16[160,128]{1,0:T(8,128)(2,1)S(1)} %get-tuple-element.53), channel_id=1, source_target_pairs={{0,2},{1,3},{2,0},{3,1},{4,6},{5,7},{6,4},{7,5},{8,10},{9,11},{10,... | collective-permute-start | bytes 122888 | tf_op jit(solution)/shard_map/ppermute | solution.py:415
  26.0 11.3 %collective-permute-start.12 = (bf16[12,64,128]{2,1,0:T(8,128)(2,1)S(1)}, bf16[12,64,128]{2,1,0:T(8,128)(2,1)S(1)}, u32[]{:S(2)}, u32[]{:S(2)}) collective-permute-start(bf16[12,64,128]{2,1,0:T(8,128)(2,1)S(1)} %get-tuple-element.47), channel_id=1, source_target_pairs={{0,2},{1,3},{2,4},{3,5},{4,6},{5,7},{6,8},{7,9},{8,10},{9,11},{10,... | collective-permute-start | bytes 589832 | tf_op jit(solution)/shard_map/ppermute | solution.py:411
  27.9 9.4 %collective-permute-start.10 = (bf16[160,128]{1,0:T(8,128)(2,1)S(1)}, bf16[160,128]{1,0:T(8,128)(2,1)S(1)}, u32[]{:S(2)}, u32[]{:S(2)}) collective-permute-start(bf16[160,128]{1,0:T(8,128)(2,1)S(1)} %add_convert_fusion), channel_id=1, source_target_pairs={{0,24},{1,25},{2,26},{3,27},{4,28},{5,29},{6,30},{7,31},{8,16},{9,... | collective-permute-start | bytes 122888 | tf_op jit(solution)/shard_map/ppermute | solution.py:415
  31.8 5.5 %collective-permute-start.8 = (bf16[160,128]{1,0:T(8,128)(2,1)S(1)}, bf16[160,128]{1,0:T(8,128)(2,1)S(1)}, u32[]{:S(2)}, u32[]{:S(2)}) collective-permute-start(bf16[160,128]{1,0:T(8,128)(2,1)S(1)} %add_convert_fusion), channel_id=1, source_target_pairs={{0,8},{1,9},{2,10},{3,11},{4,12},{5,13},{6,14},{7,15},{8,0},{9,1},... | collective-permute-start | bytes 122888 | tf_op jit(solution)/shard_map/ppermute | solution.py:415
  31.8 5.5 %collective-permute-start.9 = (bf16[160,128]{1,0:T(8,128)(2,1)S(1)}, bf16[160,128]{1,0:T(8,128)(2,1)S(1)}, u32[]{:S(2)}, u32[]{:S(2)}) collective-permute-start(bf16[160,128]{1,0:T(8,128)(2,1)S(1)} %add_convert_fusion), channel_id=1, source_target_pairs={{0,16},{1,17},{2,18},{3,19},{4,20},{5,21},{6,22},{7,23},{8,24},{9,... | collective-permute-start | bytes 122888 | tf_op jit(solution)/shard_map/ppermute | solution.py:415
  32.5 11.0 %collective-permute-start.16 = (bf16[12,64,128]{2,1,0:T(8,128)(2,1)S(1)}, bf16[12,64,128]{2,1,0:T(8,128)(2,1)S(1)}, u32[]{:S(2)}, u32[]{:S(2)}) collective-permute-start(bf16[12,64,128]{2,1,0:T(8,128)(2,1)S(1)} %get-tuple-element.46), channel_id=1, source_target_pairs={{0,30},{1,31},{2,0},{3,1},{4,2},{5,3},{6,4},{7,5},{8,6},{9,7},{10,... | collective-permute-start | bytes 589832 | tf_op jit(solution)/shard_map/ppermute | solution.py:411
  37.3 7.6 %collective-permute-start.13 = (f32[160,128]{1,0:T(8,128)S(1)}, f32[160,128]{1,0:T(8,128)S(1)}, u32[]{:S(2)}, u32[]{:S(2)}) collective-permute-start(f32[160,128]{1,0:T(8,128)S(1)} %add_add_fusion), channel_id=1, source_target_pairs={{0,2},{1,3},{2,0},{3,1},{4,6},{5,7},{6,4},{7,5},{8,10},{9,11},{10,... | collective-permute-start | bytes 245768 | tf_op jit(solution)/shard_map/ppermute | solution.py:415
  37.4 7.6 %collective-permute-start.14 = (f32[160,128]{1,0:T(8,128)S(1)}, f32[160,128]{1,0:T(8,128)S(1)}, u32[]{:S(2)}, u32[]{:S(2)}) collective-permute-start(f32[160,128]{1,0:T(8,128)S(1)} %add_add_fusion), channel_id=1, source_target_pairs={{0,4},{1,5},{2,6},{3,7},{4,0},{5,1},{6,2},{7,3},{8,12},{9,13},{10,... | collective-permute-start | bytes 245768 | tf_op jit(solution)/shard_map/ppermute | solution.py:415
  39.8 5.3 %collective-permute-start.15 = (f32[160,128]{1,0:T(8,128)S(1)}, f32[160,128]{1,0:T(8,128)S(1)}, u32[]{:S(2)}, u32[]{:S(2)}) collective-permute-start(f32[160,128]{1,0:T(8,128)S(1)} %add_add_fusion), channel_id=1, source_target_pairs={{0,6},{1,7},{2,4},{3,5},{4,2},{5,3},{6,0},{7,1},{8,14},{9,15},{10,... | collective-permute-start | bytes 245768 | tf_op jit(solution)/shard_map/ppermute | solution.py:415
  45.2 1.7 %collective-permute-start.17 = (f32[640,128]{1,0:T(8,128)S(1)}, f32[640,128]{1,0:T(8,128)S(1)}, u32[]{:S(2)}, u32[]{:S(2)}) collective-permute-start(f32[640,128]{1,0:T(8,128)S(1)} %pad_maximum_fusion.1.half_ref), channel_id=1, source_target_pairs={{0,1},{1,0},{2,3},{3,2},{4,5},{5,4},{6,7},{7,6},{8,9},{9,8},{10,11... | collective-permute-start | bytes 983048 | tf_op jit(solution)/shard_map/ppermute | solution.py:415
  (6 other events, 36.1 us)
